TPU v7x, 32 devices: a whole 2x2x4 slice. The times are simulated.
32 devices in a mesh: parts: 2 (over y), seq: 8 (over z, x), head: 2 (over core).
Axes of the slice: x: 2, y: 2, z: 4, core: 2. Of those that a mesh axis runs over, the one named last changes fastest.
Arguments:
- queries: bfloat16 [4096, 4096], P(('parts', 'seq'), 'head'), parts along dimension 0, may hold values from -144 to 144
- key_rows: bfloat16 [4096, 1024], P(('parts', 'seq'), 'head'), parts along dimension 0, may hold values from -4 to 4
- value_rows: bfloat16 [4096, 1024], P(('parts', 'seq'), 'head'), parts along dimension 0, may hold values from -4 to 4
- out_grad: bfloat16 [4096, 4096], P(('parts', 'seq'), 'head'), parts along dimension 0, may hold values from -4 to 4
- owner_slot: int32 [4096], P(('parts', 'seq')), parts along dimension 0, may hold values from 0 to 2047, as said below
- block_links: int32 [32, 5], P(('parts', 'seq')), parts along dimension 0, may hold values from 0 to 1, as said below
Outputs:
- query_grad: bfloat16 [4096, 4096], P(('parts', 'seq'), 'head'), parts along dimension 0
- key_grad: bfloat16 [4096, 1024], P(('parts', 'seq'), 'head'), parts along dimension 0
- value_grad: bfloat16 [4096, 1024], P(('parts', 'seq'), 'head'), parts along dimension 0
There are 2 independent parts, one for each index of `parts`. A program takes and returns all parts, laid end to end along the dimension named above; each array names one. Nothing has to cross between parts.
Inputs may be any that keep to these rules, and one draw needn't show every extreme that they name: A permutation: token t goes to index owner_slot[t] // 256 of seq, row owner_slot[t] % 256. The 256 tokens of one index of seq send at most 64 tokens to one index, and exactly 64 to some index in every draw. `block_links`: every block is linked to itself (column 2 is 1); columns that name blocks outside the pack are 0.
All inputs are finite; a program needn't handle non-finite values.
Results may differ from a plain program's by a relative error of at most 0.0055.
Values may be sent and summed in bfloat16 or wider, within the bound.
No kernel may reach another device: no remote copies, remote signals or barrier semaphores. Data moves between devices by JAX's collectives and lax.ppermute only.
A program may use at most 64 MiB of HBM per device.

v0:
```python
import functools

import jax
import jax.numpy as jnp
from jax import lax
from jax.experimental import pallas as pl
from jax.experimental.pallas import tpu as pltpu
from jax.sharding import PartitionSpec as P

HEAD_DIM = 128
BLOCK = 128


def padded(value, sides, width):
    for axis, dim in sides:
        peers, length = (lax.axis_size(axis), value.shape[dim])
        up = [(i, (i + 1) % peers) for i in range(peers - 1)]
        down = [(j, i) for i, j in up]
        last = lax.slice_in_dim(value, length - width, length, axis=dim)
        leading = lax.slice_in_dim(value, 0, width, axis=dim)
        before = lax.ppermute(last, axis, up)
        after = lax.ppermute(leading, axis, down)
        value = jnp.concatenate([before, value, after], axis=dim)
    return value


def from_behind(value, axis, by):
    peers = lax.axis_size(axis)
    pairs = [(i, i + by) for i in range(peers) if 0 <= i + by < peers]
    return lax.ppermute(value, axis, pairs)


def head_major(matrix, heads):
    return matrix.reshape(matrix.shape[0], heads, -1).transpose(1, 0, 2)


def relay_plan(queries, key_rows, value_rows, out_grad, owner_slot, block_links):
    row_count = queries.shape[0]
    seq_count = lax.axis_size("seq")
    capacity = 4 * max(1, row_count // seq_count // 2)
    slots = seq_count * capacity
    kv_width = key_rows.shape[1]
    kv_heads = kv_width // HEAD_DIM
    group_size = queries.shape[1] // kv_width
    score_scale = HEAD_DIM ** (-0.5)
    owner_dev = owner_slot // row_count
    owner_row = owner_slot % row_count
    member = (owner_dev[:, None] == jnp.arange(seq_count, dtype=jnp.int32)[None, :]).astype(
        jnp.int32
    )
    within = jnp.sum(jnp.cumsum(member, 0) * member, 1) - 1
    placed = owner_dev * capacity + within

    def pack_rows(matrix):
        return (
            jnp.zeros((slots, matrix.shape[1]), matrix.dtype)
            .at[placed]
            .set(matrix)
            .reshape(seq_count, capacity, matrix.shape[1])
        )

    vacant = jnp.array([row_count // 16, row_count % 16], jnp.float32)
    row_codes = jnp.stack([owner_row // 16, owner_row % 16], 1).astype(jnp.float32)
    code_buffer = (
        jnp.broadcast_to(vacant, (slots, 2))
        .at[placed]
        .set(row_codes)
        .astype(jnp.bfloat16)
        .reshape(seq_count, capacity, 2)
    )
    q_in, k_in, v_in, g_in, codes_in = (
        lax.all_to_all(pack_rows(queries), "seq", split_axis=0, concat_axis=0, tiled=True),
        lax.all_to_all(pack_rows(key_rows), "seq", split_axis=0, concat_axis=0, tiled=True),
        lax.all_to_all(pack_rows(value_rows), "seq", split_axis=0, concat_axis=0, tiled=True),
        lax.all_to_all(pack_rows(out_grad), "seq", split_axis=0, concat_axis=0, tiled=True),
        lax.all_to_all(code_buffer, "seq", split_axis=0, concat_axis=0, tiled=True),
    )
    arrived = codes_in.reshape(slots, 2).astype(jnp.float32)
    target = (arrived[:, 0] * 16.0 + arrived[:, 1]).astype(jnp.int32)

    def unpack_rows(buffer):
        flat_rows = buffer.reshape(slots, buffer.shape[2])
        return (
            jnp.zeros((row_count, flat_rows.shape[1]), flat_rows.dtype)
            .at[target]
            .set(flat_rows, mode="drop")
        )

    q_own = unpack_rows(q_in)
    k_own = unpack_rows(k_in)
    v_own = unpack_rows(v_in)
    g_own = unpack_rows(g_in)
    blocks = row_count // BLOCK
    span = block_links.shape[1]
    offset = (
        jnp.arange(3 * blocks, dtype=jnp.int32)[None, :]
        - jnp.arange(blocks, dtype=jnp.int32)[:, None]
    )
    selector = offset[:, :, None] == jnp.arange(span, dtype=jnp.int32)[None, None, :]
    allowed = jnp.sum(jnp.where(selector, block_links[:, None, :], 0), 2) > 0
    token_mask = jnp.repeat(jnp.repeat(allowed, BLOCK, 0), BLOCK, 1)
    kv_pair = jnp.concatenate([k_own, v_own], 1)
    kv_wide = padded(kv_pair, (("seq", 0),), row_count)

    def scores_of(q_group, k_group):
        raw_scores = (
            jnp.einsum("rgd,kd->grk", q_group, k_group, preferred_element_type=jnp.float32)
            * score_scale
        )
        return jnp.where(token_mask[None], raw_scores, -jnp.inf)

    def forward_head(operands):
        q_group, k_group, v_group = operands
        scores = scores_of(q_group, k_group)
        row_top = jnp.max(scores, -1, keepdims=True)
        log_total = row_top + jnp.log(jnp.sum(jnp.exp(scores - row_top), -1, keepdims=True))
        probs = jnp.exp(scores - log_total).astype(jnp.bfloat16)
        attended = jnp.einsum(
            "grk,kd->rgd", probs, v_group, preferred_element_type=jnp.float32
        ).astype(jnp.bfloat16)
        return (attended, log_total)

    def backward_head(operands):
        q_group, k_group, v_group, g_group, attended, log_total = operands
        weights = jnp.exp(scores_of(q_group, k_group) - log_total)
        row_delta = jnp.sum(g_group.astype(jnp.float32) * attended.astype(jnp.float32), -1).T[
            :, :, None
        ]
        d_probs = jnp.einsum("rgd,kd->grk", g_group, v_group, preferred_element_type=jnp.float32)
        d_scores = (weights * (d_probs - row_delta)).astype(jnp.bfloat16)
        q_grad = (
            jnp.einsum("grk,kd->rgd", d_scores, k_group, preferred_element_type=jnp.float32)
            * score_scale
        ).astype(jnp.bfloat16)
        k_grad = (
            jnp.einsum("grk,rgd->kd", d_scores, q_group, preferred_element_type=jnp.float32)
            * score_scale
        )
        v_grad = jnp.einsum(
            "grk,rgd->kd", weights.astype(jnp.bfloat16), g_group, preferred_element_type=jnp.float32
        )
        return (q_grad, k_grad, v_grad)

    query_heads = q_own.reshape(row_count, kv_heads, group_size, HEAD_DIM).transpose(1, 0, 2, 3)
    grad_heads = g_own.reshape(row_count, kv_heads, group_size, HEAD_DIM).transpose(1, 0, 2, 3)
    key_heads = head_major(kv_wide[:, :kv_width], kv_heads)
    value_heads = head_major(kv_wide[:, kv_width:], kv_heads)
    attended, log_total = lax.map(forward_head, (query_heads, key_heads, value_heads))
    q_grads, k_grads, v_grads = lax.map(
        backward_head, (query_heads, key_heads, value_heads, grad_heads, attended, log_total)
    )
    q_grad_own = q_grads.transpose(1, 0, 2, 3).reshape(row_count, kv_heads * group_size * HEAD_DIM)
    kv_grads = jnp.concatenate(
        [
            k_grads.transpose(1, 0, 2).reshape(3 * row_count, kv_width),
            v_grads.transpose(1, 0, 2).reshape(3 * row_count, kv_width),
        ],
        1,
    )
    from_above = from_behind(kv_grads[:row_count].astype(jnp.bfloat16), "seq", -1).astype(
        jnp.float32
    )
    from_below = from_behind(kv_grads[2 * row_count :].astype(jnp.bfloat16), "seq", 1).astype(
        jnp.float32
    )
    kv_total = (kv_grads[row_count : 2 * row_count] + from_above + from_below).astype(jnp.bfloat16)
    pick_rows = jnp.minimum(target, row_count - 1)

    def gather_back(matrix):
        return matrix[pick_rows].reshape(seq_count, capacity, matrix.shape[1])

    q_back, k_back, v_back = (
        lax.all_to_all(gather_back(q_grad_own), "seq", split_axis=0, concat_axis=0, tiled=True),
        lax.all_to_all(
            gather_back(kv_total[:, :kv_width]), "seq", split_axis=0, concat_axis=0, tiled=True
        ),
        lax.all_to_all(
            gather_back(kv_total[:, kv_width:]), "seq", split_axis=0, concat_axis=0, tiled=True
        ),
    )

    def settle_rows(buffer):
        return buffer.reshape(slots, buffer.shape[2])[placed]

    return (settle_rows(q_back), settle_rows(k_back), settle_rows(v_back))


LOG2_E = 1.4426950408889634
MASKED = -1e30
LANES = 128
NT = (((1,), (1,)), ((), ()))
NN = (((1,), (0,)), ((), ()))
IN_VMEM = pl.BlockSpec(memory_space=pltpu.VMEM)
IN_SMEM = pl.BlockSpec(memory_space=pltpu.SMEM)


def dot(a, b, dims):
    return lax.dot_general(a, b, dims, preferred_element_type=jnp.float32)


def flip(a):
    return a.astype(jnp.float32).T.astype(jnp.bfloat16)


def columns(ref, at):
    return ref[:, lanes_of(at)]


def lanes_of(at):
    return pl.ds(pl.multiple_of(at * HEAD_DIM, HEAD_DIM), HEAD_DIM)


def stacked_heads(ref, head, group):
    return jnp.concatenate([columns(ref, head * group + j) for j in range(group)], 0)


def masks_kernel(peers, blocks_dev, span, order_ref, notes_ref, slots_ref, key_hot_ref, query_mask_ref):
    f32, bf16 = jnp.float32, jnp.bfloat16
    rows = lax.broadcasted_iota(jnp.int32, (LANES, LANES), 0)
    lanes = lax.broadcasted_iota(jnp.int32, (LANES, LANES), 1)
    slot_rows = slots_ref.shape[0]

    def hot(slots):
        return (rows == slots // BLOCK).astype(f32).T.astype(bf16)

    for r in range(peers):
        shard = notes_ref[order_ref[r]]
        for i in range(slot_rows):
            key_hot_ref[r, i * LANES : (i + 1) * LANES, :] = hot(shard[i : i + 1, :])
    owners = lax.broadcasted_iota(jnp.int32, (LANES, peers), 0) // blocks_dev
    spread = (owners == lax.broadcasted_iota(jnp.int32, (LANES, peers), 1)).astype(f32)
    link_rows = jnp.concatenate([notes_ref[p][slot_rows : slot_rows + 1, :] for p in range(peers)], 0).astype(f32)
    of_block = dot(spread, link_rows, NN)
    table = jnp.zeros((LANES, LANES), f32)
    for s in range(span):
        picked = jnp.sum(jnp.where(lanes == (rows % blocks_dev) * span + s, of_block, 0.0), 1, keepdims=True)
        table = table + jnp.where(lanes == rows + s - span // 2, picked, 0.0)
    table = table.astype(bf16)
    for i in range(slot_rows):
        linked = dot(hot(slots_ref[i : i + 1, :]), table, NN)
        query_mask_ref[i * LANES : (i + 1) * LANES, :] = jnp.where(linked > 0.5, 0.0, MASKED).astype(bf16)


def keys_of(shards, head):
    return jnp.concatenate([columns(k, head) for k, _, _ in shards], 0)


def values_of(shards, head):
    return jnp.concatenate([columns(v, head) for _, v, _ in shards], 0)


def split(refs, count, hot_ref, at):
    shards = []
    for i in range(count):
        shards.append((refs[i].at[0], refs[i].at[1], hot_ref.at[at[i]]))
    return shards


def masked_scores(q_ref, mask, shards, hots, head, group, first):
    queries = jnp.concatenate([stacked_heads(q_ref, first + head, group), jnp.concatenate([mask] * group, 0)], 1)
    return dot(jnp.concatenate([keys_of(shards, head), hots], 1), queries, NT)


def absorb(scores, values, state):
    factor = HEAD_DIM ** (-0.5) * LOG2_E
    top = jnp.max(scores, 0, keepdims=True)
    if state is not None:
        top = jnp.maximum(top, state[0])
    weights = jnp.exp2((scores - top) * factor)
    total = jnp.sum(weights, 0, keepdims=True)
    mixed = dot(flip(values), weights.astype(jnp.bfloat16), NN)
    if state is not None:
        keep = jnp.exp2((state[0] - top) * factor)
        total = total + state[1] * keep
        mixed = mixed + state[2] * keep
    return top, total, mixed


def backprop(q_ref, g_ref, shards, scores, head, group, first, norm, delta):
    scale = HEAD_DIM ** (-0.5)
    queries, grads = stacked_heads(q_ref, first + head, group), stacked_heads(g_ref, first + head, group)
    weights = jnp.exp2(scores * (scale * LOG2_E) - norm)
    d_scores = (weights * (dot(values_of(shards, head), grads, NT) - delta)).astype(jnp.bfloat16)
    k_grad = dot(d_scores, queries, NN) * scale
    v_grad = dot(weights.astype(jnp.bfloat16), grads, NN)
    return k_grad, v_grad, dot(flip(keys_of(shards, head)), d_scores, NN)


def forward_kernel(at, heads, group, first, q_ref, mask_ref, hot_ref, *refs):
    shards = split(refs, len(at), hot_ref, at)
    state, outs = refs[len(at) : -3], refs[-3:]
    hots = jnp.concatenate([hot[...] for _, _, hot in shards], 0)
    @pl.loop(0, heads)
    def _(head):
        scores = masked_scores(q_ref, mask_ref[...], shards, hots, head, group, first)
        before = [s[head] for s in state] if state else None
        for out, value in zip(outs, absorb(scores, values_of(shards, head), before)):
            out[head] = value


def turn_kernel(at, heads, group, first, q_ref, g_ref, mask_ref, hot_ref, far_ref, top, total, mixed, norm_ref, delta_ref, q_out, grads_out):
    shards = split([far_ref], 1, hot_ref, (at,))
    @pl.loop(0, heads)
    def _(head):
        scores = masked_scores(q_ref, mask_ref[...], shards, hot_ref[at], head, group, first)
        state = absorb(scores, values_of(shards, head), (top[head], total[head], mixed[head]))
        norm = state[0] * (HEAD_DIM ** (-0.5) * LOG2_E) + jnp.log2(state[1])
        attended = (state[2] / state[1]).astype(jnp.bfloat16).astype(jnp.float32)
        grads = stacked_heads(g_ref, first + head, group).astype(jnp.float32).T
        delta = jnp.sum(grads * attended, 0, keepdims=True)
        norm_ref[head], delta_ref[head] = norm, delta
        k_grad, v_grad, q_out[head] = backprop(q_ref, g_ref, shards, scores, head, group, first, norm, delta)
        store_grads([grads_out], head, k_grad, v_grad)


def backward_kernel(at, heads, group, first, q_ref, g_ref, mask_ref, hot_ref, *refs):
    count = len(at)
    shards = split(refs, count, hot_ref, at)
    norm_ref, delta_ref, q_in, q_out = refs[count : count + 4]
    hots = jnp.concatenate([hot[...] for _, _, hot in shards], 0)
    @pl.loop(0, heads)
    def _(head):
        scores = masked_scores(q_ref, mask_ref[...], shards, hots, head, group, first)
        k_grad, v_grad, q_terms = backprop(q_ref, g_ref, shards, scores, head, group, first, norm_ref[head], delta_ref[head])
        store_grads(refs[count + 4 :], head, k_grad, v_grad)
        q_out[head] = q_in[head] + q_terms


def store_grads(outs, head, k_grad, v_grad):
    span = lanes_of(head)
    for i, out in enumerate(outs):
        rows = out.shape[1]
        out[0, :, span] = k_grad[i * rows : (i + 1) * rows].astype(out.dtype)
        out[1, :, span] = v_grad[i * rows : (i + 1) * rows].astype(out.dtype)


def last_kernel(chunks, heads, group, q_ref, g_ref, mask_ref, hot_ref, *refs):
    outs = refs[4 * chunks :]
    rows = q_ref.shape[0]
    for c in range(chunks):
        own_ref, norm_ref, delta_ref, q_in = refs[4 * c : 4 * c + 4]
        shards = split([own_ref], 1, hot_ref, (0,))
        first = c * heads
        @pl.loop(0, heads)
        def _(head):
            scores = masked_scores(q_ref, mask_ref[...], shards, hot_ref[0], head, group, first)
            k_grad, v_grad, q_terms = backprop(q_ref, g_ref, shards, scores, head, group, first, norm_ref[head], delta_ref[head])
            store_grads([outs[1 + c]], head, k_grad, v_grad)
            q_sums = (q_in[head] + q_terms) * HEAD_DIM ** (-0.5)
            for j in range(group):
                at = (first + head) * group + j
                outs[0][:, lanes_of(at)] = q_sums[:, j * rows : (j + 1) * rows].T.astype(jnp.bfloat16)


def gather_plan(queries, key_rows, value_rows, out_grad, owner_slot, block_links):
    rows = queries.shape[0]
    peers = lax.axis_size("seq")
    half = peers // 2
    kv_heads = key_rows.shape[1] // HEAD_DIM
    group = queries.shape[1] // key_rows.shape[1]
    chunks = 2
    heads = kv_heads // chunks
    width = heads * HEAD_DIM
    each = range(chunks)
    f32, bf16 = jnp.float32, jnp.bfloat16
    ring = list(range(0, peers, 2)) + list(range(peers - 1, 0, -2))
    onward = [(ring[i], ring[(i + 1) % peers]) for i in range(peers)]
    back = [(b, a) for a, b in onward]

    def send_on(value):
        return lax.ppermute(value, "seq", onward)

    def send_back(value):
        return lax.ppermute(value, "seq", back)

    def call(kernel, args, outs, products, aliases):
        return pl.pallas_call(
            kernel,
            in_specs=[IN_VMEM] * len(args),
            out_specs=[IN_VMEM] * len(outs),
            out_shape=outs,
            input_output_aliases=aliases,
            cost_estimate=pl.CostEstimate(
                flops=products * heads * group * rows * rows, bytes_accessed=4 * rows * width, transcendentals=0
            ),
            compiler_params=pltpu.CompilerParams(vmem_limit_bytes=16 * 1024 * 1024),
        )(*args)

    span = block_links.shape[1]
    slots = owner_slot.reshape(rows // LANES, LANES)
    links = jnp.pad(block_links.reshape(1, -1), ((0, 0), (0, LANES - block_links.size)))
    notes = jnp.concatenate([slots, links], 0)
    notes = jnp.pad(notes, ((0, -notes.shape[0] % 8), (0, 0)))[None]
    notes = lax.all_to_all(jnp.broadcast_to(notes, (peers,) + notes.shape[1:]), "seq", split_axis=0, concat_axis=0, tiled=True)
    me = lax.axis_index("seq")
    place = jnp.where(me % 2 == 0, me // 2, peers - (me + 1) // 2)
    place = (place - jnp.arange(peers, dtype=jnp.int32)) % peers
    order = jnp.where(place < half, 2 * place, 2 * peers - 1 - 2 * place)

    lines = jax.ShapeDtypeStruct((heads, 1, group * rows), f32)
    talls = jax.ShapeDtypeStruct((heads, HEAD_DIM, group * rows), f32)
    pairs = jax.ShapeDtypeStruct((2, rows, width), f32)

    def forward(c, shards, at, state):
        args = [queries, mask, hot, *shards, *state]
        kernel = functools.partial(forward_kernel, at, heads, group, c * heads)
        aliases = {len(args) - 3 + i: i for i in range(3)} if state else {}
        return call(kernel, args, [lines, lines, talls], 2 * len(at), aliases)

    def backward(c, shards, at, norm, delta, q_sums):
        args = [queries, out_grad, mask, hot, *shards, norm, delta, q_sums]
        kernel = functools.partial(backward_kernel, at, heads, group, c * heads)
        return call(kernel, args, [talls] + [pairs] * len(at), 5 * len(at), {len(args) - 1: 0})

    own = [jnp.stack([key_rows[:, c * width : (c + 1) * width], value_rows[:, c * width : (c + 1) * width]]) for c in each]
    behind, ahead = [[v] for v in own], [[v] for v in own]
    state = [() for _ in each]
    hot = mask = None

    def catch_up(c, r):
        shards, at = [behind[c][r], ahead[c][r]], (r, peers - r)
        if r == 1:
            shards, at = [own[c]] + shards, (0,) + at
        state[c] = tuple(forward(c, shards, at, state[c]))

    for r in range(1, half):
        for c in each:
            low, high = send_on(behind[c][-1]), send_back(ahead[c][-1])
            if r > 1:
                catch_up(c, r - 1)
                low, high, state[c] = lax.optimization_barrier((low, high, state[c]))
            elif c == 0:
                low, high, notes = lax.optimization_barrier((low, high, notes))
            behind[c].append(low)
            ahead[c].append(high)
        if r == 1:
            hot, mask = pl.pallas_call(
                functools.partial(masks_kernel, peers, rows // BLOCK, span),
                in_specs=[IN_SMEM, IN_VMEM, IN_VMEM],
                out_specs=[IN_VMEM] * 2,
                out_shape=[jax.ShapeDtypeStruct((peers, rows, LANES), bf16), jax.ShapeDtypeStruct((rows, LANES), bf16)],
                compiler_params=pltpu.CompilerParams(vmem_limit_bytes=16 * 1024 * 1024),
            )(order, notes, slots)
    far = [send_back(ahead[c][-1]) if c % 2 else send_on(behind[c][-1]) for c in each]
    norm, delta, q_sums, down, up = [[None] * chunks for _ in range(5)]
    for c in each:
        catch_up(c, half - 1)
        norm[c], delta[c], q_sums[c], sums = call(
            functools.partial(turn_kernel, half, heads, group, c * heads),
            [queries, out_grad, mask, hot, far[c], *state[c]],
            [lines, lines, talls, jax.ShapeDtypeStruct(pairs.shape, bf16)],
            7,
            {5: 0, 6: 1, 7: 2},
        )
        if c + 1 < chunks:
            sums, state[c + 1] = lax.optimization_barrier((sums, state[c + 1]))
        else:
            sums, norm[0] = lax.optimization_barrier((sums, norm[0]))
        if c % 2:
            up[c] = send_on(sums)
        else:
            down[c] = send_back(sums)
    for r in range(half - 1, 0, -1):
        for c in each:
            q_sums[c], low, high = backward(c, [behind[c][r], ahead[c][r]], (r, peers - r), norm[c], delta[c], q_sums[c])
            low = low if down[c] is None else low + down[c].astype(f32)
            high = high if up[c] is None else high + up[c].astype(f32)
            after = (c + 1) % chunks
            low, high, norm[after] = lax.optimization_barrier((low.astype(bf16), high.astype(bf16), norm[after]))
            down[c], up[c] = send_back(low), send_on(high)
    args = [queries, out_grad, mask, hot]
    for c in each:
        args += [own[c], norm[c], delta[c], q_sums[c]]
    query_grad, *mine = call(
        functools.partial(last_kernel, chunks, heads, group),
        args,
        [jax.ShapeDtypeStruct(queries.shape, bf16)] + [pairs] * chunks,
        5 * chunks,
        {},
    )
    total = [(mine[c] + down[c].astype(f32) + up[c].astype(f32)).astype(bf16) for c in each]
    return query_grad, jnp.concatenate([t[0] for t in total], 1), jnp.concatenate([t[1] for t in total], 1)


def local(queries, key_rows, value_rows, out_grad, owner_slot, block_links):
    rows = queries.shape[0]
    peers = lax.axis_size("seq")
    q_width, kv_width = queries.shape[1], key_rows.shape[1]
    slots = 4 * peers * max(1, rows // peers // 2)
    gathered = 2 * (peers - 1) * rows * 2 * kv_width
    relayed = slots * (3 * q_width + 4 * kv_width) + 4 * rows * 2 * kv_width
    fits = kv_width % (2 * HEAD_DIM) == 0 and peers > 2 and peers & (peers - 1) == 0 and rows % LANES == 0 and peers * rows // BLOCK <= LANES and block_links.size <= LANES
    plan = gather_plan if fits and gathered <= relayed else relay_plan
    return plan(queries, key_rows, value_rows, out_grad, owner_slot, block_links)


def solution(mesh):
    return jax.shard_map(
        local,
        mesh=mesh,
        in_specs=(
            P(("parts", "seq"), "head"),
            P(("parts", "seq"), "head"),
            P(("parts", "seq"), "head"),
            P(("parts", "seq"), "head"),
            P(("parts", "seq")),
            P(("parts", "seq"), None),
        ),
        out_specs=(
            P(("parts", "seq"), "head"),
            P(("parts", "seq"), "head"),
            P(("parts", "seq"), "head"),
        ),
        check_vma=False,
    )
```

profile of v0, /device:TPU:0, one launch (start us, length us, event | category | flops | bytes accessed | tf_op | source)
XLA Modules:
  0.0 101.5 jit_solution(7044104016080398715)
XLA Ops:
  0.6 1.2 %slice_bitcast_fusion.4 = (bf16[1,256,256]{2,1,0:T(8,128)(2,1)S(1)}, bf16[1,256,256]{2,1,0:T(8,128)(2,1)S(1)}, bf16[1,256,256]{2,1,0:T(8,128)(2,1)S(1)}, bf16[1,256,256]{2,1,0:T(8,128)(2,1)S(1)}) fusion(bf16[256,512]{1,0:T(8,128)(2,1)} %param.8, bf16[256,512]{1,0:T(8,128)(2,1)} %param.7), kind=kLoop, calls=%fused_computation.20 | loop fusion | bytes 1048576 | tf_op jit(solution)/shard_map/stack | solution.py:415
  1.9 3.0 %collective-permute-start.1 = (bf16[2,256,256]{2,1,0:T(8,128)(2,1)S(1)}, bf16[2,256,256]{2,1,0:T(8,128)(2,1)S(1)}, u32[]{:S(2)}, u32[]{:S(2)}) collective-permute-start(bf16[2,256,256]{2,1,0:T(8,128)(2,1)S(1)} %pad_maximum_fusion.refs_0_), channel_id=1, source_target_pairs={{4,0},{8,4},{12,8},{14,12},{10,14},{6,10},{2,6},{0,2},{5,1},{9,5},... | collective-permute-start | bytes 786440 | tf_op jit(solution)/shard_map/ppermute | solution.py:374
  5.1 1.9 %collective-permute-start.3 = (bf16[2,256,256]{2,1,0:T(8,128)(2,1)S(1)}, bf16[2,256,256]{2,1,0:T(8,128)(2,1)S(1)}, u32[]{:S(2)}, u32[]{:S(2)}) collective-permute-start(bf16[2,256,256]{2,1,0:T(8,128)(2,1)S(1)} %pad_maximum_fusion.1.refs_0_.refs_4_), channel_id=1, source_target_pairs={{4,0},{8,4},{12,8},{14,12},{10,14},{6,10},{2,6},{0,2},{5,1},{9,5},... | collective-permute-start | bytes 786440 | tf_op jit(solution)/shard_map/ppermute | solution.py:374
  7.9 13.9 %all_to_all.5.notes_ref = s32[8,8,128]{2,1,0:T(8,128)S(1)} all-to-all(s32[8,8,128]{2,1,0:T(8,128)S(1)} %broadcast_in_dim.2), channel_id=1, replica_groups=mesh['parts'=2,'seq'=8,'head'=2] {'seq'}, dimensions={0} | all-to-all | bytes 65536 | tf_op jit(solution)/shard_map/all_to_all | solution.py:394
  22.2 1.6 %collective-permute-start.7 = (bf16[2,256,256]{2,1,0:T(8,128)(2,1)S(1)}, bf16[2,256,256]{2,1,0:T(8,128)(2,1)S(1)}, u32[]{:S(2)}, u32[]{:S(2)}) collective-permute-start(bf16[2,256,256]{2,1,0:T(8,128)(2,1)S(1)} %collective-permute-done.1.refs_2_.refs_1_), channel_id=1, source_target_pairs={{4,0},{8,4},{12,8},{14,12},{10,14},{6,10},{2,6},{0,2},{5,1},{9,5},... | collective-permute-start | bytes 786440 | tf_op jit(solution)/shard_map/ppermute | solution.py:374
  24.3 1.6 %collective-permute-start.4 = (bf16[2,256,256]{2,1,0:T(8,128)(2,1)S(1)}, bf16[2,256,256]{2,1,0:T(8,128)(2,1)S(1)}, u32[]{:S(2)}, u32[]{:S(2)}) collective-permute-start(bf16[2,256,256]{2,1,0:T(8,128)(2,1)S(1)} %collective-permute-done.2.refs_1_.refs_0_), channel_id=1, source_target_pairs={{0,4},{4,8},{8,12},{12,14},{14,10},{10,6},{6,2},{2,0},{1,5},{5,9},... | collective-permute-start | bytes 786440 | tf_op jit(solution)/shard_map/ppermute | solution.py:371
  25.9 1.1 %shard_map.85 = (bf16[8,256,128]{2,1,0:T(8,128)(2,1)S(1)}, bf16[256,128]{1,0:T(8,128)(2,1)S(1)}) custom-call(s32[8]{0:T(128)S(1)} %compare_select_fusion.2.order_ref, s32[8,8,128]{2,1,0:T(8,128)S(1)} %all_to_all.5.notes_ref, s32[2,128]{1,0:T(2,128)S(1)} %bitcast.18), custom_call_target="tpu_custom_call" | custom-call | tf_op jit(solution)/shard_map/pallas_call | solution.py:437
  27.0 2.9 %shard_map.87 = (f32[2,1,1024]{2,1,0:T(1,128)S(1)}, f32[2,1,1024]{2,1,0:T(1,128)S(1)}, f32[2,128,1024]{2,1,0:T(8,128)S(1)}) custom-call(bf16[256,2048]{1,0:T(8,128)(2,1)S(1)} %copy-done, bf16[256,128]{1,0:T(8,128)(2,1)S(1)} %get-tuple-element.100.mask_ref, bf16[8,256,128]{2,1,0:T(8,128)(2,1)S(1)} %get-tuple-element.101.hot_ref, ...), custom_call_target="tpu_custom_call" | custom-call | flops 3145728 | bytes 262144 | tf_op jit(solution)/shard_map/pallas_call | solution.py:377
  29.9 1.1 %collective-permute-done.6.refs_0_ = bf16[2,256,256]{2,1,0:T(8,128)(2,1)S(1)} collective-permute-done((bf16[2,256,256]{2,1,0:T(8,128)(2,1)S(1)}, bf16[2,256,256]{2,1,0:T(8,128)(2,1)S(1)}, u32[]{:S(2)}, u32[]{:S(2)}) %collective-permute-start.6) | collective-permute-done | bytes 262176 | tf_op jit(solution)/shard_map/ppermute | solution.py:371
  31.4 0.7 collective-permute-start.10
  32.1 1.3 %collective-permute-start.11 = (bf16[2,256,256]{2,1,0:T(8,128)(2,1)S(1)}, bf16[2,256,256]{2,1,0:T(8,128)(2,1)S(1)}, u32[]{:S(2)}, u32[]{:S(2)}) collective-permute-start(bf16[2,256,256]{2,1,0:T(8,128)(2,1)S(1)} %collective-permute-done.7.refs_1_), channel_id=1, source_target_pairs={{4,0},{8,4},{12,8},{14,12},{10,14},{6,10},{2,6},{0,2},{5,1},{9,5},... | collective-permute-start | bytes 786440 | tf_op jit(solution)/shard_map/ppermute | solution.py:374
  33.5 2.9 %shard_map.86 = (f32[2,1,1024]{2,1,0:T(1,128)S(1)}, f32[2,1,1024]{2,1,0:T(1,128)S(1)}, f32[2,128,1024]{2,1,0:T(8,128)S(1)}) custom-call(bf16[256,2048]{1,0:T(8,128)(2,1)S(1)} %copy-done, bf16[256,128]{1,0:T(8,128)(2,1)S(1)} %get-tuple-element.100.mask_ref, bf16[8,256,128]{2,1,0:T(8,128)(2,1)S(1)} %get-tuple-element.101.hot_ref, ...), custom_call_target="tpu_custom_call" | custom-call | flops 3145728 | bytes 262144 | tf_op jit(solution)/shard_map/pallas_call | solution.py:377
  36.4 0.7 collective-permute-done.5.refs_1_
  37.1 0.7 collective-permute-start.8
  37.7 1.3 %collective-permute-start.9 = (bf16[2,256,256]{2,1,0:T(8,128)(2,1)S(1)}, bf16[2,256,256]{2,1,0:T(8,128)(2,1)S(1)}, u32[]{:S(2)}, u32[]{:S(2)}) collective-permute-start(bf16[2,256,256]{2,1,0:T(8,128)(2,1)S(1)} %collective-permute-done.5.refs_1_), channel_id=1, source_target_pairs={{4,0},{8,4},{12,8},{14,12},{10,14},{6,10},{2,6},{0,2},{5,1},{9,5},... | collective-permute-start | bytes 786440 | tf_op jit(solution)/shard_map/ppermute | solution.py:374
  39.1 2.2 %shard_map.89 = (f32[2,1,1024]{2,1,0:T(1,128)S(1)}, f32[2,1,1024]{2,1,0:T(1,128)S(1)}, f32[2,128,1024]{2,1,0:T(8,128)S(1)}) custom-call(bf16[256,2048]{1,0:T(8,128)(2,1)S(1)} %copy-done, bf16[256,128]{1,0:T(8,128)(2,1)S(1)} %get-tuple-element.100.mask_ref, ...), custom_call_target="tpu_custom_call", output_to_operand_aliasing={{0}: (5, {}), {1}: (6, {}), {2}: (7, {})} | custom-call | flops 2097152 | bytes 262144 | tf_op jit(solution)/shard_map/pallas_call | solution.py:377
  41.3 1.0 %collective-permute-done.10.refs_0_ = bf16[2,256,256]{2,1,0:T(8,128)(2,1)S(1)} collective-permute-done((bf16[2,256,256]{2,1,0:T(8,128)(2,1)S(1)}, bf16[2,256,256]{2,1,0:T(8,128)(2,1)S(1)}, u32[]{:S(2)}, u32[]{:S(2)}) %collective-permute-start.10) | collective-permute-done | bytes 262176 | tf_op jit(solution)/shard_map/ppermute | solution.py:371
  42.4 0.9 collective-permute-start.13
  43.4 2.2 %shard_map.88 = (f32[2,1,1024]{2,1,0:T(1,128)S(1)}, f32[2,1,1024]{2,1,0:T(1,128)S(1)}, f32[2,128,1024]{2,1,0:T(8,128)S(1)}) custom-call(bf16[256,2048]{1,0:T(8,128)(2,1)S(1)} %copy-done, bf16[256,128]{1,0:T(8,128)(2,1)S(1)} %get-tuple-element.100.mask_ref, ...), custom_call_target="tpu_custom_call", output_to_operand_aliasing={{0}: (5, {}), {1}: (6, {}), {2}: (7, {})} | custom-call | flops 2097152 | bytes 262144 | tf_op jit(solution)/shard_map/pallas_call | solution.py:377
  45.5 2.3 %collective-permute-done.8.refs_0_ = bf16[2,256,256]{2,1,0:T(8,128)(2,1)S(1)} collective-permute-done((bf16[2,256,256]{2,1,0:T(8,128)(2,1)S(1)}, bf16[2,256,256]{2,1,0:T(8,128)(2,1)S(1)}, u32[]{:S(2)}, u32[]{:S(2)}) %collective-permute-start.8) | collective-permute-done | bytes 262176 | tf_op jit(solution)/shard_map/ppermute | solution.py:371
  48.4 2.2 %shard_map.90 = (f32[2,1,1024]{2,1,0:T(1,128)S(1)}, f32[2,1,1024]{2,1,0:T(1,128)S(1)}, f32[2,128,1024]{2,1,0:T(8,128)S(1)}) custom-call(bf16[256,2048]{1,0:T(8,128)(2,1)S(1)} %copy-done, bf16[256,128]{1,0:T(8,128)(2,1)S(1)} %get-tuple-element.100.mask_ref, ...), custom_call_target="tpu_custom_call", output_to_operand_aliasing={{0}: (5, {}), {1}: (6, {}), {2}: (7, {})} | custom-call | flops 2097152 | bytes 262144 | tf_op jit(solution)/shard_map/pallas_call | solution.py:377
  50.8 3.0 %shard_map.91 = (f32[2,1,1024]{2,1,0:T(1,128)S(1)}, f32[2,1,1024]{2,1,0:T(1,128)S(1)}, f32[2,128,1024]{2,1,0:T(8,128)S(1)}, bf16[2,256,256]{2,1,0:T(8,128)(2,1)S(1)}) custom-call(bf16[256,2048]{1,0:T(8,128)(2,1)S(1)} %copy-done, bf16[256,2048]{1,0:T(8,128)(2,1)S(1)} %copy-done.1, ...), custom_call_target="tpu_custom_call", output_to_operand_aliasing={{0}: (5, {}), {1}: (6, {}), {2}: (7, {})} | custom-call | flops 3670016 | bytes 262144 | tf_op jit(solution)/shard_map/pallas_call | solution.py:377
  53.8 0.7 collective-permute-start.14
  54.5 2.2 %shard_map.92 = (f32[2,1,1024]{2,1,0:T(1,128)S(1)}, f32[2,1,1024]{2,1,0:T(1,128)S(1)}, f32[2,128,1024]{2,1,0:T(8,128)S(1)}) custom-call(bf16[256,2048]{1,0:T(8,128)(2,1)S(1)} %copy-done, bf16[256,128]{1,0:T(8,128)(2,1)S(1)} %get-tuple-element.100.mask_ref, ...), custom_call_target="tpu_custom_call", output_to_operand_aliasing={{0}: (5, {}), {1}: (6, {}), {2}: (7, {})} | custom-call | flops 2097152 | bytes 262144 | tf_op jit(solution)/shard_map/pallas_call | solution.py:377
  56.7 2.9 %shard_map.93 = (f32[2,1,1024]{2,1,0:T(1,128)S(1)}, f32[2,1,1024]{2,1,0:T(1,128)S(1)}, f32[2,128,1024]{2,1,0:T(8,128)S(1)}, bf16[2,256,256]{2,1,0:T(8,128)(2,1)S(1)}) custom-call(bf16[256,2048]{1,0:T(8,128)(2,1)S(1)} %copy-done, bf16[256,2048]{1,0:T(8,128)(2,1)S(1)} %copy-done.1, ...), custom_call_target="tpu_custom_call", output_to_operand_aliasing={{0}: (5, {}), {1}: (6, {}), {2}: (7, {})} | custom-call | flops 3670016 | bytes 262144 | tf_op jit(solution)/shard_map/pallas_call | solution.py:377
  59.6 1.6 %collective-permute-start.15 = (bf16[2,256,256]{2,1,0:T(8,128)(2,1)S(1)}, bf16[2,256,256]{2,1,0:T(8,128)(2,1)S(1)}, u32[]{:S(2)}, u32[]{:S(2)}) collective-permute-start(bf16[2,256,256]{2,1,0:T(8,128)(2,1)S(1)} %get-tuple-element.160), channel_id=1, source_target_pairs={{0,4},{4,8},{8,12},{12,14},{14,10},{10,6},{6,2},{2,0},{1,5},{5,9},... | collective-permute-start | bytes 786440 | tf_op jit(solution)/shard_map/ppermute | solution.py:371
  61.2 2.9 %shard_map.94 = (f32[2,128,1024]{2,1,0:T(8,128)S(1)}, f32[2,256,256]{2,1,0:T(8,128)S(1)}, f32[2,256,256]{2,1,0:T(8,128)S(1)}) custom-call(bf16[256,2048]{1,0:T(8,128)(2,1)S(1)} %copy-done, bf16[256,2048]{1,0:T(8,128)(2,1)S(1)} %copy-done.1, bf16[256,128]{1,0:T(8,128)(2,1)S(1)} %get-tuple-element.100.mask_ref, ...), custom_call_target="tpu_custom_call", output_to_operand_aliasing={{0}: (8, {})} | custom-call | flops 5242880 | bytes 262144 | tf_op jit(solution)/shard_map/pallas_call | solution.py:377
  64.2 0.7 collective-permute-start.16
  65.0 1.3 %collective-permute-start.17 = (bf16[2,256,256]{2,1,0:T(8,128)(2,1)S(1)}, bf16[2,256,256]{2,1,0:T(8,128)(2,1)S(1)}, u32[]{:S(2)}, u32[]{:S(2)}) collective-permute-start(bf16[2,256,256]{2,1,0:T(8,128)(2,1)S(1)} %convert_element_type.86), channel_id=1, source_target_pairs={{0,4},{4,8},{8,12},{12,14},{14,10},{10,6},{6,2},{2,0},{1,5},{5,9},... | collective-permute-start | bytes 786440 | tf_op jit(solution)/shard_map/ppermute | solution.py:371
  66.3 2.9 %shard_map.95 = (f32[2,128,1024]{2,1,0:T(8,128)S(1)}, f32[2,256,256]{2,1,0:T(8,128)S(1)}, f32[2,256,256]{2,1,0:T(8,128)S(1)}) custom-call(bf16[256,2048]{1,0:T(8,128)(2,1)S(1)} %copy-done, bf16[256,2048]{1,0:T(8,128)(2,1)S(1)} %copy-done.1, bf16[256,128]{1,0:T(8,128)(2,1)S(1)} %get-tuple-element.100.mask_ref, ...), custom_call_target="tpu_custom_call", output_to_operand_aliasing={{0}: (8, {})} | custom-call | flops 5242880 | bytes 262144 | tf_op jit(solution)/shard_map/pallas_call | solution.py:377
  69.3 0.7 collective-permute-start.18
  70.1 1.3 %collective-permute-start.19 = (bf16[2,256,256]{2,1,0:T(8,128)(2,1)S(1)}, bf16[2,256,256]{2,1,0:T(8,128)(2,1)S(1)}, u32[]{:S(2)}, u32[]{:S(2)}) collective-permute-start(bf16[2,256,256]{2,1,0:T(8,128)(2,1)S(1)} %add_convert_fusion.10), channel_id=1, source_target_pairs={{0,4},{4,8},{8,12},{12,14},{14,10},{10,6},{6,2},{2,0},{1,5},{5,9},... | collective-permute-start | bytes 786440 | tf_op jit(solution)/shard_map/ppermute | solution.py:371
  71.4 2.9 %shard_map.96 = (f32[2,128,1024]{2,1,0:T(8,128)S(1)}, f32[2,256,256]{2,1,0:T(8,128)S(1)}, f32[2,256,256]{2,1,0:T(8,128)S(1)}) custom-call(bf16[256,2048]{1,0:T(8,128)(2,1)S(1)} %copy-done, bf16[256,2048]{1,0:T(8,128)(2,1)S(1)} %copy-done.1, bf16[256,128]{1,0:T(8,128)(2,1)S(1)} %get-tuple-element.100.mask_ref, ...), custom_call_target="tpu_custom_call", output_to_operand_aliasing={{0}: (8, {})} | custom-call | flops 5242880 | bytes 262144 | tf_op jit(solution)/shard_map/pallas_call | solution.py:377
  74.5 0.7 collective-permute-start.20
  75.2 1.4 %collective-permute-start.21 = (bf16[2,256,256]{2,1,0:T(8,128)(2,1)S(1)}, bf16[2,256,256]{2,1,0:T(8,128)(2,1)S(1)}, u32[]{:S(2)}, u32[]{:S(2)}) collective-permute-start(bf16[2,256,256]{2,1,0:T(8,128)(2,1)S(1)} %add_convert_fusion.8), channel_id=1, source_target_pairs={{0,4},{4,8},{8,12},{12,14},{14,10},{10,6},{6,2},{2,0},{1,5},{5,9},... | collective-permute-start | bytes 786440 | tf_op jit(solution)/shard_map/ppermute | solution.py:371
  76.6 2.9 %shard_map.97 = (f32[2,128,1024]{2,1,0:T(8,128)S(1)}, f32[2,256,256]{2,1,0:T(8,128)S(1)}, f32[2,256,256]{2,1,0:T(8,128)S(1)}) custom-call(bf16[256,2048]{1,0:T(8,128)(2,1)S(1)} %copy-done, bf16[256,2048]{1,0:T(8,128)(2,1)S(1)} %copy-done.1, bf16[256,128]{1,0:T(8,128)(2,1)S(1)} %get-tuple-element.100.mask_ref, ...), custom_call_target="tpu_custom_call", output_to_operand_aliasing={{0}: (8, {})} | custom-call | flops 5242880 | bytes 262144 | tf_op jit(solution)/shard_map/pallas_call | solution.py:377
  79.9 0.9 collective-permute-start.22
  80.8 1.2 %collective-permute-start.23 = (bf16[2,256,256]{2,1,0:T(8,128)(2,1)S(1)}, bf16[2,256,256]{2,1,0:T(8,128)(2,1)S(1)}, u32[]{:S(2)}, u32[]{:S(2)}) collective-permute-start(bf16[2,256,256]{2,1,0:T(8,128)(2,1)S(1)} %add_convert_fusion.6), channel_id=1, source_target_pairs={{0,4},{4,8},{8,12},{12,14},{14,10},{10,6},{6,2},{2,0},{1,5},{5,9},... | collective-permute-start | bytes 786440 | tf_op jit(solution)/shard_map/ppermute | solution.py:371
  82.0 2.9 %shard_map.98 = (f32[2,128,1024]{2,1,0:T(8,128)S(1)}, f32[2,256,256]{2,1,0:T(8,128)S(1)}, f32[2,256,256]{2,1,0:T(8,128)S(1)}) custom-call(bf16[256,2048]{1,0:T(8,128)(2,1)S(1)} %copy-done, bf16[256,2048]{1,0:T(8,128)(2,1)S(1)} %copy-done.1, bf16[256,128]{1,0:T(8,128)(2,1)S(1)} %get-tuple-element.100.mask_ref, ...), custom_call_target="tpu_custom_call", output_to_operand_aliasing={{0}: (8, {})} | custom-call | flops 5242880 | bytes 262144 | tf_op jit(solution)/shard_map/pallas_call | solution.py:377
  85.5 0.9 collective-permute-start.24
  86.4 1.2 %collective-permute-start.25 = (bf16[2,256,256]{2,1,0:T(8,128)(2,1)S(1)}, bf16[2,256,256]{2,1,0:T(8,128)(2,1)S(1)}, u32[]{:S(2)}, u32[]{:S(2)}) collective-permute-start(bf16[2,256,256]{2,1,0:T(8,128)(2,1)S(1)} %add_convert_fusion.4), channel_id=1, source_target_pairs={{0,4},{4,8},{8,12},{12,14},{14,10},{10,6},{6,2},{2,0},{1,5},{5,9},... | collective-permute-start | bytes 786440 | tf_op jit(solution)/shard_map/ppermute | solution.py:371
  87.6 2.9 %shard_map.99 = (f32[2,128,1024]{2,1,0:T(8,128)S(1)}, f32[2,256,256]{2,1,0:T(8,128)S(1)}, f32[2,256,256]{2,1,0:T(8,128)S(1)}) custom-call(bf16[256,2048]{1,0:T(8,128)(2,1)S(1)} %copy-done, bf16[256,2048]{1,0:T(8,128)(2,1)S(1)} %copy-done.1, bf16[256,128]{1,0:T(8,128)(2,1)S(1)} %get-tuple-element.100.mask_ref, ...), custom_call_target="tpu_custom_call", output_to_operand_aliasing={{0}: (8, {})} | custom-call | flops 5242880 | bytes 262144 | tf_op jit(solution)/shard_map/pallas_call | solution.py:377
  91.2 0.9 collective-permute-start.26
  92.0 1.2 %collective-permute-start.27 = (bf16[2,256,256]{2,1,0:T(8,128)(2,1)S(1)}, bf16[2,256,256]{2,1,0:T(8,128)(2,1)S(1)}, u32[]{:S(2)}, u32[]{:S(2)}) collective-permute-start(bf16[2,256,256]{2,1,0:T(8,128)(2,1)S(1)} %add_convert_fusion.2), channel_id=1, source_target_pairs={{0,4},{4,8},{8,12},{12,14},{14,10},{10,6},{6,2},{2,0},{1,5},{5,9},... | collective-permute-start | bytes 786440 | tf_op jit(solution)/shard_map/ppermute | solution.py:371
  93.2 4.7 %shard_map.100 = (bf16[256,2048]{1,0:T(8,128)(2,1)}, f32[2,256,256]{2,1,0:T(8,128)S(1)}, f32[2,256,256]{2,1,0:T(8,128)S(1)}) custom-call(bf16[256,2048]{1,0:T(8,128)(2,1)S(1)} %copy-done, bf16[256,2048]{1,0:T(8,128)(2,1)S(1)} %copy-done.1, bf16[256,128]{1,0:T(8,128)(2,1)S(1)} %get-tuple-element.100.mask_ref, ...), custom_call_target="tpu_custom_call" | custom-call | flops 5242880 | bytes 262144 | tf_op jit(solution)/shard_map/pallas_call | solution.py:377
  98.8 1.2 %collective-permute-done.27 = bf16[2,256,256]{2,1,0:T(8,128)(2,1)S(1)} collective-permute-done((bf16[2,256,256]{2,1,0:T(8,128)(2,1)S(1)}, bf16[2,256,256]{2,1,0:T(8,128)(2,1)S(1)}, u32[]{:S(2)}, u32[]{:S(2)}) %collective-permute-start.27) | collective-permute-done | bytes 262176 | tf_op jit(solution)/shard_map/ppermute | solution.py:371
  100.1 0.7 pad_maximum_fusion.3
  100.8 0.7 pad_maximum_fusion.2
  (59 shorter events, 6.2 us)
Async XLA Ops:
  0.6 26.4 %copy-start = (bf16[256,2048]{1,0:T(8,128)(2,1)S(1)}, bf16[256,2048]{1,0:T(8,128)(2,1)}, u32[]{:S(2)}) copy-start(bf16[256,2048]{1,0:T(8,128)(2,1)} %q_ref.29) | copy-start | bytes 3145732
  1.9 19.9 %collective-permute-start.1 = (bf16[2,256,256]{2,1,0:T(8,128)(2,1)S(1)}, bf16[2,256,256]{2,1,0:T(8,128)(2,1)S(1)}, u32[]{:S(2)}, u32[]{:S(2)}) collective-permute-start(bf16[2,256,256]{2,1,0:T(8,128)(2,1)S(1)} %pad_maximum_fusion.refs_0_), channel_id=1, source_target_pairs={{4,0},{8,4},{12,8},{14,12},{10,14},{6,10},{2,6},{0,2},{5,1},{9,5},... | collective-permute-start | bytes 786440 | tf_op jit(solution)/shard_map/ppermute | solution.py:374
  4.9 16.9 %collective-permute-start = (bf16[2,256,256]{2,1,0:T(8,128)(2,1)S(1)}, bf16[2,256,256]{2,1,0:T(8,128)(2,1)S(1)}, u32[]{:S(2)}, u32[]{:S(2)}) collective-permute-start(bf16[2,256,256]{2,1,0:T(8,128)(2,1)S(1)} %pad_maximum_fusion.refs_0_), channel_id=1, source_target_pairs={{0,4},{4,8},{8,12},{12,14},{14,10},{10,6},{6,2},{2,0},{1,5},{5,9},... | collective-permute-start | bytes 786440 | tf_op jit(solution)/shard_map/ppermute | solution.py:371
  5.0 2.1 %copy-start.3 = (s32[2,5]{1,0:T(2,128)S(1)}, s32[2,5]{1,0:T(2,128)}, u32[]{:S(2)}) copy-start(s32[2,5]{1,0:T(2,128)} %param.11) | copy-start | bytes 124
  5.1 18.8 %collective-permute-start.3 = (bf16[2,256,256]{2,1,0:T(8,128)(2,1)S(1)}, bf16[2,256,256]{2,1,0:T(8,128)(2,1)S(1)}, u32[]{:S(2)}, u32[]{:S(2)}) collective-permute-start(bf16[2,256,256]{2,1,0:T(8,128)(2,1)S(1)} %pad_maximum_fusion.1.refs_0_.refs_4_), channel_id=1, source_target_pairs={{4,0},{8,4},{12,8},{14,12},{10,14},{6,10},{2,6},{0,2},{5,1},{9,5},... | collective-permute-start | bytes 786440 | tf_op jit(solution)/shard_map/ppermute | solution.py:374
  7.0 17.3 %collective-permute-start.2 = (bf16[2,256,256]{2,1,0:T(8,128)(2,1)S(1)}, bf16[2,256,256]{2,1,0:T(8,128)(2,1)S(1)}, u32[]{:S(2)}, u32[]{:S(2)}) collective-permute-start(bf16[2,256,256]{2,1,0:T(8,128)(2,1)S(1)} %pad_maximum_fusion.1.refs_0_.refs_4_), channel_id=1, source_target_pairs={{0,4},{4,8},{8,12},{12,14},{14,10},{10,6},{6,2},{2,0},{1,5},{5,9},... | collective-permute-start | bytes 786440 | tf_op jit(solution)/shard_map/ppermute | solution.py:371
  7.2 0.7 copy-start.2
  21.8 9.2 %collective-permute-start.6 = (bf16[2,256,256]{2,1,0:T(8,128)(2,1)S(1)}, bf16[2,256,256]{2,1,0:T(8,128)(2,1)S(1)}, u32[]{:S(2)}, u32[]{:S(2)}) collective-permute-start(bf16[2,256,256]{2,1,0:T(8,128)(2,1)S(1)} %collective-permute-done.refs_1_.refs_0_), channel_id=1, source_target_pairs={{0,4},{4,8},{8,12},{12,14},{14,10},{10,6},{6,2},{2,0},{1,5},{5,9},... | collective-permute-start | bytes 786440 | tf_op jit(solution)/shard_map/ppermute | solution.py:371
  22.2 9.2 %collective-permute-start.7 = (bf16[2,256,256]{2,1,0:T(8,128)(2,1)S(1)}, bf16[2,256,256]{2,1,0:T(8,128)(2,1)S(1)}, u32[]{:S(2)}, u32[]{:S(2)}) collective-permute-start(bf16[2,256,256]{2,1,0:T(8,128)(2,1)S(1)} %collective-permute-done.1.refs_2_.refs_1_), channel_id=1, source_target_pairs={{4,0},{8,4},{12,8},{14,12},{10,14},{6,10},{2,6},{0,2},{5,1},{9,5},... | collective-permute-start | bytes 786440 | tf_op jit(solution)/shard_map/ppermute | solution.py:374
  23.8 13.2 %collective-permute-start.5 = (bf16[2,256,256]{2,1,0:T(8,128)(2,1)S(1)}, bf16[2,256,256]{2,1,0:T(8,128)(2,1)S(1)}, u32[]{:S(2)}, u32[]{:S(2)}) collective-permute-start(bf16[2,256,256]{2,1,0:T(8,128)(2,1)S(1)} %collective-permute-done.3.refs_2_.refs_1_), channel_id=1, source_target_pairs={{4,0},{8,4},{12,8},{14,12},{10,14},{6,10},{2,6},{0,2},{5,1},{9,5},... | collective-permute-start | bytes 786440 | tf_op jit(solution)/shard_map/ppermute | solution.py:374
  24.3 12.7 %collective-permute-start.4 = (bf16[2,256,256]{2,1,0:T(8,128)(2,1)S(1)}, bf16[2,256,256]{2,1,0:T(8,128)(2,1)S(1)}, u32[]{:S(2)}, u32[]{:S(2)}) collective-permute-start(bf16[2,256,256]{2,1,0:T(8,128)(2,1)S(1)} %collective-permute-done.2.refs_1_.refs_0_), channel_id=1, source_target_pairs={{0,4},{4,8},{8,12},{12,14},{14,10},{10,6},{6,2},{2,0},{1,5},{5,9},... | collective-permute-start | bytes 786440 | tf_op jit(solution)/shard_map/ppermute | solution.py:371
  31.4 10.8 %collective-permute-start.10 = (bf16[2,256,256]{2,1,0:T(8,128)(2,1)S(1)}, bf16[2,256,256]{2,1,0:T(8,128)(2,1)S(1)}, u32[]{:S(2)}, u32[]{:S(2)}) collective-permute-start(bf16[2,256,256]{2,1,0:T(8,128)(2,1)S(1)} %collective-permute-done.6.refs_0_), channel_id=1, source_target_pairs={{0,4},{4,8},{8,12},{12,14},{14,10},{10,6},{6,2},{2,0},{1,5},{5,9},... | collective-permute-start | bytes 786440 | tf_op jit(solution)/shard_map/ppermute | solution.py:371
  32.1 10.3 %collective-permute-start.11 = (bf16[2,256,256]{2,1,0:T(8,128)(2,1)S(1)}, bf16[2,256,256]{2,1,0:T(8,128)(2,1)S(1)}, u32[]{:S(2)}, u32[]{:S(2)}) collective-permute-start(bf16[2,256,256]{2,1,0:T(8,128)(2,1)S(1)} %collective-permute-done.7.refs_1_), channel_id=1, source_target_pairs={{4,0},{8,4},{12,8},{14,12},{10,14},{6,10},{2,6},{0,2},{5,1},{9,5},... | collective-permute-start | bytes 786440 | tf_op jit(solution)/shard_map/ppermute | solution.py:374
  37.1 10.8 %collective-permute-start.8 = (bf16[2,256,256]{2,1,0:T(8,128)(2,1)S(1)}, bf16[2,256,256]{2,1,0:T(8,128)(2,1)S(1)}, u32[]{:S(2)}, u32[]{:S(2)}) collective-permute-start(bf16[2,256,256]{2,1,0:T(8,128)(2,1)S(1)} %collective-permute-done.4.refs_0_), channel_id=1, source_target_pairs={{0,4},{4,8},{8,12},{12,14},{14,10},{10,6},{6,2},{2,0},{1,5},{5,9},... | collective-permute-start | bytes 786440 | tf_op jit(solution)/shard_map/ppermute | solution.py:371
  37.7 10.2 %collective-permute-start.9 = (bf16[2,256,256]{2,1,0:T(8,128)(2,1)S(1)}, bf16[2,256,256]{2,1,0:T(8,128)(2,1)S(1)}, u32[]{:S(2)}, u32[]{:S(2)}) collective-permute-start(bf16[2,256,256]{2,1,0:T(8,128)(2,1)S(1)} %collective-permute-done.5.refs_1_), channel_id=1, source_target_pairs={{4,0},{8,4},{12,8},{14,12},{10,14},{6,10},{2,6},{0,2},{5,1},{9,5},... | collective-permute-start | bytes 786440 | tf_op jit(solution)/shard_map/ppermute | solution.py:374
  42.4 8.4 %collective-permute-start.13 = (bf16[2,256,256]{2,1,0:T(8,128)(2,1)S(1)}, bf16[2,256,256]{2,1,0:T(8,128)(2,1)S(1)}, u32[]{:S(2)}, u32[]{:S(2)}) collective-permute-start(bf16[2,256,256]{2,1,0:T(8,128)(2,1)S(1)} %collective-permute-done.10.refs_0_), channel_id=1, source_target_pairs={{0,4},{4,8},{8,12},{12,14},{14,10},{10,6},{6,2},{2,0},{1,5},{5,9},... | collective-permute-start | bytes 786440 | tf_op jit(solution)/shard_map/ppermute | solution.py:371
  47.9 2.9 %copy-start.1 = (bf16[256,2048]{1,0:T(8,128)(2,1)S(1)}, bf16[256,2048]{1,0:T(8,128)(2,1)}, u32[]{:S(2)}) copy-start(bf16[256,2048]{1,0:T(8,128)(2,1)} %g_ref.17) | copy-start | bytes 3145732
  47.9 8.8 %collective-permute-start.12 = (bf16[2,256,256]{2,1,0:T(8,128)(2,1)S(1)}, bf16[2,256,256]{2,1,0:T(8,128)(2,1)S(1)}, u32[]{:S(2)}, u32[]{:S(2)}) collective-permute-start(bf16[2,256,256]{2,1,0:T(8,128)(2,1)S(1)} %collective-permute-done.9.refs_1_), channel_id=1, source_target_pairs={{4,0},{8,4},{12,8},{14,12},{10,14},{6,10},{2,6},{0,2},{5,1},{9,5},... | collective-permute-start | bytes 786440 | tf_op jit(solution)/shard_map/ppermute | solution.py:374
  53.8 10.4 %collective-permute-start.14 = (bf16[2,256,256]{2,1,0:T(8,128)(2,1)S(1)}, bf16[2,256,256]{2,1,0:T(8,128)(2,1)S(1)}, u32[]{:S(2)}, u32[]{:S(2)}) collective-permute-start(bf16[2,256,256]{2,1,0:T(8,128)(2,1)S(1)} %get-tuple-element.152), channel_id=1, source_target_pairs={{4,0},{8,4},{12,8},{14,12},{10,14},{6,10},{2,6},{0,2},{5,1},{9,5},... | collective-permute-start | bytes 786440 | tf_op jit(solution)/shard_map/ppermute | solution.py:374
  59.6 9.6 %collective-permute-start.15 = (bf16[2,256,256]{2,1,0:T(8,128)(2,1)S(1)}, bf16[2,256,256]{2,1,0:T(8,128)(2,1)S(1)}, u32[]{:S(2)}, u32[]{:S(2)}) collective-permute-start(bf16[2,256,256]{2,1,0:T(8,128)(2,1)S(1)} %get-tuple-element.160), channel_id=1, source_target_pairs={{0,4},{4,8},{8,12},{12,14},{14,10},{10,6},{6,2},{2,0},{1,5},{5,9},... | collective-permute-start | bytes 786440 | tf_op jit(solution)/shard_map/ppermute | solution.py:371
  64.2 10.1 %collective-permute-start.16 = (bf16[2,256,256]{2,1,0:T(8,128)(2,1)S(1)}, bf16[2,256,256]{2,1,0:T(8,128)(2,1)S(1)}, u32[]{:S(2)}, u32[]{:S(2)}) collective-permute-start(bf16[2,256,256]{2,1,0:T(8,128)(2,1)S(1)} %add_convert_fusion.11), channel_id=1, source_target_pairs={{4,0},{8,4},{12,8},{14,12},{10,14},{6,10},{2,6},{0,2},{5,1},{9,5},... | collective-permute-start | bytes 786440 | tf_op jit(solution)/shard_map/ppermute | solution.py:374
  65.0 9.5 %collective-permute-start.17 = (bf16[2,256,256]{2,1,0:T(8,128)(2,1)S(1)}, bf16[2,256,256]{2,1,0:T(8,128)(2,1)S(1)}, u32[]{:S(2)}, u32[]{:S(2)}) collective-permute-start(bf16[2,256,256]{2,1,0:T(8,128)(2,1)S(1)} %convert_element_type.86), channel_id=1, source_target_pairs={{0,4},{4,8},{8,12},{12,14},{14,10},{10,6},{6,2},{2,0},{1,5},{5,9},... | collective-permute-start | bytes 786440 | tf_op jit(solution)/shard_map/ppermute | solution.py:371
  69.3 10.2 %collective-permute-start.18 = (bf16[2,256,256]{2,1,0:T(8,128)(2,1)S(1)}, bf16[2,256,256]{2,1,0:T(8,128)(2,1)S(1)}, u32[]{:S(2)}, u32[]{:S(2)}) collective-permute-start(bf16[2,256,256]{2,1,0:T(8,128)(2,1)S(1)} %convert_element_type.87), channel_id=1, source_target_pairs={{4,0},{8,4},{12,8},{14,12},{10,14},{6,10},{2,6},{0,2},{5,1},{9,5},... | collective-permute-start | bytes 786440 | tf_op jit(solution)/shard_map/ppermute | solution.py:374
  70.1 9.8 %collective-permute-start.19 = (bf16[2,256,256]{2,1,0:T(8,128)(2,1)S(1)}, bf16[2,256,256]{2,1,0:T(8,128)(2,1)S(1)}, u32[]{:S(2)}, u32[]{:S(2)}) collective-permute-start(bf16[2,256,256]{2,1,0:T(8,128)(2,1)S(1)} %add_convert_fusion.10), channel_id=1, source_target_pairs={{0,4},{4,8},{8,12},{12,14},{14,10},{10,6},{6,2},{2,0},{1,5},{5,9},... | collective-permute-start | bytes 786440 | tf_op jit(solution)/shard_map/ppermute | solution.py:371
  74.5 10.4 %collective-permute-start.20 = (bf16[2,256,256]{2,1,0:T(8,128)(2,1)S(1)}, bf16[2,256,256]{2,1,0:T(8,128)(2,1)S(1)}, u32[]{:S(2)}, u32[]{:S(2)}) collective-permute-start(bf16[2,256,256]{2,1,0:T(8,128)(2,1)S(1)} %add_convert_fusion.9), channel_id=1, source_target_pairs={{4,0},{8,4},{12,8},{14,12},{10,14},{6,10},{2,6},{0,2},{5,1},{9,5},... | collective-permute-start | bytes 786440 | tf_op jit(solution)/shard_map/ppermute | solution.py:374
  75.2 10.2 %collective-permute-start.21 = (bf16[2,256,256]{2,1,0:T(8,128)(2,1)S(1)}, bf16[2,256,256]{2,1,0:T(8,128)(2,1)S(1)}, u32[]{:S(2)}, u32[]{:S(2)}) collective-permute-start(bf16[2,256,256]{2,1,0:T(8,128)(2,1)S(1)} %add_convert_fusion.8), channel_id=1, source_target_pairs={{0,4},{4,8},{8,12},{12,14},{14,10},{10,6},{6,2},{2,0},{1,5},{5,9},... | collective-permute-start | bytes 786440 | tf_op jit(solution)/shard_map/ppermute | solution.py:371
  79.9 10.6 %collective-permute-start.22 = (bf16[2,256,256]{2,1,0:T(8,128)(2,1)S(1)}, bf16[2,256,256]{2,1,0:T(8,128)(2,1)S(1)}, u32[]{:S(2)}, u32[]{:S(2)}) collective-permute-start(bf16[2,256,256]{2,1,0:T(8,128)(2,1)S(1)} %add_convert_fusion.7), channel_id=1, source_target_pairs={{4,0},{8,4},{12,8},{14,12},{10,14},{6,10},{2,6},{0,2},{5,1},{9,5},... | collective-permute-start | bytes 786440 | tf_op jit(solution)/shard_map/ppermute | solution.py:374
  80.8 10.3 %collective-permute-start.23 = (bf16[2,256,256]{2,1,0:T(8,128)(2,1)S(1)}, bf16[2,256,256]{2,1,0:T(8,128)(2,1)S(1)}, u32[]{:S(2)}, u32[]{:S(2)}) collective-permute-start(bf16[2,256,256]{2,1,0:T(8,128)(2,1)S(1)} %add_convert_fusion.6), channel_id=1, source_target_pairs={{0,4},{4,8},{8,12},{12,14},{14,10},{10,6},{6,2},{2,0},{1,5},{5,9},... | collective-permute-start | bytes 786440 | tf_op jit(solution)/shard_map/ppermute | solution.py:371
  85.5 12.4 %collective-permute-start.24 = (bf16[2,256,256]{2,1,0:T(8,128)(2,1)S(1)}, bf16[2,256,256]{2,1,0:T(8,128)(2,1)S(1)}, u32[]{:S(2)}, u32[]{:S(2)}) collective-permute-start(bf16[2,256,256]{2,1,0:T(8,128)(2,1)S(1)} %add_convert_fusion.5), channel_id=1, source_target_pairs={{4,0},{8,4},{12,8},{14,12},{10,14},{6,10},{2,6},{0,2},{5,1},{9,5},... | collective-permute-start | bytes 786440 | tf_op jit(solution)/shard_map/ppermute | solution.py:374
  86.4 11.5 %collective-permute-start.25 = (bf16[2,256,256]{2,1,0:T(8,128)(2,1)S(1)}, bf16[2,256,256]{2,1,0:T(8,128)(2,1)S(1)}, u32[]{:S(2)}, u32[]{:S(2)}) collective-permute-start(bf16[2,256,256]{2,1,0:T(8,128)(2,1)S(1)} %add_convert_fusion.4), channel_id=1, source_target_pairs={{0,4},{4,8},{8,12},{12,14},{14,10},{10,6},{6,2},{2,0},{1,5},{5,9},... | collective-permute-start | bytes 786440 | tf_op jit(solution)/shard_map/ppermute | solution.py:371
  91.2 7.6 %collective-permute-start.26 = (bf16[2,256,256]{2,1,0:T(8,128)(2,1)S(1)}, bf16[2,256,256]{2,1,0:T(8,128)(2,1)S(1)}, u32[]{:S(2)}, u32[]{:S(2)}) collective-permute-start(bf16[2,256,256]{2,1,0:T(8,128)(2,1)S(1)} %add_convert_fusion.3), channel_id=1, source_target_pairs={{4,0},{8,4},{12,8},{14,12},{10,14},{6,10},{2,6},{0,2},{5,1},{9,5},... | collective-permute-start | bytes 786440 | tf_op jit(solution)/shard_map/ppermute | solution.py:374
  92.0 7.9 %collective-permute-start.27 = (bf16[2,256,256]{2,1,0:T(8,128)(2,1)S(1)}, bf16[2,256,256]{2,1,0:T(8,128)(2,1)S(1)}, u32[]{:S(2)}, u32[]{:S(2)}) collective-permute-start(bf16[2,256,256]{2,1,0:T(8,128)(2,1)S(1)} %add_convert_fusion.2), channel_id=1, source_target_pairs={{0,4},{4,8},{8,12},{12,14},{14,10},{10,6},{6,2},{2,0},{1,5},{5,9},... | collective-permute-start | bytes 786440 | tf_op jit(solution)/shard_map/ppermute | solution.py:371
where the time goes:
time: 102 us; the launch traced here: 101 us
  Pallas kernels  43.6 us (43%)
  starting transfers between devices  29.5 us (29%)
  blocking collectives  13.9 us (14%)
  waiting for transfers between devices  9.08 us (9%)
  other arithmetic  2.46 us (2%)
  local copies, waits for them, and re-layouts  2.04 us (2%)
    pallas_call x15, Pallas kernels, call(): pl.pallas_call(kernel, in_specs=[IN_VMEM] * len(args), out_specs=[IN_VMEM...  42.5 us
    ppermute x14, starting transfers between devices, send_back(): return lax.ppermute(value, 'seq', back)  15.7 us
    all_to_all x1, blocking collectives, gather_plan(): lax.all_to_all(jnp.broadcast_to(notes, (peers,) + notes.shape[1:]), 'seq'...  13.9 us
    ppermute x14, starting transfers between devices, send_on(): return lax.ppermute(value, 'seq', onward)  13.8 us
    ppermute x14, waiting for transfers between devices, send_on(): return lax.ppermute(value, 'seq', onward)  7.17 us
  transfers between devices with their start and end apart: 28, of which 12 were waited for; matrix products, arithmetic and copies ran while one was open for 1% of the time, Pallas kernels for 43%

commit v1 on v0

--- a/solution.py
+++ b/solution.py
@@ -250,15 +250,16 @@
 
 
 def split(refs, count, hot_ref, at):
-    shards = []
-    for i in range(count):
-        shards.append((refs[i].at[0], refs[i].at[1], hot_ref.at[at[i]]))
+    shards = [(refs[2 * i], refs[2 * i + 1], hot_ref.at[at[i]]) for i in range(count)]
+    if at[0] == 0:
+        keys, values, hot = shards[0]
+        shards[0] = (keys.at[0], values.at[1], hot)
     return shards
 
 
 def masked_scores(q_ref, mask, shards, hots, head, group, first):
     queries = jnp.concatenate([stacked_heads(q_ref, first + head, group), jnp.concatenate([mask] * group, 0)], 1)
-    return dot(jnp.concatenate([keys_of(shards, head), hots], 1), queries, NT)
+    return dot(jnp.concatenate([keys_of(shards, first + head), hots], 1), queries, NT)
 
 
 def absorb(scores, values, state):
@@ -280,30 +281,48 @@
     scale = HEAD_DIM ** (-0.5)
     queries, grads = stacked_heads(q_ref, first + head, group), stacked_heads(g_ref, first + head, group)
     weights = jnp.exp2(scores * (scale * LOG2_E) - norm)
-    d_scores = (weights * (dot(values_of(shards, head), grads, NT) - delta)).astype(jnp.bfloat16)
+    d_scores = (weights * (dot(values_of(shards, first + head), grads, NT) - delta)).astype(jnp.bfloat16)
     k_grad = dot(d_scores, queries, NN) * scale
     v_grad = dot(weights.astype(jnp.bfloat16), grads, NN)
-    return k_grad, v_grad, dot(flip(keys_of(shards, head)), d_scores, NN)
+    return k_grad, v_grad, dot(flip(keys_of(shards, first + head)), d_scores, NN)
 
 
 def forward_kernel(at, heads, group, first, q_ref, mask_ref, hot_ref, *refs):
     shards = split(refs, len(at), hot_ref, at)
-    state, outs = refs[len(at) : -3], refs[-3:]
-    hots = jnp.concatenate([hot[...] for _, _, hot in shards], 0)
+    state, outs = refs[2 * len(at) : -3], refs[-3:]
+    rows = q_ref.shape[0]
+    factor = HEAD_DIM ** (-0.5) * LOG2_E
+
     @pl.loop(0, heads)
     def _(head):
-        scores = masked_scores(q_ref, mask_ref[...], shards, hots, head, group, first)
-        before = [s[head] for s in state] if state else None
-        for out, value in zip(outs, absorb(scores, values_of(shards, head), before)):
-            out[head] = value
-
-
-def turn_kernel(at, heads, group, first, q_ref, g_ref, mask_ref, hot_ref, far_ref, top, total, mixed, norm_ref, delta_ref, q_out, grads_out):
-    shards = split([far_ref], 1, hot_ref, (at,))
+        keys = [jnp.concatenate([columns(k, first + head), hot[...]], 1) for k, _, hot in shards]
+        values = flip(values_of(shards, first + head))
+        scores, tops = [], []
+        for j in range(group):
+            span = slice(j * rows, (j + 1) * rows)
+            query = jnp.concatenate([columns(q_ref, (first + head) * group + j), mask_ref[...]], 1)
+            scores.append([dot(key, query, NT) for key in keys])
+            tops.append(functools.reduce(jnp.maximum, [jnp.max(s, 0, keepdims=True) for s in scores[j]]))
+            if state:
+                tops[j] = jnp.maximum(tops[j], state[0][head][:, span])
+        for j in range(group):
+            span = slice(j * rows, (j + 1) * rows)
+            weights = [jnp.exp2((s - tops[j]) * factor) for s in scores[j]]
+            total = sum(jnp.sum(w, 0, keepdims=True) for w in weights)
+            mixed = dot(values, jnp.concatenate([w.astype(jnp.bfloat16) for w in weights], 0), NN)
+            if state:
+                keep = jnp.exp2((state[0][head][:, span] - tops[j]) * factor)
+                total = total + state[1][head][:, span] * keep
+                mixed = mixed + state[2][head][:, span] * keep
+            outs[0][head, :, span], outs[1][head, :, span], outs[2][head, :, span] = tops[j], total, mixed
+
+
+def turn_kernel(at, heads, group, first, q_ref, g_ref, mask_ref, hot_ref, k_ref, v_ref, top, total, mixed, norm_ref, delta_ref, q_out, grads_out):
+    shards = split([k_ref, v_ref], 1, hot_ref, (at,))
     @pl.loop(0, heads)
     def _(head):
         scores = masked_scores(q_ref, mask_ref[...], shards, hot_ref[at], head, group, first)
-        state = absorb(scores, values_of(shards, head), (top[head], total[head], mixed[head]))
+        state = absorb(scores, values_of(shards, first + head), (top[head], total[head], mixed[head]))
         norm = state[0] * (HEAD_DIM ** (-0.5) * LOG2_E) + jnp.log2(state[1])
         attended = (state[2] / state[1]).astype(jnp.bfloat16).astype(jnp.float32)
         grads = stacked_heads(g_ref, first + head, group).astype(jnp.float32).T
@@ -316,13 +335,13 @@
 def backward_kernel(at, heads, group, first, q_ref, g_ref, mask_ref, hot_ref, *refs):
     count = len(at)
     shards = split(refs, count, hot_ref, at)
-    norm_ref, delta_ref, q_in, q_out = refs[count : count + 4]
+    norm_ref, delta_ref, q_in, q_out = refs[2 * count : 2 * count + 4]
     hots = jnp.concatenate([hot[...] for _, _, hot in shards], 0)
     @pl.loop(0, heads)
     def _(head):
         scores = masked_scores(q_ref, mask_ref[...], shards, hots, head, group, first)
         k_grad, v_grad, q_terms = backprop(q_ref, g_ref, shards, scores, head, group, first, norm_ref[head], delta_ref[head])
-        store_grads(refs[count + 4 :], head, k_grad, v_grad)
+        store_grads(refs[2 * count + 4 :], head, k_grad, v_grad)
         q_out[head] = q_in[head] + q_terms
 
 
@@ -334,22 +353,23 @@
         out[1, :, span] = v_grad[i * rows : (i + 1) * rows].astype(out.dtype)
 
 
-def last_kernel(chunks, heads, group, q_ref, g_ref, mask_ref, hot_ref, *refs):
-    outs = refs[4 * chunks :]
+def last_kernel(heads, group, first, q_ref, g_ref, mask_ref, hot_ref, k_ref, v_ref, norm_ref, delta_ref, *refs):
+    *q_sums, q_out, grads_out = refs
+    shards = split([k_ref, v_ref], 1, hot_ref, (0,))
     rows = q_ref.shape[0]
-    for c in range(chunks):
-        own_ref, norm_ref, delta_ref, q_in = refs[4 * c : 4 * c + 4]
-        shards = split([own_ref], 1, hot_ref, (0,))
-        first = c * heads
-        @pl.loop(0, heads)
-        def _(head):
-            scores = masked_scores(q_ref, mask_ref[...], shards, hot_ref[0], head, group, first)
-            k_grad, v_grad, q_terms = backprop(q_ref, g_ref, shards, scores, head, group, first, norm_ref[head], delta_ref[head])
-            store_grads([outs[1 + c]], head, k_grad, v_grad)
-            q_sums = (q_in[head] + q_terms) * HEAD_DIM ** (-0.5)
-            for j in range(group):
-                at = (first + head) * group + j
-                outs[0][:, lanes_of(at)] = q_sums[:, j * rows : (j + 1) * rows].T.astype(jnp.bfloat16)
+
+    def finish(at, sums):
+        for j in range(group):
+            q_out[:, lanes_of(at * group + j)] = (sums[:, j * rows : (j + 1) * rows] * HEAD_DIM ** (-0.5)).T.astype(jnp.bfloat16)
+
+    @pl.loop(0, heads)
+    def _(head):
+        scores = masked_scores(q_ref, mask_ref[...], shards, hot_ref[0], head, group, first)
+        k_grad, v_grad, q_terms = backprop(q_ref, g_ref, shards, scores, head, group, first, norm_ref[head], delta_ref[head])
+        store_grads([grads_out], head, k_grad, v_grad)
+        finish(first + head, q_sums[-1][head] + q_terms)
+        for c, done in enumerate(q_sums[:-1]):
+            finish(c * heads + head, done[head])
 
 
 def gather_plan(queries, key_rows, value_rows, out_grad, owner_slot, block_links):
@@ -381,7 +401,7 @@
             out_shape=outs,
             input_output_aliases=aliases,
             cost_estimate=pl.CostEstimate(
-                flops=products * heads * group * rows * rows, bytes_accessed=4 * rows * width, transcendentals=0
+                flops=products, bytes_accessed=rows, transcendentals=0
             ),
             compiler_params=pltpu.CompilerParams(vmem_limit_bytes=16 * 1024 * 1024),
         )(*args)
@@ -412,25 +432,40 @@
         kernel = functools.partial(backward_kernel, at, heads, group, c * heads)
         return call(kernel, args, [talls] + [pairs] * len(at), 5 * len(at), {len(args) - 1: 0})
 
-    own = [jnp.stack([key_rows[:, c * width : (c + 1) * width], value_rows[:, c * width : (c + 1) * width]]) for c in each]
+    own = (key_rows, value_rows)
     behind, ahead = [[v] for v in own], [[v] for v in own]
     state = [() for _ in each]
     hot = mask = None
 
+    def pair_at(r):
+        return [side[i][r] for side in (behind, ahead) for i in range(2)]
+
     def catch_up(c, r):
-        shards, at = [behind[c][r], ahead[c][r]], (r, peers - r)
+        shards, at = pair_at(r), (r, peers - r)
         if r == 1:
-            shards, at = [own[c]] + shards, (0,) + at
+            shards, at = [own, own, *shards], (0,) + at
         state[c] = tuple(forward(c, shards, at, state[c]))
 
     for r in range(1, half):
         for c in each:
             low, high = send_on(behind[c][-1]), send_back(ahead[c][-1])
-            if r > 1:
-                catch_up(c, r - 1)
-                low, high, state[c] = lax.optimization_barrier((low, high, state[c]))
-            elif c == 0:
+            if (r, c) == (1, 0):
+                low, high, own = lax.optimization_barrier((low, high, own))
+                own = jnp.stack(own)
+            elif (r, c) == (1, 1):
                 low, high, notes = lax.optimization_barrier((low, high, notes))
+            elif (r, c) == (2, 0):
+                low, high = lax.optimization_barrier((low, high))
+            elif (r, c) == (2, 1):
+                catch_up(0, 1)
+                low, high, state[0] = lax.optimization_barrier((low, high, state[0]))
+                catch_up(1, 1)
+            else:
+                if c:
+                    catch_up(0, r - 1)
+                low, high, state[:] = lax.optimization_barrier((low, high, state))
+                if c:
+                    catch_up(1, r - 1)
             behind[c].append(low)
             ahead[c].append(high)
         if r == 1:
@@ -441,16 +476,16 @@
                 out_shape=[jax.ShapeDtypeStruct((peers, rows, LANES), bf16), jax.ShapeDtypeStruct((rows, LANES), bf16)],
                 compiler_params=pltpu.CompilerParams(vmem_limit_bytes=16 * 1024 * 1024),
             )(order, notes, slots)
-    far = [send_back(ahead[c][-1]) if c % 2 else send_on(behind[c][-1]) for c in each]
+    far = (send_on(behind[0][-1]), send_back(ahead[1][-1]))
     norm, delta, q_sums, down, up = [[None] * chunks for _ in range(5)]
     for c in each:
         catch_up(c, half - 1)
         norm[c], delta[c], q_sums[c], sums = call(
             functools.partial(turn_kernel, half, heads, group, c * heads),
-            [queries, out_grad, mask, hot, far[c], *state[c]],
+            [queries, out_grad, mask, hot, *far, *state[c]],
             [lines, lines, talls, jax.ShapeDtypeStruct(pairs.shape, bf16)],
             7,
-            {5: 0, 6: 1, 7: 2},
+            {6: 0, 7: 1, 8: 2},
         )
         if c + 1 < chunks:
             sums, state[c + 1] = lax.optimization_barrier((sums, state[c + 1]))
@@ -462,24 +497,29 @@
             down[c] = send_back(sums)
     for r in range(half - 1, 0, -1):
         for c in each:
-            q_sums[c], low, high = backward(c, [behind[c][r], ahead[c][r]], (r, peers - r), norm[c], delta[c], q_sums[c])
+            q_sums[c], low, high = backward(c, pair_at(r), (r, peers - r), norm[c], delta[c], q_sums[c])
             low = low if down[c] is None else low + down[c].astype(f32)
             high = high if up[c] is None else high + up[c].astype(f32)
             after = (c + 1) % chunks
             low, high, norm[after] = lax.optimization_barrier((low.astype(bf16), high.astype(bf16), norm[after]))
             down[c], up[c] = send_back(low), send_on(high)
-    args = [queries, out_grad, mask, hot]
+    total = []
     for c in each:
-        args += [own[c], norm[c], delta[c], q_sums[c]]
-    query_grad, *mine = call(
-        functools.partial(last_kernel, chunks, heads, group),
-        args,
-        [jax.ShapeDtypeStruct(queries.shape, bf16)] + [pairs] * chunks,
-        5 * chunks,
-        {},
-    )
-    total = [(mine[c] + down[c].astype(f32) + up[c].astype(f32)).astype(bf16) for c in each]
-    return query_grad, jnp.concatenate([t[0] for t in total], 1), jnp.concatenate([t[1] for t in total], 1)
+        if c + 1 < chunks:
+            q_sums[c], mine = backward(c, [own, own], (0,), norm[c], delta[c], q_sums[c])
+        else:
+            query_grad, mine = call(
+                functools.partial(last_kernel, heads, group, c * heads),
+                [queries, out_grad, mask, hot, own, own, norm[c], delta[c], *q_sums],
+                [jax.ShapeDtypeStruct(queries.shape, bf16), pairs],
+                5,
+                {},
+            )
+        total.append((mine + down[c].astype(f32) + up[c].astype(f32)).astype(bf16))
+        if c + 1 < chunks:
+            total[c], norm[c + 1] = lax.optimization_barrier((total[c], norm[c + 1]))
+    total = jnp.concatenate(total, 2)
+    return query_grad, total[0], total[1]
 
 
 def local(queries, key_rows, value_rows, out_grad, owner_slot, block_links):

time: 102 us -> 97.8 us (0.959)
  blocking collectives: 13.9 us -> 0 us
  starting transfers between devices: 29.5 us -> 37.4 us
  waiting for transfers between devices: 9.08 us -> 11 us
  other arithmetic: 2.46 us -> 3.53 us
    all_to_all x1 -> x0, blocking collectives: 13.9 us -> none  [gather_plan(): lax.all_to_all(jnp.broadcast_to(notes, (peers,) + notes.shape[1:]), 'seq'...]
    all_to_all x0 -> x1, starting transfers between devices: none -> 6.25 us  [gather_plan(): lax.all_to_all(jnp.broadcast_to(notes, (peers,) + notes.shape[1:]), 'seq'...]
    all_to_all x0 -> x1, waiting for transfers between devices: none -> 4.84 us  [gather_plan(): lax.all_to_all(jnp.broadcast_to(notes, (peers,) + notes.shape[1:]), 'seq'...]
    ppermute x14, starting transfers between devices: 13.8 us -> 18 us  [send_on(): return lax.ppermute(value, 'seq', onward)]
    ppermute x14, waiting for transfers between devices: 7.17 us -> 3.89 us  [send_on(): return lax.ppermute(value, 'seq', onward)]
    ppermute x14, starting transfers between devices: 15.7 us -> 13.1 us  [send_back(): return lax.ppermute(value, 'seq', back)]
    concatenate x2 -> x0, other arithmetic: 1.44 us -> none  [the longest x1 0.72 us: gather_plan(): jnp.concatenate([t[1] for t in total], 1)]
    another operation x1 -> x0, local copies, waits for them, and re-layouts: 1.22 us -> none  [gather_plan(): jnp.stack([key_rows[:, c * width:(c + 1) * width], value_rows[:, c * widt...]
  transfers between devices with their start and end apart: 28 -> 29, of which waited for: 12 -> 11; matrix products, arithmetic and copies ran while one was open for 1% -> 4% of each run, Pallas kernels for 43% -> 41%
where the time goes in v1:
time: 97.8 us; the launch traced here: 97.6 us
  Pallas kernels  43.4 us (44%)
  starting transfers between devices  37.4 us (38%)
  waiting for transfers between devices  11 us (11%)
  other arithmetic  3.53 us (4%)
  local copies, waits for them, and re-layouts  1.4 us (1%)
    pallas_call x16, Pallas kernels, call(): pl.pallas_call(kernel, in_specs=[IN_VMEM] * len(args), out_specs=[IN_VMEM...  42.3 us
    ppermute x14, starting transfers between devices, send_on(): return lax.ppermute(value, 'seq', onward)  18 us
    ppermute x14, starting transfers between devices, send_back(): return lax.ppermute(value, 'seq', back)  13.1 us
    all_to_all x1, starting transfers between devices, gather_plan(): lax.all_to_all(jnp.broadcast_to(notes, (peers,) + notes.shape[1:]), 'seq'...  6.25 us
    all_to_all x1, waiting for transfers between devices, gather_plan(): lax.all_to_all(jnp.broadcast_to(notes, (peers,) + notes.shape[1:]), 'seq'...  4.84 us
    ppermute x14, waiting for transfers between devices, send_on(): return lax.ppermute(value, 'seq', onward)  3.89 us
    ppermute x14, waiting for transfers between devices, send_back(): return lax.ppermute(value, 'seq', back)  2.24 us
  transfers between devices with their start and end apart: 29, of which 11 were waited for; matrix products, arithmetic and copies ran while one was open for 4% of the time, Pallas kernels for 41%

profile of v1, /device:TPU:0, one launch (start us, length us, event | category | flops | bytes accessed | tf_op | source)
XLA Modules:
  0.0 97.6 jit_solution(9315411631321096111)
XLA Ops:
  0.6 3.1 %collective-permute-start.2 = (bf16[256,512]{1,0:T(8,128)(2,1)}, bf16[256,512]{1,0:T(8,128)(2,1)S(1)}, u32[]{:S(2)}, u32[]{:S(2)}) collective-permute-start(bf16[256,512]{1,0:T(8,128)(2,1)} %param.7), channel_id=1, source_target_pairs={{0,4},{4,8},{8,12},{12,14},{14,10},{10,6},{6,2},{2,0},{1,5},{5,9},... | collective-permute-start | bytes 786440 | tf_op jit(solution)/shard_map/ppermute | solution.py:391
  3.7 2.0 %collective-permute-start = (bf16[256,512]{1,0:T(8,128)(2,1)}, bf16[256,512]{1,0:T(8,128)(2,1)S(1)}, u32[]{:S(2)}, u32[]{:S(2)}) collective-permute-start(bf16[256,512]{1,0:T(8,128)(2,1)} %param.8), channel_id=1, source_target_pairs={{0,4},{4,8},{8,12},{12,14},{14,10},{10,6},{6,2},{2,0},{1,5},{5,9},... | collective-permute-start | bytes 786440 | tf_op jit(solution)/shard_map/ppermute | solution.py:391
  5.7 0.8 reshape.14
  6.5 0.7 pad_add_fusion
  7.8 6.3 %all-to-all-start = ((s32[8,8,128]{2,1,0:T(8,128)}), s32[8,8,128]{2,1,0:T(8,128)S(1)}, u32[]{:S(2)}, u32[]{:S(2)}) async-start(s32[8,8,128]{2,1,0:T(8,128)} %broadcast_in_dim.2), calls=%async_computation | async-start | bytes 65536 | tf_op jit(solution)/shard_map/all_to_all | solution.py:414
  14.1 2.1 %collective-permute-start.4 = (bf16[256,512]{1,0:T(8,128)(2,1)S(1)}, bf16[256,512]{1,0:T(8,128)(2,1)S(1)}, u32[]{:S(2)}, u32[]{:S(2)}) collective-permute-start(bf16[256,512]{1,0:T(8,128)(2,1)S(1)} %collective-permute-done.2.refs_2_.refs_0_), channel_id=1, source_target_pairs={{0,4},{4,8},{8,12},{12,14},{14,10},{10,6},{6,2},{2,0},{1,5},{5,9},... | collective-permute-start | bytes 786440 | tf_op jit(solution)/shard_map/ppermute | solution.py:391
  16.2 4.8 %all-to-all-done.notes_ref = s32[8,8,128]{2,1,0:T(8,128)S(1)} async-done(((s32[8,8,128]{2,1,0:T(8,128)}), s32[8,8,128]{2,1,0:T(8,128)S(1)}, u32[]{:S(2)}, u32[]{:S(2)}) %all-to-all-start) | async-done | bytes 32800 | tf_op jit(solution)/shard_map/all_to_all | solution.py:414
  21.1 0.7 collective-permute-start.6
  21.8 1.3 %collective-permute-start.7 = (bf16[256,512]{1,0:T(8,128)(2,1)S(1)}, bf16[256,512]{1,0:T(8,128)(2,1)S(1)}, u32[]{:S(2)}, u32[]{:S(2)}) collective-permute-start(bf16[256,512]{1,0:T(8,128)(2,1)S(1)} %collective-permute-done.1.refs_5_.refs_3_), channel_id=1, source_target_pairs={{4,0},{8,4},{12,8},{14,12},{10,14},{6,10},{2,6},{0,2},{5,1},{9,5},... | collective-permute-start | bytes 786440 | tf_op jit(solution)/shard_map/ppermute | solution.py:394
  23.1 1.1 %pad_maximum_fusion.refs_0_.refs_1_.k_ref.v_ref = bf16[2,256,512]{2,1,0:T(8,128)(2,1)S(1)} fusion(bf16[1,256,512]{2,1,0:T(8,128)(2,1)} %bitcast.9, bf16[1,256,512]{2,1,0:T(8,128)(2,1)} %bitcast.10), kind=kLoop, calls=%fused_computation | loop fusion | flops 262144 | bytes 1048576 | tf_op jit(solution)/shard_map/stack | solution.py:454
  24.2 1.3 %collective-permute-done.5.refs_2_ = bf16[256,512]{1,0:T(8,128)(2,1)S(1)} collective-permute-done((bf16[256,512]{1,0:T(8,128)(2,1)S(1)}, bf16[256,512]{1,0:T(8,128)(2,1)S(1)}, u32[]{:S(2)}, u32[]{:S(2)}) %collective-permute-start.5) | collective-permute-done | bytes 262176 | tf_op jit(solution)/shard_map/ppermute | solution.py:394
  25.6 1.5 %collective-permute-start.8 = (bf16[256,512]{1,0:T(8,128)(2,1)S(1)}, bf16[256,512]{1,0:T(8,128)(2,1)S(1)}, u32[]{:S(2)}, u32[]{:S(2)}) collective-permute-start(bf16[256,512]{1,0:T(8,128)(2,1)S(1)} %collective-permute-done.4.refs_0_), channel_id=1, source_target_pairs={{0,4},{4,8},{8,12},{12,14},{14,10},{10,6},{6,2},{2,0},{1,5},{5,9},... | collective-permute-start | bytes 786440 | tf_op jit(solution)/shard_map/ppermute | solution.py:391
  27.6 1.1 %shard_map.85 = (bf16[8,256,128]{2,1,0:T(8,128)(2,1)S(1)}, bf16[256,128]{1,0:T(8,128)(2,1)S(1)}) custom-call(s32[8]{0:T(128)S(1)} %compare_select_fusion.2.order_ref, s32[8,8,128]{2,1,0:T(8,128)S(1)} %all-to-all-done.notes_ref, s32[2,128]{1,0:T(2,128)S(1)} %bitcast.8), custom_call_target="tpu_custom_call" | custom-call | tf_op jit(solution)/shard_map/pallas_call | solution.py:472
  28.7 2.8 %shard_map.86 = (f32[2,1,1024]{2,1,0:T(1,128)S(1)}, f32[2,1,1024]{2,1,0:T(1,128)S(1)}, f32[2,128,1024]{2,1,0:T(8,128)S(1)}) custom-call(bf16[256,2048]{1,0:T(8,128)(2,1)S(1)} %copy-done, bf16[256,128]{1,0:T(8,128)(2,1)S(1)} %get-tuple-element.110.mask_ref, bf16[8,256,128]{2,1,0:T(8,128)(2,1)S(1)} %get-tuple-element.111.hot_ref, ...), custom_call_target="tpu_custom_call" | custom-call | flops 6 | bytes 256 | tf_op jit(solution)/shard_map/pallas_call | solution.py:397
  31.6 1.5 %collective-permute-start.10 = (bf16[256,512]{1,0:T(8,128)(2,1)S(1)}, bf16[256,512]{1,0:T(8,128)(2,1)S(1)}, u32[]{:S(2)}, u32[]{:S(2)}) collective-permute-start(bf16[256,512]{1,0:T(8,128)(2,1)S(1)} %collective-permute-done.6.refs_1_), channel_id=1, source_target_pairs={{0,4},{4,8},{8,12},{12,14},{14,10},{10,6},{6,2},{2,0},{1,5},{5,9},... | collective-permute-start | bytes 786440 | tf_op jit(solution)/shard_map/ppermute | solution.py:391
  33.7 2.9 %shard_map.87 = (f32[2,1,1024]{2,1,0:T(1,128)S(1)}, f32[2,1,1024]{2,1,0:T(1,128)S(1)}, f32[2,128,1024]{2,1,0:T(8,128)S(1)}) custom-call(bf16[256,2048]{1,0:T(8,128)(2,1)S(1)} %copy-done, bf16[256,128]{1,0:T(8,128)(2,1)S(1)} %get-tuple-element.110.mask_ref, bf16[8,256,128]{2,1,0:T(8,128)(2,1)S(1)} %get-tuple-element.111.hot_ref, ...), custom_call_target="tpu_custom_call" | custom-call | flops 6 | bytes 256 | tf_op jit(solution)/shard_map/pallas_call | solution.py:397
  36.8 1.5 %collective-permute-start.12 = (bf16[256,512]{1,0:T(8,128)(2,1)S(1)}, bf16[256,512]{1,0:T(8,128)(2,1)S(1)}, u32[]{:S(2)}, u32[]{:S(2)}) collective-permute-start(bf16[256,512]{1,0:T(8,128)(2,1)S(1)} %collective-permute-done.8.refs_0_), channel_id=1, source_target_pairs={{0,4},{4,8},{8,12},{12,14},{14,10},{10,6},{6,2},{2,0},{1,5},{5,9},... | collective-permute-start | bytes 786440 | tf_op jit(solution)/shard_map/ppermute | solution.py:391
  38.3 2.1 %shard_map.88 = (f32[2,1,1024]{2,1,0:T(1,128)S(1)}, f32[2,1,1024]{2,1,0:T(1,128)S(1)}, f32[2,128,1024]{2,1,0:T(8,128)S(1)}) custom-call(bf16[256,2048]{1,0:T(8,128)(2,1)S(1)} %copy-done, bf16[256,128]{1,0:T(8,128)(2,1)S(1)} %get-tuple-element.110.mask_ref, ...), custom_call_target="tpu_custom_call", output_to_operand_aliasing={{0}: (7, {}), {1}: (8, {}), {2}: (9, {})} | custom-call | flops 4 | bytes 256 | tf_op jit(solution)/shard_map/pallas_call | solution.py:397
  40.4 1.0 %collective-permute-done.10.refs_1_ = bf16[256,512]{1,0:T(8,128)(2,1)S(1)} collective-permute-done((bf16[256,512]{1,0:T(8,128)(2,1)S(1)}, bf16[256,512]{1,0:T(8,128)(2,1)S(1)}, u32[]{:S(2)}, u32[]{:S(2)}) %collective-permute-start.10) | collective-permute-done | bytes 262176 | tf_op jit(solution)/shard_map/ppermute | solution.py:391
  41.4 1.4 %collective-permute-start.13 = (bf16[256,512]{1,0:T(8,128)(2,1)S(1)}, bf16[256,512]{1,0:T(8,128)(2,1)S(1)}, u32[]{:S(2)}, u32[]{:S(2)}) collective-permute-start(bf16[256,512]{1,0:T(8,128)(2,1)S(1)} %collective-permute-done.11.refs_3_), channel_id=1, source_target_pairs={{4,0},{8,4},{12,8},{14,12},{10,14},{6,10},{2,6},{0,2},{5,1},{9,5},... | collective-permute-start | bytes 786440 | tf_op jit(solution)/shard_map/ppermute | solution.py:394
  42.8 2.1 %shard_map.91 = (f32[2,1,1024]{2,1,0:T(1,128)S(1)}, f32[2,1,1024]{2,1,0:T(1,128)S(1)}, f32[2,128,1024]{2,1,0:T(8,128)S(1)}) custom-call(bf16[256,2048]{1,0:T(8,128)(2,1)S(1)} %copy-done, bf16[256,128]{1,0:T(8,128)(2,1)S(1)} %get-tuple-element.110.mask_ref, ...), custom_call_target="tpu_custom_call", output_to_operand_aliasing={{0}: (7, {}), {1}: (8, {}), {2}: (9, {})} | custom-call | flops 4 | bytes 256 | tf_op jit(solution)/shard_map/pallas_call | solution.py:397
  45.0 2.1 %shard_map.89 = (f32[2,1,1024]{2,1,0:T(1,128)S(1)}, f32[2,1,1024]{2,1,0:T(1,128)S(1)}, f32[2,128,1024]{2,1,0:T(8,128)S(1)}) custom-call(bf16[256,2048]{1,0:T(8,128)(2,1)S(1)} %copy-done, bf16[256,128]{1,0:T(8,128)(2,1)S(1)} %get-tuple-element.110.mask_ref, ...), custom_call_target="tpu_custom_call", output_to_operand_aliasing={{0}: (7, {}), {1}: (8, {}), {2}: (9, {})} | custom-call | flops 4 | bytes 256 | tf_op jit(solution)/shard_map/pallas_call | solution.py:397
  47.8 2.9 %shard_map.90 = (f32[2,1,1024]{2,1,0:T(1,128)S(1)}, f32[2,1,1024]{2,1,0:T(1,128)S(1)}, f32[2,128,1024]{2,1,0:T(8,128)S(1)}, bf16[2,256,256]{2,1,0:T(8,128)(2,1)S(1)}) custom-call(bf16[256,2048]{1,0:T(8,128)(2,1)S(1)} %copy-done, bf16[256,2048]{1,0:T(8,128)(2,1)S(1)} %copy-done.1, ...), custom_call_target="tpu_custom_call", output_to_operand_aliasing={{0}: (6, {}), {1}: (7, {}), {2}: (8, {})} | custom-call | flops 7 | bytes 256 | tf_op jit(solution)/shard_map/pallas_call | solution.py:397
  50.7 1.5 %collective-permute-start.14 = (bf16[2,256,256]{2,1,0:T(8,128)(2,1)S(1)}, bf16[2,256,256]{2,1,0:T(8,128)(2,1)S(1)}, u32[]{:S(2)}, u32[]{:S(2)}) collective-permute-start(bf16[2,256,256]{2,1,0:T(8,128)(2,1)S(1)} %get-tuple-element.169), channel_id=1, source_target_pairs={{4,0},{8,4},{12,8},{14,12},{10,14},{6,10},{2,6},{0,2},{5,1},{9,5},... | collective-permute-start | bytes 786440 | tf_op jit(solution)/shard_map/ppermute | solution.py:394
  52.2 2.1 %shard_map.92 = (f32[2,1,1024]{2,1,0:T(1,128)S(1)}, f32[2,1,1024]{2,1,0:T(1,128)S(1)}, f32[2,128,1024]{2,1,0:T(8,128)S(1)}) custom-call(bf16[256,2048]{1,0:T(8,128)(2,1)S(1)} %copy-done, bf16[256,128]{1,0:T(8,128)(2,1)S(1)} %get-tuple-element.110.mask_ref, ...), custom_call_target="tpu_custom_call", output_to_operand_aliasing={{0}: (7, {}), {1}: (8, {}), {2}: (9, {})} | custom-call | flops 4 | bytes 256 | tf_op jit(solution)/shard_map/pallas_call | solution.py:397
  54.3 2.9 %shard_map.93 = (f32[2,1,1024]{2,1,0:T(1,128)S(1)}, f32[2,1,1024]{2,1,0:T(1,128)S(1)}, f32[2,128,1024]{2,1,0:T(8,128)S(1)}, bf16[2,256,256]{2,1,0:T(8,128)(2,1)S(1)}) custom-call(bf16[256,2048]{1,0:T(8,128)(2,1)S(1)} %copy-done, bf16[256,2048]{1,0:T(8,128)(2,1)S(1)} %copy-done.1, ...), custom_call_target="tpu_custom_call", output_to_operand_aliasing={{0}: (6, {}), {1}: (7, {}), {2}: (8, {})} | custom-call | flops 7 | bytes 256 | tf_op jit(solution)/shard_map/pallas_call | solution.py:397
  57.3 0.8 collective-permute-start.15
  58.1 2.9 %shard_map.94 = (f32[2,128,1024]{2,1,0:T(8,128)S(1)}, f32[2,256,256]{2,1,0:T(8,128)S(1)}, f32[2,256,256]{2,1,0:T(8,128)S(1)}) custom-call(bf16[256,2048]{1,0:T(8,128)(2,1)S(1)} %copy-done, bf16[256,2048]{1,0:T(8,128)(2,1)S(1)} %copy-done.1, bf16[256,128]{1,0:T(8,128)(2,1)S(1)} %get-tuple-element.110.mask_ref, ...), custom_call_target="tpu_custom_call", output_to_operand_aliasing={{0}: (10, {})} | custom-call | flops 10 | bytes 256 | tf_op jit(solution)/shard_map/pallas_call | solution.py:397
  61.2 1.5 %collective-permute-start.16 = (bf16[2,256,256]{2,1,0:T(8,128)(2,1)S(1)}, bf16[2,256,256]{2,1,0:T(8,128)(2,1)S(1)}, u32[]{:S(2)}, u32[]{:S(2)}) collective-permute-start(bf16[2,256,256]{2,1,0:T(8,128)(2,1)S(1)} %add_convert_fusion.11), channel_id=1, source_target_pairs={{4,0},{8,4},{12,8},{14,12},{10,14},{6,10},{2,6},{0,2},{5,1},{9,5},... | collective-permute-start | bytes 786440 | tf_op jit(solution)/shard_map/ppermute | solution.py:394
  63.3 2.9 %shard_map.95 = (f32[2,128,1024]{2,1,0:T(8,128)S(1)}, f32[2,256,256]{2,1,0:T(8,128)S(1)}, f32[2,256,256]{2,1,0:T(8,128)S(1)}) custom-call(bf16[256,2048]{1,0:T(8,128)(2,1)S(1)} %copy-done, bf16[256,2048]{1,0:T(8,128)(2,1)S(1)} %copy-done.1, bf16[256,128]{1,0:T(8,128)(2,1)S(1)} %get-tuple-element.110.mask_ref, ...), custom_call_target="tpu_custom_call", output_to_operand_aliasing={{0}: (10, {})} | custom-call | flops 10 | bytes 256 | tf_op jit(solution)/shard_map/pallas_call | solution.py:397
  66.6 1.2 %collective-permute-start.18 = (bf16[2,256,256]{2,1,0:T(8,128)(2,1)S(1)}, bf16[2,256,256]{2,1,0:T(8,128)(2,1)S(1)}, u32[]{:S(2)}, u32[]{:S(2)}) collective-permute-start(bf16[2,256,256]{2,1,0:T(8,128)(2,1)S(1)} %convert_element_type.87), channel_id=1, source_target_pairs={{4,0},{8,4},{12,8},{14,12},{10,14},{6,10},{2,6},{0,2},{5,1},{9,5},... | collective-permute-start | bytes 786440 | tf_op jit(solution)/shard_map/ppermute | solution.py:394
  67.8 0.8 collective-permute-start.19
  68.7 2.9 %shard_map.96 = (f32[2,128,1024]{2,1,0:T(8,128)S(1)}, f32[2,256,256]{2,1,0:T(8,128)S(1)}, f32[2,256,256]{2,1,0:T(8,128)S(1)}) custom-call(bf16[256,2048]{1,0:T(8,128)(2,1)S(1)} %copy-done, bf16[256,2048]{1,0:T(8,128)(2,1)S(1)} %copy-done.1, bf16[256,128]{1,0:T(8,128)(2,1)S(1)} %get-tuple-element.110.mask_ref, ...), custom_call_target="tpu_custom_call", output_to_operand_aliasing={{0}: (10, {})} | custom-call | flops 10 | bytes 256 | tf_op jit(solution)/shard_map/pallas_call | solution.py:397
  72.2 1.2 %collective-permute-start.20 = (bf16[2,256,256]{2,1,0:T(8,128)(2,1)S(1)}, bf16[2,256,256]{2,1,0:T(8,128)(2,1)S(1)}, u32[]{:S(2)}, u32[]{:S(2)}) collective-permute-start(bf16[2,256,256]{2,1,0:T(8,128)(2,1)S(1)} %add_convert_fusion.9), channel_id=1, source_target_pairs={{4,0},{8,4},{12,8},{14,12},{10,14},{6,10},{2,6},{0,2},{5,1},{9,5},... | collective-permute-start | bytes 786440 | tf_op jit(solution)/shard_map/ppermute | solution.py:394
  73.4 0.8 collective-permute-start.21
  74.3 2.9 %shard_map.97 = (f32[2,128,1024]{2,1,0:T(8,128)S(1)}, f32[2,256,256]{2,1,0:T(8,128)S(1)}, f32[2,256,256]{2,1,0:T(8,128)S(1)}) custom-call(bf16[256,2048]{1,0:T(8,128)(2,1)S(1)} %copy-done, bf16[256,2048]{1,0:T(8,128)(2,1)S(1)} %copy-done.1, bf16[256,128]{1,0:T(8,128)(2,1)S(1)} %get-tuple-element.110.mask_ref, ...), custom_call_target="tpu_custom_call", output_to_operand_aliasing={{0}: (10, {})} | custom-call | flops 10 | bytes 256 | tf_op jit(solution)/shard_map/pallas_call | solution.py:397
  77.8 1.2 %collective-permute-start.22 = (bf16[2,256,256]{2,1,0:T(8,128)(2,1)S(1)}, bf16[2,256,256]{2,1,0:T(8,128)(2,1)S(1)}, u32[]{:S(2)}, u32[]{:S(2)}) collective-permute-start(bf16[2,256,256]{2,1,0:T(8,128)(2,1)S(1)} %add_convert_fusion.7), channel_id=1, source_target_pairs={{4,0},{8,4},{12,8},{14,12},{10,14},{6,10},{2,6},{0,2},{5,1},{9,5},... | collective-permute-start | bytes 786440 | tf_op jit(solution)/shard_map/ppermute | solution.py:394
  79.0 0.8 collective-permute-start.23
  79.9 2.9 %shard_map.98 = (f32[2,128,1024]{2,1,0:T(8,128)S(1)}, f32[2,256,256]{2,1,0:T(8,128)S(1)}, f32[2,256,256]{2,1,0:T(8,128)S(1)}) custom-call(bf16[256,2048]{1,0:T(8,128)(2,1)S(1)} %copy-done, bf16[256,2048]{1,0:T(8,128)(2,1)S(1)} %copy-done.1, bf16[256,128]{1,0:T(8,128)(2,1)S(1)} %get-tuple-element.110.mask_ref, ...), custom_call_target="tpu_custom_call", output_to_operand_aliasing={{0}: (10, {})} | custom-call | flops 10 | bytes 256 | tf_op jit(solution)/shard_map/pallas_call | solution.py:397
  83.4 1.2 %collective-permute-start.24 = (bf16[2,256,256]{2,1,0:T(8,128)(2,1)S(1)}, bf16[2,256,256]{2,1,0:T(8,128)(2,1)S(1)}, u32[]{:S(2)}, u32[]{:S(2)}) collective-permute-start(bf16[2,256,256]{2,1,0:T(8,128)(2,1)S(1)} %add_convert_fusion.5), channel_id=1, source_target_pairs={{4,0},{8,4},{12,8},{14,12},{10,14},{6,10},{2,6},{0,2},{5,1},{9,5},... | collective-permute-start | bytes 786440 | tf_op jit(solution)/shard_map/ppermute | solution.py:394
  84.7 0.8 collective-permute-start.25
  85.5 2.9 %shard_map.99 = (f32[2,128,1024]{2,1,0:T(8,128)S(1)}, f32[2,256,256]{2,1,0:T(8,128)S(1)}, f32[2,256,256]{2,1,0:T(8,128)S(1)}) custom-call(bf16[256,2048]{1,0:T(8,128)(2,1)S(1)} %copy-done, bf16[256,2048]{1,0:T(8,128)(2,1)S(1)} %copy-done.1, bf16[256,128]{1,0:T(8,128)(2,1)S(1)} %get-tuple-element.110.mask_ref, ...), custom_call_target="tpu_custom_call", output_to_operand_aliasing={{0}: (10, {})} | custom-call | flops 10 | bytes 256 | tf_op jit(solution)/shard_map/pallas_call | solution.py:397
  89.0 1.2 %collective-permute-start.26 = (bf16[2,256,256]{2,1,0:T(8,128)(2,1)S(1)}, bf16[2,256,256]{2,1,0:T(8,128)(2,1)S(1)}, u32[]{:S(2)}, u32[]{:S(2)}) collective-permute-start(bf16[2,256,256]{2,1,0:T(8,128)(2,1)S(1)} %add_convert_fusion.3), channel_id=1, source_target_pairs={{4,0},{8,4},{12,8},{14,12},{10,14},{6,10},{2,6},{0,2},{5,1},{9,5},... | collective-permute-start | bytes 786440 | tf_op jit(solution)/shard_map/ppermute | solution.py:394
  90.3 0.8 collective-permute-start.27
  91.1 1.7 %shard_map.100 = (f32[2,128,1024]{2,1,0:T(8,128)S(1)}, f32[2,256,256]{2,1,0:T(8,128)S(1)}) custom-call(bf16[256,2048]{1,0:T(8,128)(2,1)S(1)} %copy-done, bf16[256,2048]{1,0:T(8,128)(2,1)S(1)} %copy-done.1, bf16[256,128]{1,0:T(8,128)(2,1)S(1)} %get-tuple-element.110.mask_ref, ...), custom_call_target="tpu_custom_call", output_to_operand_aliasing={{0}: (8, {})} | custom-call | flops 5 | bytes 256 | tf_op jit(solution)/shard_map/pallas_call | solution.py:397
  92.8 0.8 collective-permute-done.25
  93.7 3.0 %shard_map.101 = (bf16[256,2048]{1,0:T(8,128)(2,1)}, f32[2,256,256]{2,1,0:T(8,128)S(1)}) custom-call(bf16[256,2048]{1,0:T(8,128)(2,1)S(1)} %copy-done, bf16[256,2048]{1,0:T(8,128)(2,1)S(1)} %copy-done.1, bf16[256,128]{1,0:T(8,128)(2,1)S(1)} %get-tuple-element.110.mask_ref, bf16[8,256,128]{2,1,0:T(8,128)(2,1)S(1)} %get-tuple-element.111.hot_ref, ...), custom_call_target="tpu_custom_call" | custom-call | flops 5 | bytes 256 | tf_op jit(solution)/shard_map/pallas_call | solution.py:397
  96.8 0.8 fusion.2
  (54 shorter events, 6.4 us)
Async XLA Ops:
  0.6 28.1 %copy-start = (bf16[256,2048]{1,0:T(8,128)(2,1)S(1)}, bf16[256,2048]{1,0:T(8,128)(2,1)}, u32[]{:S(2)}) copy-start(bf16[256,2048]{1,0:T(8,128)(2,1)} %q_ref.31) | copy-start | bytes 3145732
  0.6 13.4 %collective-permute-start.2 = (bf16[256,512]{1,0:T(8,128)(2,1)}, bf16[256,512]{1,0:T(8,128)(2,1)S(1)}, u32[]{:S(2)}, u32[]{:S(2)}) collective-permute-start(bf16[256,512]{1,0:T(8,128)(2,1)} %param.7), channel_id=1, source_target_pairs={{0,4},{4,8},{8,12},{12,14},{14,10},{10,6},{6,2},{2,0},{1,5},{5,9},... | collective-permute-start | bytes 786440 | tf_op jit(solution)/shard_map/ppermute | solution.py:391
  3.7 10.4 %collective-permute-start.3 = (bf16[256,512]{1,0:T(8,128)(2,1)}, bf16[256,512]{1,0:T(8,128)(2,1)S(1)}, u32[]{:S(2)}, u32[]{:S(2)}) collective-permute-start(bf16[256,512]{1,0:T(8,128)(2,1)} %param.7), channel_id=1, source_target_pairs={{4,0},{8,4},{12,8},{14,12},{10,14},{6,10},{2,6},{0,2},{5,1},{9,5},... | collective-permute-start | bytes 786440 | tf_op jit(solution)/shard_map/ppermute | solution.py:394
  3.7 17.3 %collective-permute-start = (bf16[256,512]{1,0:T(8,128)(2,1)}, bf16[256,512]{1,0:T(8,128)(2,1)S(1)}, u32[]{:S(2)}, u32[]{:S(2)}) collective-permute-start(bf16[256,512]{1,0:T(8,128)(2,1)} %param.8), channel_id=1, source_target_pairs={{0,4},{4,8},{8,12},{12,14},{14,10},{10,6},{6,2},{2,0},{1,5},{5,9},... | collective-permute-start | bytes 786440 | tf_op jit(solution)/shard_map/ppermute | solution.py:391
  5.7 15.3 %collective-permute-start.1 = (bf16[256,512]{1,0:T(8,128)(2,1)}, bf16[256,512]{1,0:T(8,128)(2,1)S(1)}, u32[]{:S(2)}, u32[]{:S(2)}) collective-permute-start(bf16[256,512]{1,0:T(8,128)(2,1)} %param.8), channel_id=1, source_target_pairs={{4,0},{8,4},{12,8},{14,12},{10,14},{6,10},{2,6},{0,2},{5,1},{9,5},... | collective-permute-start | bytes 786440 | tf_op jit(solution)/shard_map/ppermute | solution.py:394
  7.8 13.2 %all-to-all-start = ((s32[8,8,128]{2,1,0:T(8,128)}), s32[8,8,128]{2,1,0:T(8,128)S(1)}, u32[]{:S(2)}, u32[]{:S(2)}) async-start(s32[8,8,128]{2,1,0:T(8,128)} %broadcast_in_dim.2), calls=%async_computation | async-start | bytes 65536 | tf_op jit(solution)/shard_map/all_to_all | solution.py:414
  14.1 10.1 %collective-permute-start.4 = (bf16[256,512]{1,0:T(8,128)(2,1)S(1)}, bf16[256,512]{1,0:T(8,128)(2,1)S(1)}, u32[]{:S(2)}, u32[]{:S(2)}) collective-permute-start(bf16[256,512]{1,0:T(8,128)(2,1)S(1)} %collective-permute-done.2.refs_2_.refs_0_), channel_id=1, source_target_pairs={{0,4},{4,8},{8,12},{12,14},{14,10},{10,6},{6,2},{2,0},{1,5},{5,9},... | collective-permute-start | bytes 786440 | tf_op jit(solution)/shard_map/ppermute | solution.py:391
  16.2 9.4 %collective-permute-start.5 = (bf16[256,512]{1,0:T(8,128)(2,1)S(1)}, bf16[256,512]{1,0:T(8,128)(2,1)S(1)}, u32[]{:S(2)}, u32[]{:S(2)}) collective-permute-start(bf16[256,512]{1,0:T(8,128)(2,1)S(1)} %collective-permute-done.3.refs_4_.refs_2_), channel_id=1, source_target_pairs={{4,0},{8,4},{12,8},{14,12},{10,14},{6,10},{2,6},{0,2},{5,1},{9,5},... | collective-permute-start | bytes 786440 | tf_op jit(solution)/shard_map/ppermute | solution.py:394
  21.1 10.5 %collective-permute-start.6 = (bf16[256,512]{1,0:T(8,128)(2,1)S(1)}, bf16[256,512]{1,0:T(8,128)(2,1)S(1)}, u32[]{:S(2)}, u32[]{:S(2)}) collective-permute-start(bf16[256,512]{1,0:T(8,128)(2,1)S(1)} %collective-permute-done.refs_3_.refs_1_), channel_id=1, source_target_pairs={{0,4},{4,8},{8,12},{12,14},{14,10},{10,6},{6,2},{2,0},{1,5},{5,9},... | collective-permute-start | bytes 786440 | tf_op jit(solution)/shard_map/ppermute | solution.py:391
  21.8 9.8 %collective-permute-start.7 = (bf16[256,512]{1,0:T(8,128)(2,1)S(1)}, bf16[256,512]{1,0:T(8,128)(2,1)S(1)}, u32[]{:S(2)}, u32[]{:S(2)}) collective-permute-start(bf16[256,512]{1,0:T(8,128)(2,1)S(1)} %collective-permute-done.1.refs_5_.refs_3_), channel_id=1, source_target_pairs={{4,0},{8,4},{12,8},{14,12},{10,14},{6,10},{2,6},{0,2},{5,1},{9,5},... | collective-permute-start | bytes 786440 | tf_op jit(solution)/shard_map/ppermute | solution.py:394
  23.1 4.5 %copy-start.2 = (s32[256]{0:T(256)S(1)}, s32[256]{0:T(256)}, u32[]{:S(2)}) copy-start(s32[256]{0:T(256)} %param.10) | copy-start | bytes 3076
  25.6 11.0 %collective-permute-start.8 = (bf16[256,512]{1,0:T(8,128)(2,1)S(1)}, bf16[256,512]{1,0:T(8,128)(2,1)S(1)}, u32[]{:S(2)}, u32[]{:S(2)}) collective-permute-start(bf16[256,512]{1,0:T(8,128)(2,1)S(1)} %collective-permute-done.4.refs_0_), channel_id=1, source_target_pairs={{0,4},{4,8},{8,12},{12,14},{14,10},{10,6},{6,2},{2,0},{1,5},{5,9},... | collective-permute-start | bytes 786440 | tf_op jit(solution)/shard_map/ppermute | solution.py:391
  27.0 9.8 %collective-permute-start.9 = (bf16[256,512]{1,0:T(8,128)(2,1)S(1)}, bf16[256,512]{1,0:T(8,128)(2,1)S(1)}, u32[]{:S(2)}, u32[]{:S(2)}) collective-permute-start(bf16[256,512]{1,0:T(8,128)(2,1)S(1)} %collective-permute-done.5.refs_2_), channel_id=1, source_target_pairs={{4,0},{8,4},{12,8},{14,12},{10,14},{6,10},{2,6},{0,2},{5,1},{9,5},... | collective-permute-start | bytes 786440 | tf_op jit(solution)/shard_map/ppermute | solution.py:394
  31.6 9.8 %collective-permute-start.10 = (bf16[256,512]{1,0:T(8,128)(2,1)S(1)}, bf16[256,512]{1,0:T(8,128)(2,1)S(1)}, u32[]{:S(2)}, u32[]{:S(2)}) collective-permute-start(bf16[256,512]{1,0:T(8,128)(2,1)S(1)} %collective-permute-done.6.refs_1_), channel_id=1, source_target_pairs={{0,4},{4,8},{8,12},{12,14},{14,10},{10,6},{6,2},{2,0},{1,5},{5,9},... | collective-permute-start | bytes 786440 | tf_op jit(solution)/shard_map/ppermute | solution.py:391
  33.1 8.3 %collective-permute-start.11 = (bf16[256,512]{1,0:T(8,128)(2,1)S(1)}, bf16[256,512]{1,0:T(8,128)(2,1)S(1)}, u32[]{:S(2)}, u32[]{:S(2)}) collective-permute-start(bf16[256,512]{1,0:T(8,128)(2,1)S(1)} %collective-permute-done.7.refs_3_), channel_id=1, source_target_pairs={{4,0},{8,4},{12,8},{14,12},{10,14},{6,10},{2,6},{0,2},{5,1},{9,5},... | collective-permute-start | bytes 786440 | tf_op jit(solution)/shard_map/ppermute | solution.py:394
  36.8 10.3 %collective-permute-start.12 = (bf16[256,512]{1,0:T(8,128)(2,1)S(1)}, bf16[256,512]{1,0:T(8,128)(2,1)S(1)}, u32[]{:S(2)}, u32[]{:S(2)}) collective-permute-start(bf16[256,512]{1,0:T(8,128)(2,1)S(1)} %collective-permute-done.8.refs_0_), channel_id=1, source_target_pairs={{0,4},{4,8},{8,12},{12,14},{14,10},{10,6},{6,2},{2,0},{1,5},{5,9},... | collective-permute-start | bytes 786440 | tf_op jit(solution)/shard_map/ppermute | solution.py:391
  41.4 6.4 %collective-permute-start.13 = (bf16[256,512]{1,0:T(8,128)(2,1)S(1)}, bf16[256,512]{1,0:T(8,128)(2,1)S(1)}, u32[]{:S(2)}, u32[]{:S(2)}) collective-permute-start(bf16[256,512]{1,0:T(8,128)(2,1)S(1)} %collective-permute-done.11.refs_3_), channel_id=1, source_target_pairs={{4,0},{8,4},{12,8},{14,12},{10,14},{6,10},{2,6},{0,2},{5,1},{9,5},... | collective-permute-start | bytes 786440 | tf_op jit(solution)/shard_map/ppermute | solution.py:394
  45.0 2.8 %copy-start.1 = (bf16[256,2048]{1,0:T(8,128)(2,1)S(1)}, bf16[256,2048]{1,0:T(8,128)(2,1)}, u32[]{:S(2)}) copy-start(bf16[256,2048]{1,0:T(8,128)(2,1)} %g_ref.19) | copy-start | bytes 3145732
  50.7 10.4 %collective-permute-start.14 = (bf16[2,256,256]{2,1,0:T(8,128)(2,1)S(1)}, bf16[2,256,256]{2,1,0:T(8,128)(2,1)S(1)}, u32[]{:S(2)}, u32[]{:S(2)}) collective-permute-start(bf16[2,256,256]{2,1,0:T(8,128)(2,1)S(1)} %get-tuple-element.169), channel_id=1, source_target_pairs={{4,0},{8,4},{12,8},{14,12},{10,14},{6,10},{2,6},{0,2},{5,1},{9,5},... | collective-permute-start | bytes 786440 | tf_op jit(solution)/shard_map/ppermute | solution.py:394
  57.3 9.2 %collective-permute-start.15 = (bf16[2,256,256]{2,1,0:T(8,128)(2,1)S(1)}, bf16[2,256,256]{2,1,0:T(8,128)(2,1)S(1)}, u32[]{:S(2)}, u32[]{:S(2)}) collective-permute-start(bf16[2,256,256]{2,1,0:T(8,128)(2,1)S(1)} %get-tuple-element.177), channel_id=1, source_target_pairs={{0,4},{4,8},{8,12},{12,14},{14,10},{10,6},{6,2},{2,0},{1,5},{5,9},... | collective-permute-start | bytes 786440 | tf_op jit(solution)/shard_map/ppermute | solution.py:391
  61.2 10.4 %collective-permute-start.16 = (bf16[2,256,256]{2,1,0:T(8,128)(2,1)S(1)}, bf16[2,256,256]{2,1,0:T(8,128)(2,1)S(1)}, u32[]{:S(2)}, u32[]{:S(2)}) collective-permute-start(bf16[2,256,256]{2,1,0:T(8,128)(2,1)S(1)} %add_convert_fusion.11), channel_id=1, source_target_pairs={{4,0},{8,4},{12,8},{14,12},{10,14},{6,10},{2,6},{0,2},{5,1},{9,5},... | collective-permute-start | bytes 786440 | tf_op jit(solution)/shard_map/ppermute | solution.py:394
  62.6 9.5 %collective-permute-start.17 = (bf16[2,256,256]{2,1,0:T(8,128)(2,1)S(1)}, bf16[2,256,256]{2,1,0:T(8,128)(2,1)S(1)}, u32[]{:S(2)}, u32[]{:S(2)}) collective-permute-start(bf16[2,256,256]{2,1,0:T(8,128)(2,1)S(1)} %convert_element_type.86), channel_id=1, source_target_pairs={{0,4},{4,8},{8,12},{12,14},{14,10},{10,6},{6,2},{2,0},{1,5},{5,9},... | collective-permute-start | bytes 786440 | tf_op jit(solution)/shard_map/ppermute | solution.py:391
  66.6 10.6 %collective-permute-start.18 = (bf16[2,256,256]{2,1,0:T(8,128)(2,1)S(1)}, bf16[2,256,256]{2,1,0:T(8,128)(2,1)S(1)}, u32[]{:S(2)}, u32[]{:S(2)}) collective-permute-start(bf16[2,256,256]{2,1,0:T(8,128)(2,1)S(1)} %convert_element_type.87), channel_id=1, source_target_pairs={{4,0},{8,4},{12,8},{14,12},{10,14},{6,10},{2,6},{0,2},{5,1},{9,5},... | collective-permute-start | bytes 786440 | tf_op jit(solution)/shard_map/ppermute | solution.py:394
  67.8 9.9 %collective-permute-start.19 = (bf16[2,256,256]{2,1,0:T(8,128)(2,1)S(1)}, bf16[2,256,256]{2,1,0:T(8,128)(2,1)S(1)}, u32[]{:S(2)}, u32[]{:S(2)}) collective-permute-start(bf16[2,256,256]{2,1,0:T(8,128)(2,1)S(1)} %add_convert_fusion.10), channel_id=1, source_target_pairs={{0,4},{4,8},{8,12},{12,14},{14,10},{10,6},{6,2},{2,0},{1,5},{5,9},... | collective-permute-start | bytes 786440 | tf_op jit(solution)/shard_map/ppermute | solution.py:391
  72.2 10.6 %collective-permute-start.20 = (bf16[2,256,256]{2,1,0:T(8,128)(2,1)S(1)}, bf16[2,256,256]{2,1,0:T(8,128)(2,1)S(1)}, u32[]{:S(2)}, u32[]{:S(2)}) collective-permute-start(bf16[2,256,256]{2,1,0:T(8,128)(2,1)S(1)} %add_convert_fusion.9), channel_id=1, source_target_pairs={{4,0},{8,4},{12,8},{14,12},{10,14},{6,10},{2,6},{0,2},{5,1},{9,5},... | collective-permute-start | bytes 786440 | tf_op jit(solution)/shard_map/ppermute | solution.py:394
  73.4 9.9 %collective-permute-start.21 = (bf16[2,256,256]{2,1,0:T(8,128)(2,1)S(1)}, bf16[2,256,256]{2,1,0:T(8,128)(2,1)S(1)}, u32[]{:S(2)}, u32[]{:S(2)}) collective-permute-start(bf16[2,256,256]{2,1,0:T(8,128)(2,1)S(1)} %add_convert_fusion.8), channel_id=1, source_target_pairs={{0,4},{4,8},{8,12},{12,14},{14,10},{10,6},{6,2},{2,0},{1,5},{5,9},... | collective-permute-start | bytes 786440 | tf_op jit(solution)/shard_map/ppermute | solution.py:391
  77.8 10.7 %collective-permute-start.22 = (bf16[2,256,256]{2,1,0:T(8,128)(2,1)S(1)}, bf16[2,256,256]{2,1,0:T(8,128)(2,1)S(1)}, u32[]{:S(2)}, u32[]{:S(2)}) collective-permute-start(bf16[2,256,256]{2,1,0:T(8,128)(2,1)S(1)} %add_convert_fusion.7), channel_id=1, source_target_pairs={{4,0},{8,4},{12,8},{14,12},{10,14},{6,10},{2,6},{0,2},{5,1},{9,5},... | collective-permute-start | bytes 786440 | tf_op jit(solution)/shard_map/ppermute | solution.py:394
  79.0 9.9 %collective-permute-start.23 = (bf16[2,256,256]{2,1,0:T(8,128)(2,1)S(1)}, bf16[2,256,256]{2,1,0:T(8,128)(2,1)S(1)}, u32[]{:S(2)}, u32[]{:S(2)}) collective-permute-start(bf16[2,256,256]{2,1,0:T(8,128)(2,1)S(1)} %add_convert_fusion.6), channel_id=1, source_target_pairs={{0,4},{4,8},{8,12},{12,14},{14,10},{10,6},{6,2},{2,0},{1,5},{5,9},... | collective-permute-start | bytes 786440 | tf_op jit(solution)/shard_map/ppermute | solution.py:391
  83.4 9.4 %collective-permute-start.24 = (bf16[2,256,256]{2,1,0:T(8,128)(2,1)S(1)}, bf16[2,256,256]{2,1,0:T(8,128)(2,1)S(1)}, u32[]{:S(2)}, u32[]{:S(2)}) collective-permute-start(bf16[2,256,256]{2,1,0:T(8,128)(2,1)S(1)} %add_convert_fusion.5), channel_id=1, source_target_pairs={{4,0},{8,4},{12,8},{14,12},{10,14},{6,10},{2,6},{0,2},{5,1},{9,5},... | collective-permute-start | bytes 786440 | tf_op jit(solution)/shard_map/ppermute | solution.py:394
  84.7 8.9 %collective-permute-start.25 = (bf16[2,256,256]{2,1,0:T(8,128)(2,1)S(1)}, bf16[2,256,256]{2,1,0:T(8,128)(2,1)S(1)}, u32[]{:S(2)}, u32[]{:S(2)}) collective-permute-start(bf16[2,256,256]{2,1,0:T(8,128)(2,1)S(1)} %add_convert_fusion.4), channel_id=1, source_target_pairs={{0,4},{4,8},{8,12},{12,14},{14,10},{10,6},{6,2},{2,0},{1,5},{5,9},... | collective-permute-start | bytes 786440 | tf_op jit(solution)/shard_map/ppermute | solution.py:391
  89.0 7.6 %collective-permute-start.26 = (bf16[2,256,256]{2,1,0:T(8,128)(2,1)S(1)}, bf16[2,256,256]{2,1,0:T(8,128)(2,1)S(1)}, u32[]{:S(2)}, u32[]{:S(2)}) collective-permute-start(bf16[2,256,256]{2,1,0:T(8,128)(2,1)S(1)} %add_convert_fusion.3), channel_id=1, source_target_pairs={{4,0},{8,4},{12,8},{14,12},{10,14},{6,10},{2,6},{0,2},{5,1},{9,5},... | collective-permute-start | bytes 786440 | tf_op jit(solution)/shard_map/ppermute | solution.py:394
  90.3 6.4 %collective-permute-start.27 = (bf16[2,256,256]{2,1,0:T(8,128)(2,1)S(1)}, bf16[2,256,256]{2,1,0:T(8,128)(2,1)S(1)}, u32[]{:S(2)}, u32[]{:S(2)}) collective-permute-start(bf16[2,256,256]{2,1,0:T(8,128)(2,1)S(1)} %add_convert_fusion.2), channel_id=1, source_target_pairs={{0,4},{4,8},{8,12},{12,14},{14,10},{10,6},{6,2},{2,0},{1,5},{5,9},... | collective-permute-start | bytes 786440 | tf_op jit(solution)/shard_map/ppermute | solution.py:391

commit v2 on v1

--- a/solution.py
+++ b/solution.py
@@ -188,6 +188,7 @@
 LOG2_E = 1.4426950408889634
 MASKED = -1e30
 LANES = 128
+SAVED_FROM = 3
 NT = (((1,), (1,)), ((), ()))
 NN = (((1,), (0,)), ((), ()))
 IN_VMEM = pl.BlockSpec(memory_space=pltpu.VMEM)
@@ -214,17 +215,19 @@
     return jnp.concatenate([columns(ref, head * group + j) for j in range(group)], 0)
 
 
-def masks_kernel(peers, blocks_dev, span, order_ref, notes_ref, slots_ref, key_hot_ref, query_mask_ref):
+def masks_kernel(peers, blocks_dev, span, slot_rows, notes_ref, key_hot_ref, query_mask_ref):
     f32, bf16 = jnp.float32, jnp.bfloat16
     rows = lax.broadcasted_iota(jnp.int32, (LANES, LANES), 0)
     lanes = lax.broadcasted_iota(jnp.int32, (LANES, LANES), 1)
-    slot_rows = slots_ref.shape[0]
 
     def hot(slots):
         return (rows == slots // BLOCK).astype(f32).T.astype(bf16)
 
+    me = lax.axis_index("seq")
+    place = jnp.where(me % 2 == 0, me // 2, peers - (me + 1) // 2)
     for r in range(peers):
-        shard = notes_ref[order_ref[r]]
+        behind = (place + peers - r) % peers
+        shard = notes_ref[jnp.where(behind < peers // 2, 2 * behind, 2 * peers - 1 - 2 * behind)]
         for i in range(slot_rows):
             key_hot_ref[r, i * LANES : (i + 1) * LANES, :] = hot(shard[i : i + 1, :])
     owners = lax.broadcasted_iota(jnp.int32, (LANES, peers), 0) // blocks_dev
@@ -236,9 +239,8 @@
         picked = jnp.sum(jnp.where(lanes == (rows % blocks_dev) * span + s, of_block, 0.0), 1, keepdims=True)
         table = table + jnp.where(lanes == rows + s - span // 2, picked, 0.0)
     table = table.astype(bf16)
-    for i in range(slot_rows):
-        linked = dot(hot(slots_ref[i : i + 1, :]), table, NN)
-        query_mask_ref[i * LANES : (i + 1) * LANES, :] = jnp.where(linked > 0.5, 0.0, MASKED).astype(bf16)
+    linked = dot(key_hot_ref[0], table, NN)
+    query_mask_ref[...] = jnp.where(linked > 0.5, 0.0, MASKED).astype(bf16)
 
 
 def keys_of(shards, head):
@@ -287,9 +289,9 @@
     return k_grad, v_grad, dot(flip(keys_of(shards, first + head)), d_scores, NN)
 
 
-def forward_kernel(at, heads, group, first, q_ref, mask_ref, hot_ref, *refs):
+def forward_kernel(at, heads, group, first, saved, q_ref, mask_ref, hot_ref, *refs):
     shards = split(refs, len(at), hot_ref, at)
-    state, outs = refs[2 * len(at) : -3], refs[-3:]
+    state, outs = refs[2 * len(at) : -3 - saved], refs[len(refs) - 3 - saved :]
     rows = q_ref.shape[0]
     factor = HEAD_DIM ** (-0.5) * LOG2_E
 
@@ -302,6 +304,9 @@
             span = slice(j * rows, (j + 1) * rows)
             query = jnp.concatenate([columns(q_ref, (first + head) * group + j), mask_ref[...]], 1)
             scores.append([dot(key, query, NT) for key in keys])
+            if saved:
+                for i, part in enumerate(scores[j]):
+                    outs[3][head, i * rows : (i + 1) * rows, span] = part
             tops.append(functools.reduce(jnp.maximum, [jnp.max(s, 0, keepdims=True) for s in scores[j]]))
             if state:
                 tops[j] = jnp.maximum(tops[j], state[0][head][:, span])
@@ -332,14 +337,16 @@
         store_grads([grads_out], head, k_grad, v_grad)
 
 
-def backward_kernel(at, heads, group, first, q_ref, g_ref, mask_ref, hot_ref, *refs):
+def backward_kernel(at, heads, group, first, saved, q_ref, g_ref, mask_ref, hot_ref, *refs):
     count = len(at)
+    if saved:
+        scores_ref, *refs = refs
     shards = split(refs, count, hot_ref, at)
     norm_ref, delta_ref, q_in, q_out = refs[2 * count : 2 * count + 4]
     hots = jnp.concatenate([hot[...] for _, _, hot in shards], 0)
     @pl.loop(0, heads)
     def _(head):
-        scores = masked_scores(q_ref, mask_ref[...], shards, hots, head, group, first)
+        scores = scores_ref[head] if saved else masked_scores(q_ref, mask_ref[...], shards, hots, head, group, first)
         k_grad, v_grad, q_terms = backprop(q_ref, g_ref, shards, scores, head, group, first, norm_ref[head], delta_ref[head])
         store_grads(refs[2 * count + 4 :], head, k_grad, v_grad)
         q_out[head] = q_in[head] + q_terms
@@ -353,23 +360,16 @@
         out[1, :, span] = v_grad[i * rows : (i + 1) * rows].astype(out.dtype)
 
 
-def last_kernel(heads, group, first, q_ref, g_ref, mask_ref, hot_ref, k_ref, v_ref, norm_ref, delta_ref, *refs):
-    *q_sums, q_out, grads_out = refs
-    shards = split([k_ref, v_ref], 1, hot_ref, (0,))
-    rows = q_ref.shape[0]
-
-    def finish(at, sums):
-        for j in range(group):
-            q_out[:, lanes_of(at * group + j)] = (sums[:, j * rows : (j + 1) * rows] * HEAD_DIM ** (-0.5)).T.astype(jnp.bfloat16)
+def finish_kernel(heads, group, *refs):
+    *q_sums, q_out = refs
+    rows = q_out.shape[0]
 
     @pl.loop(0, heads)
     def _(head):
-        scores = masked_scores(q_ref, mask_ref[...], shards, hot_ref[0], head, group, first)
-        k_grad, v_grad, q_terms = backprop(q_ref, g_ref, shards, scores, head, group, first, norm_ref[head], delta_ref[head])
-        store_grads([grads_out], head, k_grad, v_grad)
-        finish(first + head, q_sums[-1][head] + q_terms)
-        for c, done in enumerate(q_sums[:-1]):
-            finish(c * heads + head, done[head])
+        for c, sums in enumerate(q_sums):
+            for j in range(group):
+                part = sums[head, :, j * rows : (j + 1) * rows] * HEAD_DIM ** (-0.5)
+                q_out[:, lanes_of((c * heads + head) * group + j)] = part.T.astype(jnp.bfloat16)
 
 
 def gather_plan(queries, key_rows, value_rows, out_grad, owner_slot, block_links):
@@ -403,7 +403,7 @@
             cost_estimate=pl.CostEstimate(
                 flops=products, bytes_accessed=rows, transcendentals=0
             ),
-            compiler_params=pltpu.CompilerParams(vmem_limit_bytes=16 * 1024 * 1024),
+            compiler_params=pltpu.CompilerParams(vmem_limit_bytes=12 * 1024 * 1024),
         )(*args)
 
     span = block_links.shape[1]
@@ -412,30 +412,28 @@
     notes = jnp.concatenate([slots, links], 0)
     notes = jnp.pad(notes, ((0, -notes.shape[0] % 8), (0, 0)))[None]
     notes = lax.all_to_all(jnp.broadcast_to(notes, (peers,) + notes.shape[1:]), "seq", split_axis=0, concat_axis=0, tiled=True)
-    me = lax.axis_index("seq")
-    place = jnp.where(me % 2 == 0, me // 2, peers - (me + 1) // 2)
-    place = (place - jnp.arange(peers, dtype=jnp.int32)) % peers
-    order = jnp.where(place < half, 2 * place, 2 * peers - 1 - 2 * place)
-
     lines = jax.ShapeDtypeStruct((heads, 1, group * rows), f32)
     talls = jax.ShapeDtypeStruct((heads, HEAD_DIM, group * rows), f32)
     pairs = jax.ShapeDtypeStruct((2, rows, width), f32)
 
-    def forward(c, shards, at, state):
+    def forward(c, shards, at, state, saved):
         args = [queries, mask, hot, *shards, *state]
-        kernel = functools.partial(forward_kernel, at, heads, group, c * heads)
+        kernel = functools.partial(forward_kernel, at, heads, group, c * heads, saved)
         aliases = {len(args) - 3 + i: i for i in range(3)} if state else {}
-        return call(kernel, args, [lines, lines, talls], 2 * len(at), aliases)
-
-    def backward(c, shards, at, norm, delta, q_sums):
-        args = [queries, out_grad, mask, hot, *shards, norm, delta, q_sums]
-        kernel = functools.partial(backward_kernel, at, heads, group, c * heads)
+        kept = [jax.ShapeDtypeStruct((heads, len(at) * rows, group * rows), f32)] * saved
+        return call(kernel, args, [lines, lines, talls] + kept, 2 * len(at), aliases)
+
+    def backward(c, shards, at, norm, delta, q_sums, scores=None):
+        saved = scores is not None
+        args = [queries, out_grad, mask, hot, *([scores] * saved), *shards, norm, delta, q_sums]
+        kernel = functools.partial(backward_kernel, at, heads, group, c * heads, saved)
         return call(kernel, args, [talls] + [pairs] * len(at), 5 * len(at), {len(args) - 1: 0})
 
     own = (key_rows, value_rows)
     behind, ahead = [[v] for v in own], [[v] for v in own]
     state = [() for _ in each]
     hot = mask = None
+    scores = {}
 
     def pair_at(r):
         return [side[i][r] for side in (behind, ahead) for i in range(2)]
@@ -444,7 +442,9 @@
         shards, at = pair_at(r), (r, peers - r)
         if r == 1:
             shards, at = [own, own, *shards], (0,) + at
-        state[c] = tuple(forward(c, shards, at, state[c]))
+        *state[c], = forward(c, shards, at, state[c], r >= SAVED_FROM)
+        if r >= SAVED_FROM:
+            scores[c, r] = state[c].pop()
 
     for r in range(1, half):
         for c in each:
@@ -455,7 +455,7 @@
             elif (r, c) == (1, 1):
                 low, high, notes = lax.optimization_barrier((low, high, notes))
             elif (r, c) == (2, 0):
-                low, high = lax.optimization_barrier((low, high))
+                low, high, own = lax.optimization_barrier((low, high, own))
             elif (r, c) == (2, 1):
                 catch_up(0, 1)
                 low, high, state[0] = lax.optimization_barrier((low, high, state[0]))
@@ -470,16 +470,18 @@
             ahead[c].append(high)
         if r == 1:
             hot, mask = pl.pallas_call(
-                functools.partial(masks_kernel, peers, rows // BLOCK, span),
-                in_specs=[IN_SMEM, IN_VMEM, IN_VMEM],
+                functools.partial(masks_kernel, peers, rows // BLOCK, span, rows // LANES),
+                in_specs=[IN_VMEM],
                 out_specs=[IN_VMEM] * 2,
                 out_shape=[jax.ShapeDtypeStruct((peers, rows, LANES), bf16), jax.ShapeDtypeStruct((rows, LANES), bf16)],
-                compiler_params=pltpu.CompilerParams(vmem_limit_bytes=16 * 1024 * 1024),
-            )(order, notes, slots)
+                compiler_params=pltpu.CompilerParams(vmem_limit_bytes=12 * 1024 * 1024),
+            )(notes)
     far = (send_on(behind[0][-1]), send_back(ahead[1][-1]))
     norm, delta, q_sums, down, up = [[None] * chunks for _ in range(5)]
     for c in each:
         catch_up(c, half - 1)
+    state[:] = lax.optimization_barrier(state)
+    for c in each:
         norm[c], delta[c], q_sums[c], sums = call(
             functools.partial(turn_kernel, half, heads, group, c * heads),
             [queries, out_grad, mask, hot, *far, *state[c]],
@@ -497,7 +499,7 @@
             down[c] = send_back(sums)
     for r in range(half - 1, 0, -1):
         for c in each:
-            q_sums[c], low, high = backward(c, pair_at(r), (r, peers - r), norm[c], delta[c], q_sums[c])
+            q_sums[c], low, high = backward(c, pair_at(r), (r, peers - r), norm[c], delta[c], q_sums[c], scores.get((c, r)))
             low = low if down[c] is None else low + down[c].astype(f32)
             high = high if up[c] is None else high + up[c].astype(f32)
             after = (c + 1) % chunks
@@ -505,19 +507,12 @@
             down[c], up[c] = send_back(low), send_on(high)
     total = []
     for c in each:
-        if c + 1 < chunks:
-            q_sums[c], mine = backward(c, [own, own], (0,), norm[c], delta[c], q_sums[c])
-        else:
-            query_grad, mine = call(
-                functools.partial(last_kernel, heads, group, c * heads),
-                [queries, out_grad, mask, hot, own, own, norm[c], delta[c], *q_sums],
-                [jax.ShapeDtypeStruct(queries.shape, bf16), pairs],
-                5,
-                {},
-            )
+        q_sums[c], mine = backward(c, [own, own], (0,), norm[c], delta[c], q_sums[c])
         total.append((mine + down[c].astype(f32) + up[c].astype(f32)).astype(bf16))
-        if c + 1 < chunks:
-            total[c], norm[c + 1] = lax.optimization_barrier((total[c], norm[c + 1]))
+    total[0], q_sums = lax.optimization_barrier((total[0], q_sums))
+    (query_grad,) = call(
+        functools.partial(finish_kernel, heads, group), q_sums, [jax.ShapeDtypeStruct(queries.shape, bf16)], 0, {}
+    )
     total = jnp.concatenate(total, 2)
     return query_grad, total[0], total[1]
 

time: 97.8 us -> 97.4 us (level)
  Pallas kernels: 43.4 us -> 41.9 us
  local copies, waits for them, and re-layouts: 1.4 us -> 2.62 us
    unnamed x6 -> x4, local copies, waits for them, and re-layouts: 0.02 us -> 1.23 us
    ppermute x14, waiting for transfers between devices: 2.24 us -> 1.07 us  [send_back(): return lax.ppermute(value, 'seq', back)]
    ppermute x14, waiting for transfers between devices: 3.89 us -> 4.97 us  [send_on(): return lax.ppermute(value, 'seq', onward)]
    pallas_call x16 -> x17, Pallas kernels: 42.3 us -> 41.4 us  [call(): pl.pallas_call(kernel, in_specs=[IN_VMEM] * len(args), out_specs=[IN_VMEM...]
  transfers between devices with their start and end apart: 29 -> 29, of which waited for: 11 -> 10; matrix products, arithmetic and copies ran while one was open for 4% -> 4% of each run, Pallas kernels for 41% -> 40%
where the time goes in v2:
time: 97.4 us; the launch traced here: 97.1 us
  Pallas kernels  41.9 us (43%)
  starting transfers between devices  37.3 us (38%)
  waiting for transfers between devices  10.9 us (11%)
  other arithmetic  3.39 us (3%)
  local copies, waits for them, and re-layouts  2.62 us (3%)
  between operations  1 us (1%)
    pallas_call x17, Pallas kernels, call(): pl.pallas_call(kernel, in_specs=[IN_VMEM] * len(args), out_specs=[IN_VMEM...  41.4 us
    ppermute x14, starting transfers between devices, send_on(): return lax.ppermute(value, 'seq', onward)  17.8 us
    ppermute x14, starting transfers between devices, send_back(): return lax.ppermute(value, 'seq', back)  13.3 us
    all_to_all x1, starting transfers between devices, gather_plan(): lax.all_to_all(jnp.broadcast_to(notes, (peers,) + notes.shape[1:]), 'seq'...  6.25 us
    ppermute x14, waiting for transfers between devices, send_on(): return lax.ppermute(value, 'seq', onward)  4.97 us
    all_to_all x1, waiting for transfers between devices, gather_plan(): lax.all_to_all(jnp.broadcast_to(notes, (peers,) + notes.shape[1:]), 'seq'...  4.84 us
  transfers between devices with their start and end apart: 29, of which 10 were waited for; matrix products, arithmetic and copies ran while one was open for 4% of the time, Pallas kernels for 40%

profile of v2, /device:TPU:0, one launch (start us, length us, event | category | flops | bytes accessed | tf_op | source)
XLA Modules:
  0.0 97.1 jit_solution(3750774401302044078)
XLA Ops:
  0.6 3.1 %collective-permute-start.2 = (bf16[256,512]{1,0:T(8,128)(2,1)}, bf16[256,512]{1,0:T(8,128)(2,1)S(1)}, u32[]{:S(2)}, u32[]{:S(2)}) collective-permute-start(bf16[256,512]{1,0:T(8,128)(2,1)} %param.7), channel_id=1, source_target_pairs={{0,4},{4,8},{8,12},{12,14},{14,10},{10,6},{6,2},{2,0},{1,5},{5,9},... | collective-permute-start | bytes 786440 | tf_op jit(solution)/shard_map/ppermute | solution.py:391
  3.7 2.0 %collective-permute-start = (bf16[256,512]{1,0:T(8,128)(2,1)}, bf16[256,512]{1,0:T(8,128)(2,1)S(1)}, u32[]{:S(2)}, u32[]{:S(2)}) collective-permute-start(bf16[256,512]{1,0:T(8,128)(2,1)} %param.8), channel_id=1, source_target_pairs={{0,4},{4,8},{8,12},{12,14},{14,10},{10,6},{6,2},{2,0},{1,5},{5,9},... | collective-permute-start | bytes 786440 | tf_op jit(solution)/shard_map/ppermute | solution.py:391
  5.7 0.8 reshape.14
  6.5 0.7 pad_add_fusion
  7.8 6.3 %all-to-all-start = ((s32[8,8,128]{2,1,0:T(8,128)}), s32[8,8,128]{2,1,0:T(8,128)S(1)}, u32[]{:S(2)}, u32[]{:S(2)}) async-start(s32[8,8,128]{2,1,0:T(8,128)} %broadcast_in_dim.2), calls=%async_computation | async-start | bytes 65536 | tf_op jit(solution)/shard_map/all_to_all | solution.py:414
  14.1 2.1 %collective-permute-start.4 = (bf16[256,512]{1,0:T(8,128)(2,1)S(1)}, bf16[256,512]{1,0:T(8,128)(2,1)S(1)}, u32[]{:S(2)}, u32[]{:S(2)}) collective-permute-start(bf16[256,512]{1,0:T(8,128)(2,1)S(1)} %collective-permute-done.2.refs_2_.refs_0_), channel_id=1, source_target_pairs={{0,4},{4,8},{8,12},{12,14},{14,10},{10,6},{6,2},{2,0},{1,5},{5,9},... | collective-permute-start | bytes 786440 | tf_op jit(solution)/shard_map/ppermute | solution.py:391
  16.2 4.8 %all-to-all-done.notes_ref = s32[8,8,128]{2,1,0:T(8,128)S(1)} async-done(((s32[8,8,128]{2,1,0:T(8,128)}), s32[8,8,128]{2,1,0:T(8,128)S(1)}, u32[]{:S(2)}, u32[]{:S(2)}) %all-to-all-start) | async-done | bytes 32800 | tf_op jit(solution)/shard_map/all_to_all | solution.py:414
  21.1 0.7 collective-permute-start.6
  21.8 1.3 %collective-permute-start.7 = (bf16[256,512]{1,0:T(8,128)(2,1)S(1)}, bf16[256,512]{1,0:T(8,128)(2,1)S(1)}, u32[]{:S(2)}, u32[]{:S(2)}) collective-permute-start(bf16[256,512]{1,0:T(8,128)(2,1)S(1)} %collective-permute-done.1.refs_5_.refs_3_), channel_id=1, source_target_pairs={{4,0},{8,4},{12,8},{14,12},{10,14},{6,10},{2,6},{0,2},{5,1},{9,5},... | collective-permute-start | bytes 786440 | tf_op jit(solution)/shard_map/ppermute | solution.py:394
  23.6 1.1 %pad_maximum_fusion.refs_0_.refs_1_ = bf16[2,256,512]{2,1,0:T(8,128)(2,1)S(1)} fusion(bf16[1,256,512]{2,1,0:T(8,128)(2,1)} %bitcast.7, bf16[1,256,512]{2,1,0:T(8,128)(2,1)} %bitcast.8), kind=kLoop, calls=%fused_computation | loop fusion | flops 262144 | bytes 1048576 | tf_op jit(solution)/shard_map/stack | solution.py:454
  24.7 0.9 collective-permute-done.5.refs_2_
  25.6 1.5 %collective-permute-start.8 = (bf16[256,512]{1,0:T(8,128)(2,1)S(1)}, bf16[256,512]{1,0:T(8,128)(2,1)S(1)}, u32[]{:S(2)}, u32[]{:S(2)}) collective-permute-start(bf16[256,512]{1,0:T(8,128)(2,1)S(1)} %collective-permute-done.4.refs_0_), channel_id=1, source_target_pairs={{0,4},{4,8},{8,12},{12,14},{14,10},{10,6},{6,2},{2,0},{1,5},{5,9},... | collective-permute-start | bytes 786440 | tf_op jit(solution)/shard_map/ppermute | solution.py:391
  27.6 1.2 %copy-done = bf16[256,2048]{1,0:T(8,128)(2,1)S(1)} copy-done((bf16[256,2048]{1,0:T(8,128)(2,1)S(1)}, bf16[256,2048]{1,0:T(8,128)(2,1)}, u32[]{:S(2)}) %copy-start) | copy-done | bytes 1048600
  28.8 2.8 %shard_map.86 = (f32[2,1,1024]{2,1,0:T(1,128)S(1)}, f32[2,1,1024]{2,1,0:T(1,128)S(1)}, f32[2,128,1024]{2,1,0:T(8,128)S(1)}) custom-call(bf16[256,2048]{1,0:T(8,128)(2,1)S(1)} %copy-done, bf16[256,128]{1,0:T(8,128)(2,1)S(1)} %get-tuple-element.120.mask_ref, bf16[8,256,128]{2,1,0:T(8,128)(2,1)S(1)} %get-tuple-element.121.hot_ref, ...), custom_call_target="tpu_custom_call" | custom-call | flops 6 | bytes 256 | tf_op jit(solution)/shard_map/pallas_call | solution.py:397
  31.7 1.5 %collective-permute-start.10 = (bf16[256,512]{1,0:T(8,128)(2,1)S(1)}, bf16[256,512]{1,0:T(8,128)(2,1)S(1)}, u32[]{:S(2)}, u32[]{:S(2)}) collective-permute-start(bf16[256,512]{1,0:T(8,128)(2,1)S(1)} %collective-permute-done.6.refs_1_), channel_id=1, source_target_pairs={{0,4},{4,8},{8,12},{12,14},{14,10},{10,6},{6,2},{2,0},{1,5},{5,9},... | collective-permute-start | bytes 786440 | tf_op jit(solution)/shard_map/ppermute | solution.py:391
  33.7 2.9 %shard_map.87 = (f32[2,1,1024]{2,1,0:T(1,128)S(1)}, f32[2,1,1024]{2,1,0:T(1,128)S(1)}, f32[2,128,1024]{2,1,0:T(8,128)S(1)}) custom-call(bf16[256,2048]{1,0:T(8,128)(2,1)S(1)} %copy-done, bf16[256,128]{1,0:T(8,128)(2,1)S(1)} %get-tuple-element.120.mask_ref, bf16[8,256,128]{2,1,0:T(8,128)(2,1)S(1)} %get-tuple-element.121.hot_ref, ...), custom_call_target="tpu_custom_call" | custom-call | flops 6 | bytes 256 | tf_op jit(solution)/shard_map/pallas_call | solution.py:397
  36.8 1.5 %collective-permute-start.12 = (bf16[256,512]{1,0:T(8,128)(2,1)S(1)}, bf16[256,512]{1,0:T(8,128)(2,1)S(1)}, u32[]{:S(2)}, u32[]{:S(2)}) collective-permute-start(bf16[256,512]{1,0:T(8,128)(2,1)S(1)} %collective-permute-done.8.refs_0_.refs_1_), channel_id=1, source_target_pairs={{0,4},{4,8},{8,12},{12,14},{14,10},{10,6},{6,2},{2,0},{1,5},{5,9},... | collective-permute-start | bytes 786440 | tf_op jit(solution)/shard_map/ppermute | solution.py:391
  38.3 2.1 %shard_map.88 = (f32[2,1,1024]{2,1,0:T(1,128)S(1)}, f32[2,1,1024]{2,1,0:T(1,128)S(1)}, f32[2,128,1024]{2,1,0:T(8,128)S(1)}) custom-call(bf16[256,2048]{1,0:T(8,128)(2,1)S(1)} %copy-done, bf16[256,128]{1,0:T(8,128)(2,1)S(1)} %get-tuple-element.120.mask_ref, ...), custom_call_target="tpu_custom_call", output_to_operand_aliasing={{0}: (7, {}), {1}: (8, {}), {2}: (9, {})} | custom-call | flops 4 | bytes 256 | tf_op jit(solution)/shard_map/pallas_call | solution.py:397
  40.4 1.0 %collective-permute-done.10.refs_1_.refs_2_ = bf16[256,512]{1,0:T(8,128)(2,1)S(1)} collective-permute-done((bf16[256,512]{1,0:T(8,128)(2,1)S(1)}, bf16[256,512]{1,0:T(8,128)(2,1)S(1)}, u32[]{:S(2)}, u32[]{:S(2)}) %collective-permute-start.10) | collective-permute-done | bytes 262176 | tf_op jit(solution)/shard_map/ppermute | solution.py:391
  41.4 1.4 %collective-permute-start.13 = (bf16[256,512]{1,0:T(8,128)(2,1)S(1)}, bf16[256,512]{1,0:T(8,128)(2,1)S(1)}, u32[]{:S(2)}, u32[]{:S(2)}) collective-permute-start(bf16[256,512]{1,0:T(8,128)(2,1)S(1)} %collective-permute-done.11.refs_3_.refs_4_), channel_id=1, source_target_pairs={{4,0},{8,4},{12,8},{14,12},{10,14},{6,10},{2,6},{0,2},{5,1},{9,5},... | collective-permute-start | bytes 786440 | tf_op jit(solution)/shard_map/ppermute | solution.py:394
  42.8 2.1 %shard_map.89 = (f32[2,1,1024]{2,1,0:T(1,128)S(1)}, f32[2,1,1024]{2,1,0:T(1,128)S(1)}, f32[2,128,1024]{2,1,0:T(8,128)S(1)}) custom-call(bf16[256,2048]{1,0:T(8,128)(2,1)S(1)} %copy-done, bf16[256,128]{1,0:T(8,128)(2,1)S(1)} %get-tuple-element.120.mask_ref, ...), custom_call_target="tpu_custom_call", output_to_operand_aliasing={{0}: (7, {}), {1}: (8, {}), {2}: (9, {})} | custom-call | flops 4 | bytes 256 | tf_op jit(solution)/shard_map/pallas_call | solution.py:397
  45.0 2.3 %shard_map.90 = (f32[2,1,1024]{2,1,0:T(1,128)S(1)}, f32[2,1,1024]{2,1,0:T(1,128)S(1)}, f32[2,128,1024]{2,1,0:T(8,128)S(1)}, f32[2,512,1024]{2,1,0:T(8,128)S(1)}) custom-call(bf16[256,2048]{1,0:T(8,128)(2,1)S(1)} %copy-done, bf16[256,128]{1,0:T(8,128)(2,1)S(1)} %get-tuple-element.120.mask_ref, ...), custom_call_target="tpu_custom_call", output_to_operand_aliasing={{0}: (7, {}), {1}: (8, {}), {2}: (9, {})} | custom-call | flops 4 | bytes 256 | tf_op jit(solution)/shard_map/pallas_call | solution.py:397
  47.3 2.2 %shard_map.91 = (f32[2,1,1024]{2,1,0:T(1,128)S(1)}, f32[2,1,1024]{2,1,0:T(1,128)S(1)}, f32[2,128,1024]{2,1,0:T(8,128)S(1)}, f32[2,512,1024]{2,1,0:T(8,128)S(1)}) custom-call(bf16[256,2048]{1,0:T(8,128)(2,1)S(1)} %copy-done, bf16[256,128]{1,0:T(8,128)(2,1)S(1)} %get-tuple-element.120.mask_ref, ...), custom_call_target="tpu_custom_call", output_to_operand_aliasing={{0}: (7, {}), {1}: (8, {}), {2}: (9, {})} | custom-call | flops 4 | bytes 256 | tf_op jit(solution)/shard_map/pallas_call | solution.py:397
  49.5 2.9 %shard_map.92 = (f32[2,1,1024]{2,1,0:T(1,128)S(1)}, f32[2,1,1024]{2,1,0:T(1,128)S(1)}, f32[2,128,1024]{2,1,0:T(8,128)S(1)}, bf16[2,256,256]{2,1,0:T(8,128)(2,1)S(1)}) custom-call(bf16[256,2048]{1,0:T(8,128)(2,1)S(1)} %copy-done, bf16[256,2048]{1,0:T(8,128)(2,1)S(1)} %copy-done.1, ...), custom_call_target="tpu_custom_call", output_to_operand_aliasing={{0}: (6, {}), {1}: (7, {}), {2}: (8, {})} | custom-call | flops 7 | bytes 256 | tf_op jit(solution)/shard_map/pallas_call | solution.py:397
  52.4 1.1 %collective-permute-start.14 = (bf16[2,256,256]{2,1,0:T(8,128)(2,1)S(1)}, bf16[2,256,256]{2,1,0:T(8,128)(2,1)S(1)}, u32[]{:S(2)}, u32[]{:S(2)}) collective-permute-start(bf16[2,256,256]{2,1,0:T(8,128)(2,1)S(1)} %get-tuple-element.188), channel_id=1, source_target_pairs={{4,0},{8,4},{12,8},{14,12},{10,14},{6,10},{2,6},{0,2},{5,1},{9,5},... | collective-permute-start | bytes 786440 | tf_op jit(solution)/shard_map/ppermute | solution.py:394
  53.5 2.9 %shard_map.93 = (f32[2,1,1024]{2,1,0:T(1,128)S(1)}, f32[2,1,1024]{2,1,0:T(1,128)S(1)}, f32[2,128,1024]{2,1,0:T(8,128)S(1)}, bf16[2,256,256]{2,1,0:T(8,128)(2,1)S(1)}) custom-call(bf16[256,2048]{1,0:T(8,128)(2,1)S(1)} %copy-done, bf16[256,2048]{1,0:T(8,128)(2,1)S(1)} %copy-done.1, ...), custom_call_target="tpu_custom_call", output_to_operand_aliasing={{0}: (6, {}), {1}: (7, {}), {2}: (8, {})} | custom-call | flops 7 | bytes 256 | tf_op jit(solution)/shard_map/pallas_call | solution.py:397
  56.5 1.2 %collective-permute-start.15 = (bf16[2,256,256]{2,1,0:T(8,128)(2,1)S(1)}, bf16[2,256,256]{2,1,0:T(8,128)(2,1)S(1)}, u32[]{:S(2)}, u32[]{:S(2)}) collective-permute-start(bf16[2,256,256]{2,1,0:T(8,128)(2,1)S(1)} %get-tuple-element.196), channel_id=1, source_target_pairs={{0,4},{4,8},{8,12},{12,14},{14,10},{10,6},{6,2},{2,0},{1,5},{5,9},... | collective-permute-start | bytes 786440 | tf_op jit(solution)/shard_map/ppermute | solution.py:391
  57.7 2.3 %shard_map.94 = (f32[2,128,1024]{2,1,0:T(8,128)S(1)}, f32[2,256,256]{2,1,0:T(8,128)S(1)}, f32[2,256,256]{2,1,0:T(8,128)S(1)}) custom-call(bf16[256,2048]{1,0:T(8,128)(2,1)S(1)} %copy-done, bf16[256,2048]{1,0:T(8,128)(2,1)S(1)} %copy-done.1, bf16[256,128]{1,0:T(8,128)(2,1)S(1)} %get-tuple-element.120.mask_ref, ...), custom_call_target="tpu_custom_call", output_to_operand_aliasing={{0}: (11, {})} | custom-call | flops 10 | bytes 256 | tf_op jit(solution)/shard_map/pallas_call | solution.py:397
  60.1 1.1 %collective-permute-start.16 = (bf16[2,256,256]{2,1,0:T(8,128)(2,1)S(1)}, bf16[2,256,256]{2,1,0:T(8,128)(2,1)S(1)}, u32[]{:S(2)}, u32[]{:S(2)}) collective-permute-start(bf16[2,256,256]{2,1,0:T(8,128)(2,1)S(1)} %add_convert_fusion.11), channel_id=1, source_target_pairs={{4,0},{8,4},{12,8},{14,12},{10,14},{6,10},{2,6},{0,2},{5,1},{9,5},... | collective-permute-start | bytes 786440 | tf_op jit(solution)/shard_map/ppermute | solution.py:394
  61.2 1.0 %collective-permute-start.17 = (bf16[2,256,256]{2,1,0:T(8,128)(2,1)S(1)}, bf16[2,256,256]{2,1,0:T(8,128)(2,1)S(1)}, u32[]{:S(2)}, u32[]{:S(2)}) collective-permute-start(bf16[2,256,256]{2,1,0:T(8,128)(2,1)S(1)} %convert_element_type.86), channel_id=1, source_target_pairs={{0,4},{4,8},{8,12},{12,14},{14,10},{10,6},{6,2},{2,0},{1,5},{5,9},... | collective-permute-start | bytes 786440 | tf_op jit(solution)/shard_map/ppermute | solution.py:391
  62.2 2.3 %shard_map.95 = (f32[2,128,1024]{2,1,0:T(8,128)S(1)}, f32[2,256,256]{2,1,0:T(8,128)S(1)}, f32[2,256,256]{2,1,0:T(8,128)S(1)}) custom-call(bf16[256,2048]{1,0:T(8,128)(2,1)S(1)} %copy-done, bf16[256,2048]{1,0:T(8,128)(2,1)S(1)} %copy-done.1, bf16[256,128]{1,0:T(8,128)(2,1)S(1)} %get-tuple-element.120.mask_ref, ...), custom_call_target="tpu_custom_call", output_to_operand_aliasing={{0}: (11, {})} | custom-call | flops 10 | bytes 256 | tf_op jit(solution)/shard_map/pallas_call | solution.py:397
  64.5 1.3 %collective-permute-done.15 = bf16[2,256,256]{2,1,0:T(8,128)(2,1)S(1)} collective-permute-done((bf16[2,256,256]{2,1,0:T(8,128)(2,1)S(1)}, bf16[2,256,256]{2,1,0:T(8,128)(2,1)S(1)}, u32[]{:S(2)}, u32[]{:S(2)}) %collective-permute-start.15) | collective-permute-done | bytes 262176 | tf_op jit(solution)/shard_map/ppermute | solution.py:391
  66.0 1.4 %collective-permute-start.18 = (bf16[2,256,256]{2,1,0:T(8,128)(2,1)S(1)}, bf16[2,256,256]{2,1,0:T(8,128)(2,1)S(1)}, u32[]{:S(2)}, u32[]{:S(2)}) collective-permute-start(bf16[2,256,256]{2,1,0:T(8,128)(2,1)S(1)} %convert_element_type.87), channel_id=1, source_target_pairs={{4,0},{8,4},{12,8},{14,12},{10,14},{6,10},{2,6},{0,2},{5,1},{9,5},... | collective-permute-start | bytes 786440 | tf_op jit(solution)/shard_map/ppermute | solution.py:394
  67.4 0.6 collective-permute-start.19
  68.0 2.9 %shard_map.96 = (f32[2,128,1024]{2,1,0:T(8,128)S(1)}, f32[2,256,256]{2,1,0:T(8,128)S(1)}, f32[2,256,256]{2,1,0:T(8,128)S(1)}) custom-call(bf16[256,2048]{1,0:T(8,128)(2,1)S(1)} %copy-done, bf16[256,2048]{1,0:T(8,128)(2,1)S(1)} %copy-done.1, bf16[256,128]{1,0:T(8,128)(2,1)S(1)} %get-tuple-element.120.mask_ref, ...), custom_call_target="tpu_custom_call", output_to_operand_aliasing={{0}: (10, {})} | custom-call | flops 10 | bytes 256 | tf_op jit(solution)/shard_map/pallas_call | solution.py:397
  71.5 1.4 %collective-permute-start.20 = (bf16[2,256,256]{2,1,0:T(8,128)(2,1)S(1)}, bf16[2,256,256]{2,1,0:T(8,128)(2,1)S(1)}, u32[]{:S(2)}, u32[]{:S(2)}) collective-permute-start(bf16[2,256,256]{2,1,0:T(8,128)(2,1)S(1)} %add_convert_fusion.9), channel_id=1, source_target_pairs={{4,0},{8,4},{12,8},{14,12},{10,14},{6,10},{2,6},{0,2},{5,1},{9,5},... | collective-permute-start | bytes 786440 | tf_op jit(solution)/shard_map/ppermute | solution.py:394
  73.6 2.9 %shard_map.97 = (f32[2,128,1024]{2,1,0:T(8,128)S(1)}, f32[2,256,256]{2,1,0:T(8,128)S(1)}, f32[2,256,256]{2,1,0:T(8,128)S(1)}) custom-call(bf16[256,2048]{1,0:T(8,128)(2,1)S(1)} %copy-done, bf16[256,2048]{1,0:T(8,128)(2,1)S(1)} %copy-done.1, bf16[256,128]{1,0:T(8,128)(2,1)S(1)} %get-tuple-element.120.mask_ref, ...), custom_call_target="tpu_custom_call", output_to_operand_aliasing={{0}: (10, {})} | custom-call | flops 10 | bytes 256 | tf_op jit(solution)/shard_map/pallas_call | solution.py:397
  77.2 1.4 %collective-permute-start.22 = (bf16[2,256,256]{2,1,0:T(8,128)(2,1)S(1)}, bf16[2,256,256]{2,1,0:T(8,128)(2,1)S(1)}, u32[]{:S(2)}, u32[]{:S(2)}) collective-permute-start(bf16[2,256,256]{2,1,0:T(8,128)(2,1)S(1)} %add_convert_fusion.7), channel_id=1, source_target_pairs={{4,0},{8,4},{12,8},{14,12},{10,14},{6,10},{2,6},{0,2},{5,1},{9,5},... | collective-permute-start | bytes 786440 | tf_op jit(solution)/shard_map/ppermute | solution.py:394
  78.6 0.7 collective-permute-start.23
  79.2 2.9 %shard_map.98 = (f32[2,128,1024]{2,1,0:T(8,128)S(1)}, f32[2,256,256]{2,1,0:T(8,128)S(1)}, f32[2,256,256]{2,1,0:T(8,128)S(1)}) custom-call(bf16[256,2048]{1,0:T(8,128)(2,1)S(1)} %copy-done, bf16[256,2048]{1,0:T(8,128)(2,1)S(1)} %copy-done.1, bf16[256,128]{1,0:T(8,128)(2,1)S(1)} %get-tuple-element.120.mask_ref, ...), custom_call_target="tpu_custom_call", output_to_operand_aliasing={{0}: (10, {})} | custom-call | flops 10 | bytes 256 | tf_op jit(solution)/shard_map/pallas_call | solution.py:397
  82.8 1.4 %collective-permute-start.24 = (bf16[2,256,256]{2,1,0:T(8,128)(2,1)S(1)}, bf16[2,256,256]{2,1,0:T(8,128)(2,1)S(1)}, u32[]{:S(2)}, u32[]{:S(2)}) collective-permute-start(bf16[2,256,256]{2,1,0:T(8,128)(2,1)S(1)} %add_convert_fusion.5), channel_id=1, source_target_pairs={{4,0},{8,4},{12,8},{14,12},{10,14},{6,10},{2,6},{0,2},{5,1},{9,5},... | collective-permute-start | bytes 786440 | tf_op jit(solution)/shard_map/ppermute | solution.py:394
  84.9 2.9 %shard_map.99 = (f32[2,128,1024]{2,1,0:T(8,128)S(1)}, f32[2,256,256]{2,1,0:T(8,128)S(1)}, f32[2,256,256]{2,1,0:T(8,128)S(1)}) custom-call(bf16[256,2048]{1,0:T(8,128)(2,1)S(1)} %copy-done, bf16[256,2048]{1,0:T(8,128)(2,1)S(1)} %copy-done.1, bf16[256,128]{1,0:T(8,128)(2,1)S(1)} %get-tuple-element.120.mask_ref, ...), custom_call_target="tpu_custom_call", output_to_operand_aliasing={{0}: (10, {})} | custom-call | flops 10 | bytes 256 | tf_op jit(solution)/shard_map/pallas_call | solution.py:397
  88.4 1.4 %collective-permute-start.26 = (bf16[2,256,256]{2,1,0:T(8,128)(2,1)S(1)}, bf16[2,256,256]{2,1,0:T(8,128)(2,1)S(1)}, u32[]{:S(2)}, u32[]{:S(2)}) collective-permute-start(bf16[2,256,256]{2,1,0:T(8,128)(2,1)S(1)} %add_convert_fusion.3), channel_id=1, source_target_pairs={{4,0},{8,4},{12,8},{14,12},{10,14},{6,10},{2,6},{0,2},{5,1},{9,5},... | collective-permute-start | bytes 786440 | tf_op jit(solution)/shard_map/ppermute | solution.py:394
  90.5 1.7 %shard_map.101 = (f32[2,128,1024]{2,1,0:T(8,128)S(1)}, f32[2,256,256]{2,1,0:T(8,128)S(1)}) custom-call(bf16[256,2048]{1,0:T(8,128)(2,1)S(1)} %copy-done, bf16[256,2048]{1,0:T(8,128)(2,1)S(1)} %copy-done.1, bf16[256,128]{1,0:T(8,128)(2,1)S(1)} %get-tuple-element.120.mask_ref, ...), custom_call_target="tpu_custom_call", output_to_operand_aliasing={{0}: (8, {})} | custom-call | flops 5 | bytes 256 | tf_op jit(solution)/shard_map/pallas_call | solution.py:397
  92.2 1.7 %shard_map.100 = (f32[2,128,1024]{2,1,0:T(8,128)S(1)}, f32[2,256,256]{2,1,0:T(8,128)S(1)}) custom-call(bf16[256,2048]{1,0:T(8,128)(2,1)S(1)} %copy-done, bf16[256,2048]{1,0:T(8,128)(2,1)S(1)} %copy-done.1, bf16[256,128]{1,0:T(8,128)(2,1)S(1)} %get-tuple-element.120.mask_ref, ...), custom_call_target="tpu_custom_call", output_to_operand_aliasing={{0}: (8, {})} | custom-call | flops 5 | bytes 256 | tf_op jit(solution)/shard_map/pallas_call | solution.py:397
  94.0 1.5 %shard_map.102 = bf16[256,2048]{1,0:T(8,128)(2,1)} custom-call(f32[2,128,1024]{2,1,0:T(8,128)S(1)} %get-tuple-element.229.refs_0_, f32[2,128,1024]{2,1,0:T(8,128)S(1)} %get-tuple-element.230.refs_1_), custom_call_target="tpu_custom_call" | custom-call | bytes 256 | tf_op jit(solution)/shard_map/pallas_call | solution.py:397
  95.5 0.7 collective-permute-done.27
  96.3 0.8 fusion.2
  (52 shorter events, 7.1 us)
Async XLA Ops:
  0.6 13.4 %collective-permute-start.2 = (bf16[256,512]{1,0:T(8,128)(2,1)}, bf16[256,512]{1,0:T(8,128)(2,1)S(1)}, u32[]{:S(2)}, u32[]{:S(2)}) collective-permute-start(bf16[256,512]{1,0:T(8,128)(2,1)} %param.7), channel_id=1, source_target_pairs={{0,4},{4,8},{8,12},{12,14},{14,10},{10,6},{6,2},{2,0},{1,5},{5,9},... | collective-permute-start | bytes 786440 | tf_op jit(solution)/shard_map/ppermute | solution.py:391
  3.7 10.4 %collective-permute-start.3 = (bf16[256,512]{1,0:T(8,128)(2,1)}, bf16[256,512]{1,0:T(8,128)(2,1)S(1)}, u32[]{:S(2)}, u32[]{:S(2)}) collective-permute-start(bf16[256,512]{1,0:T(8,128)(2,1)} %param.7), channel_id=1, source_target_pairs={{4,0},{8,4},{12,8},{14,12},{10,14},{6,10},{2,6},{0,2},{5,1},{9,5},... | collective-permute-start | bytes 786440 | tf_op jit(solution)/shard_map/ppermute | solution.py:394
  3.7 17.3 %collective-permute-start = (bf16[256,512]{1,0:T(8,128)(2,1)}, bf16[256,512]{1,0:T(8,128)(2,1)S(1)}, u32[]{:S(2)}, u32[]{:S(2)}) collective-permute-start(bf16[256,512]{1,0:T(8,128)(2,1)} %param.8), channel_id=1, source_target_pairs={{0,4},{4,8},{8,12},{12,14},{14,10},{10,6},{6,2},{2,0},{1,5},{5,9},... | collective-permute-start | bytes 786440 | tf_op jit(solution)/shard_map/ppermute | solution.py:391
  5.7 15.3 %collective-permute-start.1 = (bf16[256,512]{1,0:T(8,128)(2,1)}, bf16[256,512]{1,0:T(8,128)(2,1)S(1)}, u32[]{:S(2)}, u32[]{:S(2)}) collective-permute-start(bf16[256,512]{1,0:T(8,128)(2,1)} %param.8), channel_id=1, source_target_pairs={{4,0},{8,4},{12,8},{14,12},{10,14},{6,10},{2,6},{0,2},{5,1},{9,5},... | collective-permute-start | bytes 786440 | tf_op jit(solution)/shard_map/ppermute | solution.py:394
  7.8 13.2 %all-to-all-start = ((s32[8,8,128]{2,1,0:T(8,128)}), s32[8,8,128]{2,1,0:T(8,128)S(1)}, u32[]{:S(2)}, u32[]{:S(2)}) async-start(s32[8,8,128]{2,1,0:T(8,128)} %broadcast_in_dim.2), calls=%async_computation | async-start | bytes 65536 | tf_op jit(solution)/shard_map/all_to_all | solution.py:414
  14.1 10.6 %collective-permute-start.4 = (bf16[256,512]{1,0:T(8,128)(2,1)S(1)}, bf16[256,512]{1,0:T(8,128)(2,1)S(1)}, u32[]{:S(2)}, u32[]{:S(2)}) collective-permute-start(bf16[256,512]{1,0:T(8,128)(2,1)S(1)} %collective-permute-done.2.refs_2_.refs_0_), channel_id=1, source_target_pairs={{0,4},{4,8},{8,12},{12,14},{14,10},{10,6},{6,2},{2,0},{1,5},{5,9},... | collective-permute-start | bytes 786440 | tf_op jit(solution)/shard_map/ppermute | solution.py:391
  16.1 9.4 %collective-permute-start.5 = (bf16[256,512]{1,0:T(8,128)(2,1)S(1)}, bf16[256,512]{1,0:T(8,128)(2,1)S(1)}, u32[]{:S(2)}, u32[]{:S(2)}) collective-permute-start(bf16[256,512]{1,0:T(8,128)(2,1)S(1)} %collective-permute-done.3.refs_4_.refs_2_), channel_id=1, source_target_pairs={{4,0},{8,4},{12,8},{14,12},{10,14},{6,10},{2,6},{0,2},{5,1},{9,5},... | collective-permute-start | bytes 786440 | tf_op jit(solution)/shard_map/ppermute | solution.py:394
  21.1 10.6 %collective-permute-start.6 = (bf16[256,512]{1,0:T(8,128)(2,1)S(1)}, bf16[256,512]{1,0:T(8,128)(2,1)S(1)}, u32[]{:S(2)}, u32[]{:S(2)}) collective-permute-start(bf16[256,512]{1,0:T(8,128)(2,1)S(1)} %collective-permute-done.refs_3_.refs_1_), channel_id=1, source_target_pairs={{0,4},{4,8},{8,12},{12,14},{14,10},{10,6},{6,2},{2,0},{1,5},{5,9},... | collective-permute-start | bytes 786440 | tf_op jit(solution)/shard_map/ppermute | solution.py:391
  21.8 9.9 %collective-permute-start.7 = (bf16[256,512]{1,0:T(8,128)(2,1)S(1)}, bf16[256,512]{1,0:T(8,128)(2,1)S(1)}, u32[]{:S(2)}, u32[]{:S(2)}) collective-permute-start(bf16[256,512]{1,0:T(8,128)(2,1)S(1)} %collective-permute-done.1.refs_5_.refs_3_), channel_id=1, source_target_pairs={{4,0},{8,4},{12,8},{14,12},{10,14},{6,10},{2,6},{0,2},{5,1},{9,5},... | collective-permute-start | bytes 786440 | tf_op jit(solution)/shard_map/ppermute | solution.py:394
  25.6 11.1 %collective-permute-start.8 = (bf16[256,512]{1,0:T(8,128)(2,1)S(1)}, bf16[256,512]{1,0:T(8,128)(2,1)S(1)}, u32[]{:S(2)}, u32[]{:S(2)}) collective-permute-start(bf16[256,512]{1,0:T(8,128)(2,1)S(1)} %collective-permute-done.4.refs_0_), channel_id=1, source_target_pairs={{0,4},{4,8},{8,12},{12,14},{14,10},{10,6},{6,2},{2,0},{1,5},{5,9},... | collective-permute-start | bytes 786440 | tf_op jit(solution)/shard_map/ppermute | solution.py:391
  27.0 9.8 %collective-permute-start.9 = (bf16[256,512]{1,0:T(8,128)(2,1)S(1)}, bf16[256,512]{1,0:T(8,128)(2,1)S(1)}, u32[]{:S(2)}, u32[]{:S(2)}) collective-permute-start(bf16[256,512]{1,0:T(8,128)(2,1)S(1)} %collective-permute-done.5.refs_2_), channel_id=1, source_target_pairs={{4,0},{8,4},{12,8},{14,12},{10,14},{6,10},{2,6},{0,2},{5,1},{9,5},... | collective-permute-start | bytes 786440 | tf_op jit(solution)/shard_map/ppermute | solution.py:394
  27.6 1.2 %copy-start = (bf16[256,2048]{1,0:T(8,128)(2,1)S(1)}, bf16[256,2048]{1,0:T(8,128)(2,1)}, u32[]{:S(2)}) copy-start(bf16[256,2048]{1,0:T(8,128)(2,1)} %q_ref.31) | copy-start | bytes 3145732
  31.7 9.7 %collective-permute-start.10 = (bf16[256,512]{1,0:T(8,128)(2,1)S(1)}, bf16[256,512]{1,0:T(8,128)(2,1)S(1)}, u32[]{:S(2)}, u32[]{:S(2)}) collective-permute-start(bf16[256,512]{1,0:T(8,128)(2,1)S(1)} %collective-permute-done.6.refs_1_), channel_id=1, source_target_pairs={{0,4},{4,8},{8,12},{12,14},{14,10},{10,6},{6,2},{2,0},{1,5},{5,9},... | collective-permute-start | bytes 786440 | tf_op jit(solution)/shard_map/ppermute | solution.py:391
  33.2 8.2 %collective-permute-start.11 = (bf16[256,512]{1,0:T(8,128)(2,1)S(1)}, bf16[256,512]{1,0:T(8,128)(2,1)S(1)}, u32[]{:S(2)}, u32[]{:S(2)}) collective-permute-start(bf16[256,512]{1,0:T(8,128)(2,1)S(1)} %collective-permute-done.7.refs_3_), channel_id=1, source_target_pairs={{4,0},{8,4},{12,8},{14,12},{10,14},{6,10},{2,6},{0,2},{5,1},{9,5},... | collective-permute-start | bytes 786440 | tf_op jit(solution)/shard_map/ppermute | solution.py:394
  36.8 12.7 %collective-permute-start.12 = (bf16[256,512]{1,0:T(8,128)(2,1)S(1)}, bf16[256,512]{1,0:T(8,128)(2,1)S(1)}, u32[]{:S(2)}, u32[]{:S(2)}) collective-permute-start(bf16[256,512]{1,0:T(8,128)(2,1)S(1)} %collective-permute-done.8.refs_0_.refs_1_), channel_id=1, source_target_pairs={{0,4},{4,8},{8,12},{12,14},{14,10},{10,6},{6,2},{2,0},{1,5},{5,9},... | collective-permute-start | bytes 786440 | tf_op jit(solution)/shard_map/ppermute | solution.py:391
  41.4 8.1 %collective-permute-start.13 = (bf16[256,512]{1,0:T(8,128)(2,1)S(1)}, bf16[256,512]{1,0:T(8,128)(2,1)S(1)}, u32[]{:S(2)}, u32[]{:S(2)}) collective-permute-start(bf16[256,512]{1,0:T(8,128)(2,1)S(1)} %collective-permute-done.11.refs_3_.refs_4_), channel_id=1, source_target_pairs={{4,0},{8,4},{12,8},{14,12},{10,14},{6,10},{2,6},{0,2},{5,1},{9,5},... | collective-permute-start | bytes 786440 | tf_op jit(solution)/shard_map/ppermute | solution.py:394
  45.0 4.5 %copy-start.1 = (bf16[256,2048]{1,0:T(8,128)(2,1)S(1)}, bf16[256,2048]{1,0:T(8,128)(2,1)}, u32[]{:S(2)}) copy-start(bf16[256,2048]{1,0:T(8,128)(2,1)} %g_ref.19) | copy-start | bytes 3145732
  52.4 7.6 %collective-permute-start.14 = (bf16[2,256,256]{2,1,0:T(8,128)(2,1)S(1)}, bf16[2,256,256]{2,1,0:T(8,128)(2,1)S(1)}, u32[]{:S(2)}, u32[]{:S(2)}) collective-permute-start(bf16[2,256,256]{2,1,0:T(8,128)(2,1)S(1)} %get-tuple-element.188), channel_id=1, source_target_pairs={{4,0},{8,4},{12,8},{14,12},{10,14},{6,10},{2,6},{0,2},{5,1},{9,5},... | collective-permute-start | bytes 786440 | tf_op jit(solution)/shard_map/ppermute | solution.py:394
  56.5 9.4 %collective-permute-start.15 = (bf16[2,256,256]{2,1,0:T(8,128)(2,1)S(1)}, bf16[2,256,256]{2,1,0:T(8,128)(2,1)S(1)}, u32[]{:S(2)}, u32[]{:S(2)}) collective-permute-start(bf16[2,256,256]{2,1,0:T(8,128)(2,1)S(1)} %get-tuple-element.196), channel_id=1, source_target_pairs={{0,4},{4,8},{8,12},{12,14},{14,10},{10,6},{6,2},{2,0},{1,5},{5,9},... | collective-permute-start | bytes 786440 | tf_op jit(solution)/shard_map/ppermute | solution.py:391
  60.1 10.9 %collective-permute-start.16 = (bf16[2,256,256]{2,1,0:T(8,128)(2,1)S(1)}, bf16[2,256,256]{2,1,0:T(8,128)(2,1)S(1)}, u32[]{:S(2)}, u32[]{:S(2)}) collective-permute-start(bf16[2,256,256]{2,1,0:T(8,128)(2,1)S(1)} %add_convert_fusion.11), channel_id=1, source_target_pairs={{4,0},{8,4},{12,8},{14,12},{10,14},{6,10},{2,6},{0,2},{5,1},{9,5},... | collective-permute-start | bytes 786440 | tf_op jit(solution)/shard_map/ppermute | solution.py:394
  61.2 10.3 %collective-permute-start.17 = (bf16[2,256,256]{2,1,0:T(8,128)(2,1)S(1)}, bf16[2,256,256]{2,1,0:T(8,128)(2,1)S(1)}, u32[]{:S(2)}, u32[]{:S(2)}) collective-permute-start(bf16[2,256,256]{2,1,0:T(8,128)(2,1)S(1)} %convert_element_type.86), channel_id=1, source_target_pairs={{0,4},{4,8},{8,12},{12,14},{14,10},{10,6},{6,2},{2,0},{1,5},{5,9},... | collective-permute-start | bytes 786440 | tf_op jit(solution)/shard_map/ppermute | solution.py:391
  66.0 10.6 %collective-permute-start.18 = (bf16[2,256,256]{2,1,0:T(8,128)(2,1)S(1)}, bf16[2,256,256]{2,1,0:T(8,128)(2,1)S(1)}, u32[]{:S(2)}, u32[]{:S(2)}) collective-permute-start(bf16[2,256,256]{2,1,0:T(8,128)(2,1)S(1)} %convert_element_type.87), channel_id=1, source_target_pairs={{4,0},{8,4},{12,8},{14,12},{10,14},{6,10},{2,6},{0,2},{5,1},{9,5},... | collective-permute-start | bytes 786440 | tf_op jit(solution)/shard_map/ppermute | solution.py:394
  67.4 9.7 %collective-permute-start.19 = (bf16[2,256,256]{2,1,0:T(8,128)(2,1)S(1)}, bf16[2,256,256]{2,1,0:T(8,128)(2,1)S(1)}, u32[]{:S(2)}, u32[]{:S(2)}) collective-permute-start(bf16[2,256,256]{2,1,0:T(8,128)(2,1)S(1)} %add_convert_fusion.10), channel_id=1, source_target_pairs={{0,4},{4,8},{8,12},{12,14},{14,10},{10,6},{6,2},{2,0},{1,5},{5,9},... | collective-permute-start | bytes 786440 | tf_op jit(solution)/shard_map/ppermute | solution.py:391
  71.5 10.6 %collective-permute-start.20 = (bf16[2,256,256]{2,1,0:T(8,128)(2,1)S(1)}, bf16[2,256,256]{2,1,0:T(8,128)(2,1)S(1)}, u32[]{:S(2)}, u32[]{:S(2)}) collective-permute-start(bf16[2,256,256]{2,1,0:T(8,128)(2,1)S(1)} %add_convert_fusion.9), channel_id=1, source_target_pairs={{4,0},{8,4},{12,8},{14,12},{10,14},{6,10},{2,6},{0,2},{5,1},{9,5},... | collective-permute-start | bytes 786440 | tf_op jit(solution)/shard_map/ppermute | solution.py:394
  73.0 9.7 %collective-permute-start.21 = (bf16[2,256,256]{2,1,0:T(8,128)(2,1)S(1)}, bf16[2,256,256]{2,1,0:T(8,128)(2,1)S(1)}, u32[]{:S(2)}, u32[]{:S(2)}) collective-permute-start(bf16[2,256,256]{2,1,0:T(8,128)(2,1)S(1)} %add_convert_fusion.8), channel_id=1, source_target_pairs={{0,4},{4,8},{8,12},{12,14},{14,10},{10,6},{6,2},{2,0},{1,5},{5,9},... | collective-permute-start | bytes 786440 | tf_op jit(solution)/shard_map/ppermute | solution.py:391
  77.2 10.6 %collective-permute-start.22 = (bf16[2,256,256]{2,1,0:T(8,128)(2,1)S(1)}, bf16[2,256,256]{2,1,0:T(8,128)(2,1)S(1)}, u32[]{:S(2)}, u32[]{:S(2)}) collective-permute-start(bf16[2,256,256]{2,1,0:T(8,128)(2,1)S(1)} %add_convert_fusion.7), channel_id=1, source_target_pairs={{4,0},{8,4},{12,8},{14,12},{10,14},{6,10},{2,6},{0,2},{5,1},{9,5},... | collective-permute-start | bytes 786440 | tf_op jit(solution)/shard_map/ppermute | solution.py:394
  78.6 9.7 %collective-permute-start.23 = (bf16[2,256,256]{2,1,0:T(8,128)(2,1)S(1)}, bf16[2,256,256]{2,1,0:T(8,128)(2,1)S(1)}, u32[]{:S(2)}, u32[]{:S(2)}) collective-permute-start(bf16[2,256,256]{2,1,0:T(8,128)(2,1)S(1)} %add_convert_fusion.6), channel_id=1, source_target_pairs={{0,4},{4,8},{8,12},{12,14},{14,10},{10,6},{6,2},{2,0},{1,5},{5,9},... | collective-permute-start | bytes 786440 | tf_op jit(solution)/shard_map/ppermute | solution.py:391
  82.8 11.1 %collective-permute-start.24 = (bf16[2,256,256]{2,1,0:T(8,128)(2,1)S(1)}, bf16[2,256,256]{2,1,0:T(8,128)(2,1)S(1)}, u32[]{:S(2)}, u32[]{:S(2)}) collective-permute-start(bf16[2,256,256]{2,1,0:T(8,128)(2,1)S(1)} %add_convert_fusion.5), channel_id=1, source_target_pairs={{4,0},{8,4},{12,8},{14,12},{10,14},{6,10},{2,6},{0,2},{5,1},{9,5},... | collective-permute-start | bytes 786440 | tf_op jit(solution)/shard_map/ppermute | solution.py:394
  84.2 9.7 %collective-permute-start.25 = (bf16[2,256,256]{2,1,0:T(8,128)(2,1)S(1)}, bf16[2,256,256]{2,1,0:T(8,128)(2,1)S(1)}, u32[]{:S(2)}, u32[]{:S(2)}) collective-permute-start(bf16[2,256,256]{2,1,0:T(8,128)(2,1)S(1)} %add_convert_fusion.4), channel_id=1, source_target_pairs={{0,4},{4,8},{8,12},{12,14},{14,10},{10,6},{6,2},{2,0},{1,5},{5,9},... | collective-permute-start | bytes 786440 | tf_op jit(solution)/shard_map/ppermute | solution.py:391
  88.4 7.1 %collective-permute-start.26 = (bf16[2,256,256]{2,1,0:T(8,128)(2,1)S(1)}, bf16[2,256,256]{2,1,0:T(8,128)(2,1)S(1)}, u32[]{:S(2)}, u32[]{:S(2)}) collective-permute-start(bf16[2,256,256]{2,1,0:T(8,128)(2,1)S(1)} %add_convert_fusion.3), channel_id=1, source_target_pairs={{4,0},{8,4},{12,8},{14,12},{10,14},{6,10},{2,6},{0,2},{5,1},{9,5},... | collective-permute-start | bytes 786440 | tf_op jit(solution)/shard_map/ppermute | solution.py:394
  89.8 6.4 %collective-permute-start.27 = (bf16[2,256,256]{2,1,0:T(8,128)(2,1)S(1)}, bf16[2,256,256]{2,1,0:T(8,128)(2,1)S(1)}, u32[]{:S(2)}, u32[]{:S(2)}) collective-permute-start(bf16[2,256,256]{2,1,0:T(8,128)(2,1)S(1)} %add_convert_fusion.2), channel_id=1, source_target_pairs={{0,4},{4,8},{8,12},{12,14},{14,10},{10,6},{6,2},{2,0},{1,5},{5,9},... | collective-permute-start | bytes 786440 | tf_op jit(solution)/shard_map/ppermute | solution.py:391

commit v3 on v2

--- a/solution.py
+++ b/solution.py
@@ -463,9 +463,8 @@
             else:
                 if c:
                     catch_up(0, r - 1)
+                    catch_up(1, r - 1)
                 low, high, state[:] = lax.optimization_barrier((low, high, state))
-                if c:
-                    catch_up(1, r - 1)
             behind[c].append(low)
             ahead[c].append(high)
         if r == 1:

time: 97.4 us -> 95.7 us (0.983)
    ppermute x14, starting transfers between devices: 13.3 us -> 9.15 us  [send_back(): return lax.ppermute(value, 'seq', back)]
    ppermute x14, starting transfers between devices: 17.8 us -> 21.1 us  [send_on(): return lax.ppermute(value, 'seq', onward)]
    ppermute x14, waiting for transfers between devices: 4.97 us -> 1.89 us  [send_on(): return lax.ppermute(value, 'seq', onward)]
    ppermute x14, waiting for transfers between devices: 1.07 us -> 3.27 us  [send_back(): return lax.ppermute(value, 'seq', back)]
  transfers between devices with their start and end apart: 29 -> 29, of which waited for: 10 -> 9; matrix products, arithmetic and copies ran while one was open for 4% -> 4% of each run, Pallas kernels for 40% -> 41%
where the time goes in v3:
time: 95.7 us; the launch traced here: 95.5 us
  Pallas kernels  41.9 us (44%)
  starting transfers between devices  36.5 us (38%)
  waiting for transfers between devices  9.99 us (10%)
  other arithmetic  3.39 us (4%)
  local copies, waits for them, and re-layouts  2.61 us (3%)
  between operations  1.01 us (1%)
    pallas_call x17, Pallas kernels, call(): pl.pallas_call(kernel, in_specs=[IN_VMEM] * len(args), out_specs=[IN_VMEM...  41.4 us
    ppermute x14, starting transfers between devices, send_on(): return lax.ppermute(value, 'seq', onward)  21.1 us
    ppermute x14, starting transfers between devices, send_back(): return lax.ppermute(value, 'seq', back)  9.15 us
    all_to_all x1, starting transfers between devices, gather_plan(): lax.all_to_all(jnp.broadcast_to(notes, (peers,) + notes.shape[1:]), 'seq'...  6.25 us
    all_to_all x1, waiting for transfers between devices, gather_plan(): lax.all_to_all(jnp.broadcast_to(notes, (peers,) + notes.shape[1:]), 'seq'...  4.84 us
    ppermute x14, waiting for transfers between devices, send_back(): return lax.ppermute(value, 'seq', back)  3.27 us
  transfers between devices with their start and end apart: 29, of which 9 were waited for; matrix products, arithmetic and copies ran while one was open for 4% of the time, Pallas kernels for 41%

profile of v3, /device:TPU:0, one launch (start us, length us, event | category | flops | bytes accessed | tf_op | source)
XLA Modules:
  0.0 95.5 jit_solution(4108322065507700725)
XLA Ops:
  0.6 3.1 %collective-permute-start.2 = (bf16[256,512]{1,0:T(8,128)(2,1)}, bf16[256,512]{1,0:T(8,128)(2,1)S(1)}, u32[]{:S(2)}, u32[]{:S(2)}) collective-permute-start(bf16[256,512]{1,0:T(8,128)(2,1)} %param.7), channel_id=1, source_target_pairs={{0,4},{4,8},{8,12},{12,14},{14,10},{10,6},{6,2},{2,0},{1,5},{5,9},... | collective-permute-start | bytes 786440 | tf_op jit(solution)/shard_map/ppermute | solution.py:391
  3.7 2.0 %collective-permute-start = (bf16[256,512]{1,0:T(8,128)(2,1)}, bf16[256,512]{1,0:T(8,128)(2,1)S(1)}, u32[]{:S(2)}, u32[]{:S(2)}) collective-permute-start(bf16[256,512]{1,0:T(8,128)(2,1)} %param.8), channel_id=1, source_target_pairs={{0,4},{4,8},{8,12},{12,14},{14,10},{10,6},{6,2},{2,0},{1,5},{5,9},... | collective-permute-start | bytes 786440 | tf_op jit(solution)/shard_map/ppermute | solution.py:391
  5.7 0.8 reshape.14
  6.5 0.7 pad_add_fusion
  7.2 0.6 broadcast_in_dim.2
  7.8 6.3 %all-to-all-start = ((s32[8,8,128]{2,1,0:T(8,128)}), s32[8,8,128]{2,1,0:T(8,128)S(1)}, u32[]{:S(2)}, u32[]{:S(2)}) async-start(s32[8,8,128]{2,1,0:T(8,128)} %broadcast_in_dim.2), calls=%async_computation | async-start | bytes 65536 | tf_op jit(solution)/shard_map/all_to_all | solution.py:414
  14.1 2.1 %collective-permute-start.4 = (bf16[256,512]{1,0:T(8,128)(2,1)S(1)}, bf16[256,512]{1,0:T(8,128)(2,1)S(1)}, u32[]{:S(2)}, u32[]{:S(2)}) collective-permute-start(bf16[256,512]{1,0:T(8,128)(2,1)S(1)} %collective-permute-done.2.refs_2_.refs_0_), channel_id=1, source_target_pairs={{0,4},{4,8},{8,12},{12,14},{14,10},{10,6},{6,2},{2,0},{1,5},{5,9},... | collective-permute-start | bytes 786440 | tf_op jit(solution)/shard_map/ppermute | solution.py:391
  16.2 4.8 %all-to-all-done.notes_ref = s32[8,8,128]{2,1,0:T(8,128)S(1)} async-done(((s32[8,8,128]{2,1,0:T(8,128)}), s32[8,8,128]{2,1,0:T(8,128)S(1)}, u32[]{:S(2)}, u32[]{:S(2)}) %all-to-all-start) | async-done | bytes 32800 | tf_op jit(solution)/shard_map/all_to_all | solution.py:414
  21.1 0.7 collective-permute-start.6
  21.8 1.3 %collective-permute-start.7 = (bf16[256,512]{1,0:T(8,128)(2,1)S(1)}, bf16[256,512]{1,0:T(8,128)(2,1)S(1)}, u32[]{:S(2)}, u32[]{:S(2)}) collective-permute-start(bf16[256,512]{1,0:T(8,128)(2,1)S(1)} %collective-permute-done.1.refs_5_.refs_3_), channel_id=1, source_target_pairs={{4,0},{8,4},{12,8},{14,12},{10,14},{6,10},{2,6},{0,2},{5,1},{9,5},... | collective-permute-start | bytes 786440 | tf_op jit(solution)/shard_map/ppermute | solution.py:394
  23.1 1.1 %pad_maximum_fusion.refs_0_.refs_1_ = bf16[2,256,512]{2,1,0:T(8,128)(2,1)S(1)} fusion(bf16[1,256,512]{2,1,0:T(8,128)(2,1)} %bitcast.7, bf16[1,256,512]{2,1,0:T(8,128)(2,1)} %bitcast.8), kind=kLoop, calls=%fused_computation | loop fusion | flops 262144 | bytes 1048576 | tf_op jit(solution)/shard_map/stack | solution.py:454
  24.2 1.4 %collective-permute-done.5.refs_2_ = bf16[256,512]{1,0:T(8,128)(2,1)S(1)} collective-permute-done((bf16[256,512]{1,0:T(8,128)(2,1)S(1)}, bf16[256,512]{1,0:T(8,128)(2,1)S(1)}, u32[]{:S(2)}, u32[]{:S(2)}) %collective-permute-start.5) | collective-permute-done | bytes 262176 | tf_op jit(solution)/shard_map/ppermute | solution.py:394
  25.6 1.5 %collective-permute-start.8 = (bf16[256,512]{1,0:T(8,128)(2,1)S(1)}, bf16[256,512]{1,0:T(8,128)(2,1)S(1)}, u32[]{:S(2)}, u32[]{:S(2)}) collective-permute-start(bf16[256,512]{1,0:T(8,128)(2,1)S(1)} %collective-permute-done.4.refs_0_), channel_id=1, source_target_pairs={{0,4},{4,8},{8,12},{12,14},{14,10},{10,6},{6,2},{2,0},{1,5},{5,9},... | collective-permute-start | bytes 786440 | tf_op jit(solution)/shard_map/ppermute | solution.py:391
  28.1 1.2 %copy-done = bf16[256,2048]{1,0:T(8,128)(2,1)S(1)} copy-done((bf16[256,2048]{1,0:T(8,128)(2,1)S(1)}, bf16[256,2048]{1,0:T(8,128)(2,1)}, u32[]{:S(2)}) %copy-start) | copy-done | bytes 1048600
  29.3 2.8 %shard_map.86 = (f32[2,1,1024]{2,1,0:T(1,128)S(1)}, f32[2,1,1024]{2,1,0:T(1,128)S(1)}, f32[2,128,1024]{2,1,0:T(8,128)S(1)}) custom-call(bf16[256,2048]{1,0:T(8,128)(2,1)S(1)} %copy-done, bf16[256,128]{1,0:T(8,128)(2,1)S(1)} %get-tuple-element.120.mask_ref, bf16[8,256,128]{2,1,0:T(8,128)(2,1)S(1)} %get-tuple-element.121.hot_ref, ...), custom_call_target="tpu_custom_call" | custom-call | flops 6 | bytes 256 | tf_op jit(solution)/shard_map/pallas_call | solution.py:397
  32.2 1.5 %collective-permute-start.10 = (bf16[256,512]{1,0:T(8,128)(2,1)S(1)}, bf16[256,512]{1,0:T(8,128)(2,1)S(1)}, u32[]{:S(2)}, u32[]{:S(2)}) collective-permute-start(bf16[256,512]{1,0:T(8,128)(2,1)S(1)} %collective-permute-done.6.refs_1_), channel_id=1, source_target_pairs={{0,4},{4,8},{8,12},{12,14},{14,10},{10,6},{6,2},{2,0},{1,5},{5,9},... | collective-permute-start | bytes 786440 | tf_op jit(solution)/shard_map/ppermute | solution.py:391
  34.2 2.9 %shard_map.87 = (f32[2,1,1024]{2,1,0:T(1,128)S(1)}, f32[2,1,1024]{2,1,0:T(1,128)S(1)}, f32[2,128,1024]{2,1,0:T(8,128)S(1)}) custom-call(bf16[256,2048]{1,0:T(8,128)(2,1)S(1)} %copy-done, bf16[256,128]{1,0:T(8,128)(2,1)S(1)} %get-tuple-element.120.mask_ref, bf16[8,256,128]{2,1,0:T(8,128)(2,1)S(1)} %get-tuple-element.121.hot_ref, ...), custom_call_target="tpu_custom_call" | custom-call | flops 6 | bytes 256 | tf_op jit(solution)/shard_map/pallas_call | solution.py:397
  37.1 1.5 %collective-permute-start.12 = (bf16[256,512]{1,0:T(8,128)(2,1)S(1)}, bf16[256,512]{1,0:T(8,128)(2,1)S(1)}, u32[]{:S(2)}, u32[]{:S(2)}) collective-permute-start(bf16[256,512]{1,0:T(8,128)(2,1)S(1)} %collective-permute-done.8.refs_0_.refs_1_), channel_id=1, source_target_pairs={{0,4},{4,8},{8,12},{12,14},{14,10},{10,6},{6,2},{2,0},{1,5},{5,9},... | collective-permute-start | bytes 786440 | tf_op jit(solution)/shard_map/ppermute | solution.py:391
  38.7 2.1 %shard_map.88 = (f32[2,1,1024]{2,1,0:T(1,128)S(1)}, f32[2,1,1024]{2,1,0:T(1,128)S(1)}, f32[2,128,1024]{2,1,0:T(8,128)S(1)}) custom-call(bf16[256,2048]{1,0:T(8,128)(2,1)S(1)} %copy-done, bf16[256,128]{1,0:T(8,128)(2,1)S(1)} %get-tuple-element.120.mask_ref, ...), custom_call_target="tpu_custom_call", output_to_operand_aliasing={{0}: (7, {}), {1}: (8, {}), {2}: (9, {})} | custom-call | flops 4 | bytes 256 | tf_op jit(solution)/shard_map/pallas_call | solution.py:397
  40.8 2.1 %shard_map.89 = (f32[2,1,1024]{2,1,0:T(1,128)S(1)}, f32[2,1,1024]{2,1,0:T(1,128)S(1)}, f32[2,128,1024]{2,1,0:T(8,128)S(1)}) custom-call(bf16[256,2048]{1,0:T(8,128)(2,1)S(1)} %copy-done, bf16[256,128]{1,0:T(8,128)(2,1)S(1)} %get-tuple-element.120.mask_ref, ...), custom_call_target="tpu_custom_call", output_to_operand_aliasing={{0}: (7, {}), {1}: (8, {}), {2}: (9, {})} | custom-call | flops 4 | bytes 256 | tf_op jit(solution)/shard_map/pallas_call | solution.py:397
  42.9 0.6 collective-permute-start.13
  43.5 2.3 %shard_map.90 = (f32[2,1,1024]{2,1,0:T(1,128)S(1)}, f32[2,1,1024]{2,1,0:T(1,128)S(1)}, f32[2,128,1024]{2,1,0:T(8,128)S(1)}, f32[2,512,1024]{2,1,0:T(8,128)S(1)}) custom-call(bf16[256,2048]{1,0:T(8,128)(2,1)S(1)} %copy-done, bf16[256,128]{1,0:T(8,128)(2,1)S(1)} %get-tuple-element.120.mask_ref, ...), custom_call_target="tpu_custom_call", output_to_operand_aliasing={{0}: (7, {}), {1}: (8, {}), {2}: (9, {})} | custom-call | flops 4 | bytes 256 | tf_op jit(solution)/shard_map/pallas_call | solution.py:397
  45.8 2.2 %shard_map.91 = (f32[2,1,1024]{2,1,0:T(1,128)S(1)}, f32[2,1,1024]{2,1,0:T(1,128)S(1)}, f32[2,128,1024]{2,1,0:T(8,128)S(1)}, f32[2,512,1024]{2,1,0:T(8,128)S(1)}) custom-call(bf16[256,2048]{1,0:T(8,128)(2,1)S(1)} %copy-done, bf16[256,128]{1,0:T(8,128)(2,1)S(1)} %get-tuple-element.120.mask_ref, ...), custom_call_target="tpu_custom_call", output_to_operand_aliasing={{0}: (7, {}), {1}: (8, {}), {2}: (9, {})} | custom-call | flops 4 | bytes 256 | tf_op jit(solution)/shard_map/pallas_call | solution.py:397
  48.1 1.3 %collective-permute-done.13.v_ref = bf16[256,512]{1,0:T(8,128)(2,1)S(1)} collective-permute-done((bf16[256,512]{1,0:T(8,128)(2,1)S(1)}, bf16[256,512]{1,0:T(8,128)(2,1)S(1)}, u32[]{:S(2)}, u32[]{:S(2)}) %collective-permute-start.13) | collective-permute-done | bytes 262176 | tf_op jit(solution)/shard_map/ppermute | solution.py:394
  49.4 2.9 %shard_map.92 = (f32[2,1,1024]{2,1,0:T(1,128)S(1)}, f32[2,1,1024]{2,1,0:T(1,128)S(1)}, f32[2,128,1024]{2,1,0:T(8,128)S(1)}, bf16[2,256,256]{2,1,0:T(8,128)(2,1)S(1)}) custom-call(bf16[256,2048]{1,0:T(8,128)(2,1)S(1)} %copy-done, bf16[256,2048]{1,0:T(8,128)(2,1)S(1)} %copy-done.1, ...), custom_call_target="tpu_custom_call", output_to_operand_aliasing={{0}: (6, {}), {1}: (7, {}), {2}: (8, {})} | custom-call | flops 7 | bytes 256 | tf_op jit(solution)/shard_map/pallas_call | solution.py:397
  52.9 2.9 %shard_map.93 = (f32[2,1,1024]{2,1,0:T(1,128)S(1)}, f32[2,1,1024]{2,1,0:T(1,128)S(1)}, f32[2,128,1024]{2,1,0:T(8,128)S(1)}, bf16[2,256,256]{2,1,0:T(8,128)(2,1)S(1)}) custom-call(bf16[256,2048]{1,0:T(8,128)(2,1)S(1)} %copy-done, bf16[256,2048]{1,0:T(8,128)(2,1)S(1)} %copy-done.1, ...), custom_call_target="tpu_custom_call", output_to_operand_aliasing={{0}: (6, {}), {1}: (7, {}), {2}: (8, {})} | custom-call | flops 7 | bytes 256 | tf_op jit(solution)/shard_map/pallas_call | solution.py:397
  55.8 1.7 %collective-permute-start.15 = (bf16[2,256,256]{2,1,0:T(8,128)(2,1)S(1)}, bf16[2,256,256]{2,1,0:T(8,128)(2,1)S(1)}, u32[]{:S(2)}, u32[]{:S(2)}) collective-permute-start(bf16[2,256,256]{2,1,0:T(8,128)(2,1)S(1)} %get-tuple-element.196), channel_id=1, source_target_pairs={{0,4},{4,8},{8,12},{12,14},{14,10},{10,6},{6,2},{2,0},{1,5},{5,9},... | collective-permute-start | bytes 786440 | tf_op jit(solution)/shard_map/ppermute | solution.py:391
  57.5 2.3 %shard_map.94 = (f32[2,128,1024]{2,1,0:T(8,128)S(1)}, f32[2,256,256]{2,1,0:T(8,128)S(1)}, f32[2,256,256]{2,1,0:T(8,128)S(1)}) custom-call(bf16[256,2048]{1,0:T(8,128)(2,1)S(1)} %copy-done, bf16[256,2048]{1,0:T(8,128)(2,1)S(1)} %copy-done.1, bf16[256,128]{1,0:T(8,128)(2,1)S(1)} %get-tuple-element.120.mask_ref, ...), custom_call_target="tpu_custom_call", output_to_operand_aliasing={{0}: (11, {})} | custom-call | flops 10 | bytes 256 | tf_op jit(solution)/shard_map/pallas_call | solution.py:397
  61.0 1.6 %collective-permute-start.17 = (bf16[2,256,256]{2,1,0:T(8,128)(2,1)S(1)}, bf16[2,256,256]{2,1,0:T(8,128)(2,1)S(1)}, u32[]{:S(2)}, u32[]{:S(2)}) collective-permute-start(bf16[2,256,256]{2,1,0:T(8,128)(2,1)S(1)} %convert_element_type.86), channel_id=1, source_target_pairs={{0,4},{4,8},{8,12},{12,14},{14,10},{10,6},{6,2},{2,0},{1,5},{5,9},... | collective-permute-start | bytes 786440 | tf_op jit(solution)/shard_map/ppermute | solution.py:391
  62.6 2.3 %shard_map.95 = (f32[2,128,1024]{2,1,0:T(8,128)S(1)}, f32[2,256,256]{2,1,0:T(8,128)S(1)}, f32[2,256,256]{2,1,0:T(8,128)S(1)}) custom-call(bf16[256,2048]{1,0:T(8,128)(2,1)S(1)} %copy-done, bf16[256,2048]{1,0:T(8,128)(2,1)S(1)} %copy-done.1, bf16[256,128]{1,0:T(8,128)(2,1)S(1)} %get-tuple-element.120.mask_ref, ...), custom_call_target="tpu_custom_call", output_to_operand_aliasing={{0}: (11, {})} | custom-call | flops 10 | bytes 256 | tf_op jit(solution)/shard_map/pallas_call | solution.py:397
  65.0 0.7 collective-permute-start.18
  65.7 1.4 %collective-permute-start.19 = (bf16[2,256,256]{2,1,0:T(8,128)(2,1)S(1)}, bf16[2,256,256]{2,1,0:T(8,128)(2,1)S(1)}, u32[]{:S(2)}, u32[]{:S(2)}) collective-permute-start(bf16[2,256,256]{2,1,0:T(8,128)(2,1)S(1)} %add_convert_fusion.10), channel_id=1, source_target_pairs={{0,4},{4,8},{8,12},{12,14},{14,10},{10,6},{6,2},{2,0},{1,5},{5,9},... | collective-permute-start | bytes 786440 | tf_op jit(solution)/shard_map/ppermute | solution.py:391
  67.1 2.9 %shard_map.96 = (f32[2,128,1024]{2,1,0:T(8,128)S(1)}, f32[2,256,256]{2,1,0:T(8,128)S(1)}, f32[2,256,256]{2,1,0:T(8,128)S(1)}) custom-call(bf16[256,2048]{1,0:T(8,128)(2,1)S(1)} %copy-done, bf16[256,2048]{1,0:T(8,128)(2,1)S(1)} %copy-done.1, bf16[256,128]{1,0:T(8,128)(2,1)S(1)} %get-tuple-element.120.mask_ref, ...), custom_call_target="tpu_custom_call", output_to_operand_aliasing={{0}: (10, {})} | custom-call | flops 10 | bytes 256 | tf_op jit(solution)/shard_map/pallas_call | solution.py:397
  70.3 1.1 %collective-permute-start.20 = (bf16[2,256,256]{2,1,0:T(8,128)(2,1)S(1)}, bf16[2,256,256]{2,1,0:T(8,128)(2,1)S(1)}, u32[]{:S(2)}, u32[]{:S(2)}) collective-permute-start(bf16[2,256,256]{2,1,0:T(8,128)(2,1)S(1)} %add_convert_fusion.9), channel_id=1, source_target_pairs={{4,0},{8,4},{12,8},{14,12},{10,14},{6,10},{2,6},{0,2},{5,1},{9,5},... | collective-permute-start | bytes 786440 | tf_op jit(solution)/shard_map/ppermute | solution.py:394
  71.3 1.0 %collective-permute-start.21 = (bf16[2,256,256]{2,1,0:T(8,128)(2,1)S(1)}, bf16[2,256,256]{2,1,0:T(8,128)(2,1)S(1)}, u32[]{:S(2)}, u32[]{:S(2)}) collective-permute-start(bf16[2,256,256]{2,1,0:T(8,128)(2,1)S(1)} %add_convert_fusion.8), channel_id=1, source_target_pairs={{0,4},{4,8},{8,12},{12,14},{14,10},{10,6},{6,2},{2,0},{1,5},{5,9},... | collective-permute-start | bytes 786440 | tf_op jit(solution)/shard_map/ppermute | solution.py:391
  72.3 2.9 %shard_map.97 = (f32[2,128,1024]{2,1,0:T(8,128)S(1)}, f32[2,256,256]{2,1,0:T(8,128)S(1)}, f32[2,256,256]{2,1,0:T(8,128)S(1)}) custom-call(bf16[256,2048]{1,0:T(8,128)(2,1)S(1)} %copy-done, bf16[256,2048]{1,0:T(8,128)(2,1)S(1)} %copy-done.1, bf16[256,128]{1,0:T(8,128)(2,1)S(1)} %get-tuple-element.120.mask_ref, ...), custom_call_target="tpu_custom_call", output_to_operand_aliasing={{0}: (10, {})} | custom-call | flops 10 | bytes 256 | tf_op jit(solution)/shard_map/pallas_call | solution.py:397
  75.9 1.1 %collective-permute-start.22 = (bf16[2,256,256]{2,1,0:T(8,128)(2,1)S(1)}, bf16[2,256,256]{2,1,0:T(8,128)(2,1)S(1)}, u32[]{:S(2)}, u32[]{:S(2)}) collective-permute-start(bf16[2,256,256]{2,1,0:T(8,128)(2,1)S(1)} %add_convert_fusion.7), channel_id=1, source_target_pairs={{4,0},{8,4},{12,8},{14,12},{10,14},{6,10},{2,6},{0,2},{5,1},{9,5},... | collective-permute-start | bytes 786440 | tf_op jit(solution)/shard_map/ppermute | solution.py:394
  76.9 1.0 %collective-permute-start.23 = (bf16[2,256,256]{2,1,0:T(8,128)(2,1)S(1)}, bf16[2,256,256]{2,1,0:T(8,128)(2,1)S(1)}, u32[]{:S(2)}, u32[]{:S(2)}) collective-permute-start(bf16[2,256,256]{2,1,0:T(8,128)(2,1)S(1)} %add_convert_fusion.6), channel_id=1, source_target_pairs={{0,4},{4,8},{8,12},{12,14},{14,10},{10,6},{6,2},{2,0},{1,5},{5,9},... | collective-permute-start | bytes 786440 | tf_op jit(solution)/shard_map/ppermute | solution.py:391
  78.0 2.9 %shard_map.98 = (f32[2,128,1024]{2,1,0:T(8,128)S(1)}, f32[2,256,256]{2,1,0:T(8,128)S(1)}, f32[2,256,256]{2,1,0:T(8,128)S(1)}) custom-call(bf16[256,2048]{1,0:T(8,128)(2,1)S(1)} %copy-done, bf16[256,2048]{1,0:T(8,128)(2,1)S(1)} %copy-done.1, bf16[256,128]{1,0:T(8,128)(2,1)S(1)} %get-tuple-element.120.mask_ref, ...), custom_call_target="tpu_custom_call", output_to_operand_aliasing={{0}: (10, {})} | custom-call | flops 10 | bytes 256 | tf_op jit(solution)/shard_map/pallas_call | solution.py:397
  81.5 1.1 %collective-permute-start.24 = (bf16[2,256,256]{2,1,0:T(8,128)(2,1)S(1)}, bf16[2,256,256]{2,1,0:T(8,128)(2,1)S(1)}, u32[]{:S(2)}, u32[]{:S(2)}) collective-permute-start(bf16[2,256,256]{2,1,0:T(8,128)(2,1)S(1)} %add_convert_fusion.5), channel_id=1, source_target_pairs={{4,0},{8,4},{12,8},{14,12},{10,14},{6,10},{2,6},{0,2},{5,1},{9,5},... | collective-permute-start | bytes 786440 | tf_op jit(solution)/shard_map/ppermute | solution.py:394
  82.6 1.0 %collective-permute-start.25 = (bf16[2,256,256]{2,1,0:T(8,128)(2,1)S(1)}, bf16[2,256,256]{2,1,0:T(8,128)(2,1)S(1)}, u32[]{:S(2)}, u32[]{:S(2)}) collective-permute-start(bf16[2,256,256]{2,1,0:T(8,128)(2,1)S(1)} %add_convert_fusion.4), channel_id=1, source_target_pairs={{0,4},{4,8},{8,12},{12,14},{14,10},{10,6},{6,2},{2,0},{1,5},{5,9},... | collective-permute-start | bytes 786440 | tf_op jit(solution)/shard_map/ppermute | solution.py:391
  83.6 2.9 %shard_map.99 = (f32[2,128,1024]{2,1,0:T(8,128)S(1)}, f32[2,256,256]{2,1,0:T(8,128)S(1)}, f32[2,256,256]{2,1,0:T(8,128)S(1)}) custom-call(bf16[256,2048]{1,0:T(8,128)(2,1)S(1)} %copy-done, bf16[256,2048]{1,0:T(8,128)(2,1)S(1)} %copy-done.1, bf16[256,128]{1,0:T(8,128)(2,1)S(1)} %get-tuple-element.120.mask_ref, ...), custom_call_target="tpu_custom_call", output_to_operand_aliasing={{0}: (10, {})} | custom-call | flops 10 | bytes 256 | tf_op jit(solution)/shard_map/pallas_call | solution.py:397
  87.1 1.1 %collective-permute-start.26 = (bf16[2,256,256]{2,1,0:T(8,128)(2,1)S(1)}, bf16[2,256,256]{2,1,0:T(8,128)(2,1)S(1)}, u32[]{:S(2)}, u32[]{:S(2)}) collective-permute-start(bf16[2,256,256]{2,1,0:T(8,128)(2,1)S(1)} %add_convert_fusion.3), channel_id=1, source_target_pairs={{4,0},{8,4},{12,8},{14,12},{10,14},{6,10},{2,6},{0,2},{5,1},{9,5},... | collective-permute-start | bytes 786440 | tf_op jit(solution)/shard_map/ppermute | solution.py:394
  88.2 1.0 %collective-permute-start.27 = (bf16[2,256,256]{2,1,0:T(8,128)(2,1)S(1)}, bf16[2,256,256]{2,1,0:T(8,128)(2,1)S(1)}, u32[]{:S(2)}, u32[]{:S(2)}) collective-permute-start(bf16[2,256,256]{2,1,0:T(8,128)(2,1)S(1)} %add_convert_fusion.2), channel_id=1, source_target_pairs={{0,4},{4,8},{8,12},{12,14},{14,10},{10,6},{6,2},{2,0},{1,5},{5,9},... | collective-permute-start | bytes 786440 | tf_op jit(solution)/shard_map/ppermute | solution.py:391
  89.2 1.7 %shard_map.101 = (f32[2,128,1024]{2,1,0:T(8,128)S(1)}, f32[2,256,256]{2,1,0:T(8,128)S(1)}) custom-call(bf16[256,2048]{1,0:T(8,128)(2,1)S(1)} %copy-done, bf16[256,2048]{1,0:T(8,128)(2,1)S(1)} %copy-done.1, bf16[256,128]{1,0:T(8,128)(2,1)S(1)} %get-tuple-element.120.mask_ref, ...), custom_call_target="tpu_custom_call", output_to_operand_aliasing={{0}: (8, {})} | custom-call | flops 5 | bytes 256 | tf_op jit(solution)/shard_map/pallas_call | solution.py:397
  90.9 1.7 %shard_map.100 = (f32[2,128,1024]{2,1,0:T(8,128)S(1)}, f32[2,256,256]{2,1,0:T(8,128)S(1)}) custom-call(bf16[256,2048]{1,0:T(8,128)(2,1)S(1)} %copy-done, bf16[256,2048]{1,0:T(8,128)(2,1)S(1)} %copy-done.1, bf16[256,128]{1,0:T(8,128)(2,1)S(1)} %get-tuple-element.120.mask_ref, ...), custom_call_target="tpu_custom_call", output_to_operand_aliasing={{0}: (8, {})} | custom-call | flops 5 | bytes 256 | tf_op jit(solution)/shard_map/pallas_call | solution.py:397
  92.7 1.5 %shard_map.102 = bf16[256,2048]{1,0:T(8,128)(2,1)} custom-call(f32[2,128,1024]{2,1,0:T(8,128)S(1)} %get-tuple-element.229.refs_0_, f32[2,128,1024]{2,1,0:T(8,128)S(1)} %get-tuple-element.230.refs_1_), custom_call_target="tpu_custom_call" | custom-call | bytes 256 | tf_op jit(solution)/shard_map/pallas_call | solution.py:397
  94.6 0.8 fusion.2
  (52 shorter events, 6.0 us)
Async XLA Ops:
  0.6 13.4 %collective-permute-start.2 = (bf16[256,512]{1,0:T(8,128)(2,1)}, bf16[256,512]{1,0:T(8,128)(2,1)S(1)}, u32[]{:S(2)}, u32[]{:S(2)}) collective-permute-start(bf16[256,512]{1,0:T(8,128)(2,1)} %param.7), channel_id=1, source_target_pairs={{0,4},{4,8},{8,12},{12,14},{14,10},{10,6},{6,2},{2,0},{1,5},{5,9},... | collective-permute-start | bytes 786440 | tf_op jit(solution)/shard_map/ppermute | solution.py:391
  3.7 10.4 %collective-permute-start.3 = (bf16[256,512]{1,0:T(8,128)(2,1)}, bf16[256,512]{1,0:T(8,128)(2,1)S(1)}, u32[]{:S(2)}, u32[]{:S(2)}) collective-permute-start(bf16[256,512]{1,0:T(8,128)(2,1)} %param.7), channel_id=1, source_target_pairs={{4,0},{8,4},{12,8},{14,12},{10,14},{6,10},{2,6},{0,2},{5,1},{9,5},... | collective-permute-start | bytes 786440 | tf_op jit(solution)/shard_map/ppermute | solution.py:394
  3.7 17.3 %collective-permute-start = (bf16[256,512]{1,0:T(8,128)(2,1)}, bf16[256,512]{1,0:T(8,128)(2,1)S(1)}, u32[]{:S(2)}, u32[]{:S(2)}) collective-permute-start(bf16[256,512]{1,0:T(8,128)(2,1)} %param.8), channel_id=1, source_target_pairs={{0,4},{4,8},{8,12},{12,14},{14,10},{10,6},{6,2},{2,0},{1,5},{5,9},... | collective-permute-start | bytes 786440 | tf_op jit(solution)/shard_map/ppermute | solution.py:391
  5.7 15.3 %collective-permute-start.1 = (bf16[256,512]{1,0:T(8,128)(2,1)}, bf16[256,512]{1,0:T(8,128)(2,1)S(1)}, u32[]{:S(2)}, u32[]{:S(2)}) collective-permute-start(bf16[256,512]{1,0:T(8,128)(2,1)} %param.8), channel_id=1, source_target_pairs={{4,0},{8,4},{12,8},{14,12},{10,14},{6,10},{2,6},{0,2},{5,1},{9,5},... | collective-permute-start | bytes 786440 | tf_op jit(solution)/shard_map/ppermute | solution.py:394
  7.8 13.2 %all-to-all-start = ((s32[8,8,128]{2,1,0:T(8,128)}), s32[8,8,128]{2,1,0:T(8,128)S(1)}, u32[]{:S(2)}, u32[]{:S(2)}) async-start(s32[8,8,128]{2,1,0:T(8,128)} %broadcast_in_dim.2), calls=%async_computation | async-start | bytes 65536 | tf_op jit(solution)/shard_map/all_to_all | solution.py:414
  14.1 10.1 %collective-permute-start.4 = (bf16[256,512]{1,0:T(8,128)(2,1)S(1)}, bf16[256,512]{1,0:T(8,128)(2,1)S(1)}, u32[]{:S(2)}, u32[]{:S(2)}) collective-permute-start(bf16[256,512]{1,0:T(8,128)(2,1)S(1)} %collective-permute-done.2.refs_2_.refs_0_), channel_id=1, source_target_pairs={{0,4},{4,8},{8,12},{12,14},{14,10},{10,6},{6,2},{2,0},{1,5},{5,9},... | collective-permute-start | bytes 786440 | tf_op jit(solution)/shard_map/ppermute | solution.py:391
  16.1 9.4 %collective-permute-start.5 = (bf16[256,512]{1,0:T(8,128)(2,1)S(1)}, bf16[256,512]{1,0:T(8,128)(2,1)S(1)}, u32[]{:S(2)}, u32[]{:S(2)}) collective-permute-start(bf16[256,512]{1,0:T(8,128)(2,1)S(1)} %collective-permute-done.3.refs_4_.refs_2_), channel_id=1, source_target_pairs={{4,0},{8,4},{12,8},{14,12},{10,14},{6,10},{2,6},{0,2},{5,1},{9,5},... | collective-permute-start | bytes 786440 | tf_op jit(solution)/shard_map/ppermute | solution.py:394
  21.1 11.1 %collective-permute-start.6 = (bf16[256,512]{1,0:T(8,128)(2,1)S(1)}, bf16[256,512]{1,0:T(8,128)(2,1)S(1)}, u32[]{:S(2)}, u32[]{:S(2)}) collective-permute-start(bf16[256,512]{1,0:T(8,128)(2,1)S(1)} %collective-permute-done.refs_3_.refs_1_), channel_id=1, source_target_pairs={{0,4},{4,8},{8,12},{12,14},{14,10},{10,6},{6,2},{2,0},{1,5},{5,9},... | collective-permute-start | bytes 786440 | tf_op jit(solution)/shard_map/ppermute | solution.py:391
  21.8 10.3 %collective-permute-start.7 = (bf16[256,512]{1,0:T(8,128)(2,1)S(1)}, bf16[256,512]{1,0:T(8,128)(2,1)S(1)}, u32[]{:S(2)}, u32[]{:S(2)}) collective-permute-start(bf16[256,512]{1,0:T(8,128)(2,1)S(1)} %collective-permute-done.1.refs_5_.refs_3_), channel_id=1, source_target_pairs={{4,0},{8,4},{12,8},{14,12},{10,14},{6,10},{2,6},{0,2},{5,1},{9,5},... | collective-permute-start | bytes 786440 | tf_op jit(solution)/shard_map/ppermute | solution.py:394
  25.6 11.6 %collective-permute-start.8 = (bf16[256,512]{1,0:T(8,128)(2,1)S(1)}, bf16[256,512]{1,0:T(8,128)(2,1)S(1)}, u32[]{:S(2)}, u32[]{:S(2)}) collective-permute-start(bf16[256,512]{1,0:T(8,128)(2,1)S(1)} %collective-permute-done.4.refs_0_), channel_id=1, source_target_pairs={{0,4},{4,8},{8,12},{12,14},{14,10},{10,6},{6,2},{2,0},{1,5},{5,9},... | collective-permute-start | bytes 786440 | tf_op jit(solution)/shard_map/ppermute | solution.py:391
  27.0 10.1 %collective-permute-start.9 = (bf16[256,512]{1,0:T(8,128)(2,1)S(1)}, bf16[256,512]{1,0:T(8,128)(2,1)S(1)}, u32[]{:S(2)}, u32[]{:S(2)}) collective-permute-start(bf16[256,512]{1,0:T(8,128)(2,1)S(1)} %collective-permute-done.5.refs_2_), channel_id=1, source_target_pairs={{4,0},{8,4},{12,8},{14,12},{10,14},{6,10},{2,6},{0,2},{5,1},{9,5},... | collective-permute-start | bytes 786440 | tf_op jit(solution)/shard_map/ppermute | solution.py:394
  28.1 1.2 %copy-start = (bf16[256,2048]{1,0:T(8,128)(2,1)S(1)}, bf16[256,2048]{1,0:T(8,128)(2,1)}, u32[]{:S(2)}) copy-start(bf16[256,2048]{1,0:T(8,128)(2,1)} %q_ref.31) | copy-start | bytes 3145732
  32.2 10.8 %collective-permute-start.10 = (bf16[256,512]{1,0:T(8,128)(2,1)S(1)}, bf16[256,512]{1,0:T(8,128)(2,1)S(1)}, u32[]{:S(2)}, u32[]{:S(2)}) collective-permute-start(bf16[256,512]{1,0:T(8,128)(2,1)S(1)} %collective-permute-done.6.refs_1_), channel_id=1, source_target_pairs={{0,4},{4,8},{8,12},{12,14},{14,10},{10,6},{6,2},{2,0},{1,5},{5,9},... | collective-permute-start | bytes 786440 | tf_op jit(solution)/shard_map/ppermute | solution.py:391
  33.7 9.3 %collective-permute-start.11 = (bf16[256,512]{1,0:T(8,128)(2,1)S(1)}, bf16[256,512]{1,0:T(8,128)(2,1)S(1)}, u32[]{:S(2)}, u32[]{:S(2)}) collective-permute-start(bf16[256,512]{1,0:T(8,128)(2,1)S(1)} %collective-permute-done.7.refs_3_), channel_id=1, source_target_pairs={{4,0},{8,4},{12,8},{14,12},{10,14},{6,10},{2,6},{0,2},{5,1},{9,5},... | collective-permute-start | bytes 786440 | tf_op jit(solution)/shard_map/ppermute | solution.py:394
  37.1 10.9 %collective-permute-start.12 = (bf16[256,512]{1,0:T(8,128)(2,1)S(1)}, bf16[256,512]{1,0:T(8,128)(2,1)S(1)}, u32[]{:S(2)}, u32[]{:S(2)}) collective-permute-start(bf16[256,512]{1,0:T(8,128)(2,1)S(1)} %collective-permute-done.8.refs_0_.refs_1_), channel_id=1, source_target_pairs={{0,4},{4,8},{8,12},{12,14},{14,10},{10,6},{6,2},{2,0},{1,5},{5,9},... | collective-permute-start | bytes 786440 | tf_op jit(solution)/shard_map/ppermute | solution.py:391
  42.9 6.5 %copy-start.1 = (bf16[256,2048]{1,0:T(8,128)(2,1)S(1)}, bf16[256,2048]{1,0:T(8,128)(2,1)}, u32[]{:S(2)}) copy-start(bf16[256,2048]{1,0:T(8,128)(2,1)} %g_ref.19) | copy-start | bytes 3145732
  42.9 6.4 %collective-permute-start.13 = (bf16[256,512]{1,0:T(8,128)(2,1)S(1)}, bf16[256,512]{1,0:T(8,128)(2,1)S(1)}, u32[]{:S(2)}, u32[]{:S(2)}) collective-permute-start(bf16[256,512]{1,0:T(8,128)(2,1)S(1)} %collective-permute-done.11.refs_3_.refs_4_), channel_id=1, source_target_pairs={{4,0},{8,4},{12,8},{14,12},{10,14},{6,10},{2,6},{0,2},{5,1},{9,5},... | collective-permute-start | bytes 786440 | tf_op jit(solution)/shard_map/ppermute | solution.py:394
  52.3 8.2 %collective-permute-start.14 = (bf16[2,256,256]{2,1,0:T(8,128)(2,1)S(1)}, bf16[2,256,256]{2,1,0:T(8,128)(2,1)S(1)}, u32[]{:S(2)}, u32[]{:S(2)}) collective-permute-start(bf16[2,256,256]{2,1,0:T(8,128)(2,1)S(1)} %get-tuple-element.188), channel_id=1, source_target_pairs={{4,0},{8,4},{12,8},{14,12},{10,14},{6,10},{2,6},{0,2},{5,1},{9,5},... | collective-permute-start | bytes 786440 | tf_op jit(solution)/shard_map/ppermute | solution.py:394
  55.8 9.1 %collective-permute-start.15 = (bf16[2,256,256]{2,1,0:T(8,128)(2,1)S(1)}, bf16[2,256,256]{2,1,0:T(8,128)(2,1)S(1)}, u32[]{:S(2)}, u32[]{:S(2)}) collective-permute-start(bf16[2,256,256]{2,1,0:T(8,128)(2,1)S(1)} %get-tuple-element.196), channel_id=1, source_target_pairs={{0,4},{4,8},{8,12},{12,14},{14,10},{10,6},{6,2},{2,0},{1,5},{5,9},... | collective-permute-start | bytes 786440 | tf_op jit(solution)/shard_map/ppermute | solution.py:391
  60.5 9.5 %collective-permute-start.16 = (bf16[2,256,256]{2,1,0:T(8,128)(2,1)S(1)}, bf16[2,256,256]{2,1,0:T(8,128)(2,1)S(1)}, u32[]{:S(2)}, u32[]{:S(2)}) collective-permute-start(bf16[2,256,256]{2,1,0:T(8,128)(2,1)S(1)} %add_convert_fusion.11), channel_id=1, source_target_pairs={{4,0},{8,4},{12,8},{14,12},{10,14},{6,10},{2,6},{0,2},{5,1},{9,5},... | collective-permute-start | bytes 786440 | tf_op jit(solution)/shard_map/ppermute | solution.py:394
  61.0 9.2 %collective-permute-start.17 = (bf16[2,256,256]{2,1,0:T(8,128)(2,1)S(1)}, bf16[2,256,256]{2,1,0:T(8,128)(2,1)S(1)}, u32[]{:S(2)}, u32[]{:S(2)}) collective-permute-start(bf16[2,256,256]{2,1,0:T(8,128)(2,1)S(1)} %convert_element_type.86), channel_id=1, source_target_pairs={{0,4},{4,8},{8,12},{12,14},{14,10},{10,6},{6,2},{2,0},{1,5},{5,9},... | collective-permute-start | bytes 786440 | tf_op jit(solution)/shard_map/ppermute | solution.py:391
  65.0 10.2 %collective-permute-start.18 = (bf16[2,256,256]{2,1,0:T(8,128)(2,1)S(1)}, bf16[2,256,256]{2,1,0:T(8,128)(2,1)S(1)}, u32[]{:S(2)}, u32[]{:S(2)}) collective-permute-start(bf16[2,256,256]{2,1,0:T(8,128)(2,1)S(1)} %convert_element_type.87), channel_id=1, source_target_pairs={{4,0},{8,4},{12,8},{14,12},{10,14},{6,10},{2,6},{0,2},{5,1},{9,5},... | collective-permute-start | bytes 786440 | tf_op jit(solution)/shard_map/ppermute | solution.py:394
  65.7 10.1 %collective-permute-start.19 = (bf16[2,256,256]{2,1,0:T(8,128)(2,1)S(1)}, bf16[2,256,256]{2,1,0:T(8,128)(2,1)S(1)}, u32[]{:S(2)}, u32[]{:S(2)}) collective-permute-start(bf16[2,256,256]{2,1,0:T(8,128)(2,1)S(1)} %add_convert_fusion.10), channel_id=1, source_target_pairs={{0,4},{4,8},{8,12},{12,14},{14,10},{10,6},{6,2},{2,0},{1,5},{5,9},... | collective-permute-start | bytes 786440 | tf_op jit(solution)/shard_map/ppermute | solution.py:391
  70.3 10.6 %collective-permute-start.20 = (bf16[2,256,256]{2,1,0:T(8,128)(2,1)S(1)}, bf16[2,256,256]{2,1,0:T(8,128)(2,1)S(1)}, u32[]{:S(2)}, u32[]{:S(2)}) collective-permute-start(bf16[2,256,256]{2,1,0:T(8,128)(2,1)S(1)} %add_convert_fusion.9), channel_id=1, source_target_pairs={{4,0},{8,4},{12,8},{14,12},{10,14},{6,10},{2,6},{0,2},{5,1},{9,5},... | collective-permute-start | bytes 786440 | tf_op jit(solution)/shard_map/ppermute | solution.py:394
  71.3 10.1 %collective-permute-start.21 = (bf16[2,256,256]{2,1,0:T(8,128)(2,1)S(1)}, bf16[2,256,256]{2,1,0:T(8,128)(2,1)S(1)}, u32[]{:S(2)}, u32[]{:S(2)}) collective-permute-start(bf16[2,256,256]{2,1,0:T(8,128)(2,1)S(1)} %add_convert_fusion.8), channel_id=1, source_target_pairs={{0,4},{4,8},{8,12},{12,14},{14,10},{10,6},{6,2},{2,0},{1,5},{5,9},... | collective-permute-start | bytes 786440 | tf_op jit(solution)/shard_map/ppermute | solution.py:391
  75.9 10.6 %collective-permute-start.22 = (bf16[2,256,256]{2,1,0:T(8,128)(2,1)S(1)}, bf16[2,256,256]{2,1,0:T(8,128)(2,1)S(1)}, u32[]{:S(2)}, u32[]{:S(2)}) collective-permute-start(bf16[2,256,256]{2,1,0:T(8,128)(2,1)S(1)} %add_convert_fusion.7), channel_id=1, source_target_pairs={{4,0},{8,4},{12,8},{14,12},{10,14},{6,10},{2,6},{0,2},{5,1},{9,5},... | collective-permute-start | bytes 786440 | tf_op jit(solution)/shard_map/ppermute | solution.py:394
  76.9 10.1 %collective-permute-start.23 = (bf16[2,256,256]{2,1,0:T(8,128)(2,1)S(1)}, bf16[2,256,256]{2,1,0:T(8,128)(2,1)S(1)}, u32[]{:S(2)}, u32[]{:S(2)}) collective-permute-start(bf16[2,256,256]{2,1,0:T(8,128)(2,1)S(1)} %add_convert_fusion.6), channel_id=1, source_target_pairs={{0,4},{4,8},{8,12},{12,14},{14,10},{10,6},{6,2},{2,0},{1,5},{5,9},... | collective-permute-start | bytes 786440 | tf_op jit(solution)/shard_map/ppermute | solution.py:391
  81.5 11.1 %collective-permute-start.24 = (bf16[2,256,256]{2,1,0:T(8,128)(2,1)S(1)}, bf16[2,256,256]{2,1,0:T(8,128)(2,1)S(1)}, u32[]{:S(2)}, u32[]{:S(2)}) collective-permute-start(bf16[2,256,256]{2,1,0:T(8,128)(2,1)S(1)} %add_convert_fusion.5), channel_id=1, source_target_pairs={{4,0},{8,4},{12,8},{14,12},{10,14},{6,10},{2,6},{0,2},{5,1},{9,5},... | collective-permute-start | bytes 786440 | tf_op jit(solution)/shard_map/ppermute | solution.py:394
  82.6 10.1 %collective-permute-start.25 = (bf16[2,256,256]{2,1,0:T(8,128)(2,1)S(1)}, bf16[2,256,256]{2,1,0:T(8,128)(2,1)S(1)}, u32[]{:S(2)}, u32[]{:S(2)}) collective-permute-start(bf16[2,256,256]{2,1,0:T(8,128)(2,1)S(1)} %add_convert_fusion.4), channel_id=1, source_target_pairs={{0,4},{4,8},{8,12},{12,14},{14,10},{10,6},{6,2},{2,0},{1,5},{5,9},... | collective-permute-start | bytes 786440 | tf_op jit(solution)/shard_map/ppermute | solution.py:391
  87.1 7.1 %collective-permute-start.26 = (bf16[2,256,256]{2,1,0:T(8,128)(2,1)S(1)}, bf16[2,256,256]{2,1,0:T(8,128)(2,1)S(1)}, u32[]{:S(2)}, u32[]{:S(2)}) collective-permute-start(bf16[2,256,256]{2,1,0:T(8,128)(2,1)S(1)} %add_convert_fusion.3), channel_id=1, source_target_pairs={{4,0},{8,4},{12,8},{14,12},{10,14},{6,10},{2,6},{0,2},{5,1},{9,5},... | collective-permute-start | bytes 786440 | tf_op jit(solution)/shard_map/ppermute | solution.py:394
  88.2 6.4 %collective-permute-start.27 = (bf16[2,256,256]{2,1,0:T(8,128)(2,1)S(1)}, bf16[2,256,256]{2,1,0:T(8,128)(2,1)S(1)}, u32[]{:S(2)}, u32[]{:S(2)}) collective-permute-start(bf16[2,256,256]{2,1,0:T(8,128)(2,1)S(1)} %add_convert_fusion.2), channel_id=1, source_target_pairs={{0,4},{4,8},{8,12},{12,14},{14,10},{10,6},{6,2},{2,0},{1,5},{5,9},... | collective-permute-start | bytes 786440 | tf_op jit(solution)/shard_map/ppermute | solution.py:391

commit v4 on v3

--- a/solution.py
+++ b/solution.py
@@ -188,7 +188,7 @@
 LOG2_E = 1.4426950408889634
 MASKED = -1e30
 LANES = 128
-SAVED_FROM = 3
+SAVED_FROM = 64
 NT = (((1,), (1,)), ((), ()))
 NN = (((1,), (0,)), ((), ()))
 IN_VMEM = pl.BlockSpec(memory_space=pltpu.VMEM)
@@ -324,8 +324,7 @@
 
 def turn_kernel(at, heads, group, first, q_ref, g_ref, mask_ref, hot_ref, k_ref, v_ref, top, total, mixed, norm_ref, delta_ref, q_out, grads_out):
     shards = split([k_ref, v_ref], 1, hot_ref, (at,))
-    @pl.loop(0, heads)
-    def _(head):
+    for head in range(heads):
         scores = masked_scores(q_ref, mask_ref[...], shards, hot_ref[at], head, group, first)
         state = absorb(scores, values_of(shards, first + head), (top[head], total[head], mixed[head]))
         norm = state[0] * (HEAD_DIM ** (-0.5) * LOG2_E) + jnp.log2(state[1])
@@ -461,9 +460,7 @@
                 low, high, state[0] = lax.optimization_barrier((low, high, state[0]))
                 catch_up(1, 1)
             else:
-                if c:
-                    catch_up(0, r - 1)
-                    catch_up(1, r - 1)
+                catch_up(c, r - 1)
                 low, high, state[:] = lax.optimization_barrier((low, high, state))
             behind[c].append(low)
             ahead[c].append(high)

time: 95.7 us -> 95.2 us (level)
  local copies, waits for them, and re-layouts: 2.61 us -> 1.4 us
    ppermute x14, starting transfers between devices: 9.15 us -> 11.6 us  [send_back(): return lax.ppermute(value, 'seq', back)]
    ppermute x14, starting transfers between devices: 21.1 us -> 18.9 us  [send_on(): return lax.ppermute(value, 'seq', onward)]
    unnamed x4, local copies, waits for them, and re-layouts: 1.23 us -> 0.01 us
  transfers between devices with their start and end apart: 29 -> 29, of which waited for: 9 -> 9; matrix products, arithmetic and copies ran while one was open for 4% -> 4% of each run, Pallas kernels for 41% -> 42%
where the time goes in v4:
time: 95.2 us; the launch traced here: 95 us
  Pallas kernels  42.4 us (45%)
  starting transfers between devices  36.8 us (39%)
  waiting for transfers between devices  9.91 us (10%)
  other arithmetic  3.45 us (4%)
  local copies, waits for them, and re-layouts  1.4 us (1%)
  between operations  1 us (1%)
    pallas_call x17, Pallas kernels, call(): pl.pallas_call(kernel, in_specs=[IN_VMEM] * len(args), out_specs=[IN_VMEM...  41.9 us
    ppermute x14, starting transfers between devices, send_on(): return lax.ppermute(value, 'seq', onward)  18.9 us
    ppermute x14, starting transfers between devices, send_back(): return lax.ppermute(value, 'seq', back)  11.6 us
    all_to_all x1, starting transfers between devices, gather_plan(): lax.all_to_all(jnp.broadcast_to(notes, (peers,) + notes.shape[1:]), 'seq'...  6.25 us
    all_to_all x1, waiting for transfers between devices, gather_plan(): lax.all_to_all(jnp.broadcast_to(notes, (peers,) + notes.shape[1:]), 'seq'...  4.84 us
    ppermute x14, waiting for transfers between devices, send_back(): return lax.ppermute(value, 'seq', back)  2.88 us
    ppermute x14, waiting for transfers between devices, send_on(): return lax.ppermute(value, 'seq', onward)  2.18 us
  transfers between devices with their start and end apart: 29, of which 9 were waited for; matrix products, arithmetic and copies ran while one was open for 4% of the time, Pallas kernels for 42%

profile of v4, /device:TPU:0, one launch (start us, length us, event | category | flops | bytes accessed | tf_op | source)
XLA Modules:
  0.0 95.0 jit_solution(3972949495523593227)
XLA Ops:
  0.6 3.1 %collective-permute-start.2 = (bf16[256,512]{1,0:T(8,128)(2,1)}, bf16[256,512]{1,0:T(8,128)(2,1)S(1)}, u32[]{:S(2)}, u32[]{:S(2)}) collective-permute-start(bf16[256,512]{1,0:T(8,128)(2,1)} %param.7), channel_id=1, source_target_pairs={{0,4},{4,8},{8,12},{12,14},{14,10},{10,6},{6,2},{2,0},{1,5},{5,9},... | collective-permute-start | bytes 786440 | tf_op jit(solution)/shard_map/ppermute | solution.py:390
  3.7 2.0 %collective-permute-start = (bf16[256,512]{1,0:T(8,128)(2,1)}, bf16[256,512]{1,0:T(8,128)(2,1)S(1)}, u32[]{:S(2)}, u32[]{:S(2)}) collective-permute-start(bf16[256,512]{1,0:T(8,128)(2,1)} %param.8), channel_id=1, source_target_pairs={{0,4},{4,8},{8,12},{12,14},{14,10},{10,6},{6,2},{2,0},{1,5},{5,9},... | collective-permute-start | bytes 786440 | tf_op jit(solution)/shard_map/ppermute | solution.py:390
  5.7 0.8 reshape.14
  7.8 6.3 %all-to-all-start = ((s32[8,8,128]{2,1,0:T(8,128)}), s32[8,8,128]{2,1,0:T(8,128)S(1)}, u32[]{:S(2)}, u32[]{:S(2)}) async-start(s32[8,8,128]{2,1,0:T(8,128)} %broadcast_in_dim.2), calls=%async_computation | async-start | bytes 65536 | tf_op jit(solution)/shard_map/all_to_all | solution.py:413
  14.1 2.1 %collective-permute-start.4 = (bf16[256,512]{1,0:T(8,128)(2,1)S(1)}, bf16[256,512]{1,0:T(8,128)(2,1)S(1)}, u32[]{:S(2)}, u32[]{:S(2)}) collective-permute-start(bf16[256,512]{1,0:T(8,128)(2,1)S(1)} %collective-permute-done.2.refs_2_.refs_0_), channel_id=1, source_target_pairs={{0,4},{4,8},{8,12},{12,14},{14,10},{10,6},{6,2},{2,0},{1,5},{5,9},... | collective-permute-start | bytes 786440 | tf_op jit(solution)/shard_map/ppermute | solution.py:390
  16.2 4.8 %all-to-all-done.notes_ref = s32[8,8,128]{2,1,0:T(8,128)S(1)} async-done(((s32[8,8,128]{2,1,0:T(8,128)}), s32[8,8,128]{2,1,0:T(8,128)S(1)}, u32[]{:S(2)}, u32[]{:S(2)}) %all-to-all-start) | async-done | bytes 32800 | tf_op jit(solution)/shard_map/all_to_all | solution.py:413
  21.1 0.7 collective-permute-start.6
  21.8 1.3 %collective-permute-start.7 = (bf16[256,512]{1,0:T(8,128)(2,1)S(1)}, bf16[256,512]{1,0:T(8,128)(2,1)S(1)}, u32[]{:S(2)}, u32[]{:S(2)}) collective-permute-start(bf16[256,512]{1,0:T(8,128)(2,1)S(1)} %collective-permute-done.1.refs_5_.refs_3_), channel_id=1, source_target_pairs={{4,0},{8,4},{12,8},{14,12},{10,14},{6,10},{2,6},{0,2},{5,1},{9,5},... | collective-permute-start | bytes 786440 | tf_op jit(solution)/shard_map/ppermute | solution.py:393
  23.6 1.1 %pad_maximum_fusion.refs_0_.refs_1_ = bf16[2,256,512]{2,1,0:T(8,128)(2,1)S(1)} fusion(bf16[1,256,512]{2,1,0:T(8,128)(2,1)} %bitcast.7, bf16[1,256,512]{2,1,0:T(8,128)(2,1)} %bitcast.8), kind=kLoop, calls=%fused_computation | loop fusion | flops 262144 | bytes 1048576 | tf_op jit(solution)/shard_map/stack | solution.py:453
  24.7 0.9 collective-permute-done.5.refs_2_
  25.6 1.5 %collective-permute-start.8 = (bf16[256,512]{1,0:T(8,128)(2,1)S(1)}, bf16[256,512]{1,0:T(8,128)(2,1)S(1)}, u32[]{:S(2)}, u32[]{:S(2)}) collective-permute-start(bf16[256,512]{1,0:T(8,128)(2,1)S(1)} %collective-permute-done.4.refs_0_), channel_id=1, source_target_pairs={{0,4},{4,8},{8,12},{12,14},{14,10},{10,6},{6,2},{2,0},{1,5},{5,9},... | collective-permute-start | bytes 786440 | tf_op jit(solution)/shard_map/ppermute | solution.py:390
  27.6 2.8 %shard_map.86 = (f32[2,1,1024]{2,1,0:T(1,128)S(1)}, f32[2,1,1024]{2,1,0:T(1,128)S(1)}, f32[2,128,1024]{2,1,0:T(8,128)S(1)}) custom-call(bf16[256,2048]{1,0:T(8,128)(2,1)S(1)} %copy-done, bf16[256,128]{1,0:T(8,128)(2,1)S(1)} %get-tuple-element.118.mask_ref, bf16[8,256,128]{2,1,0:T(8,128)(2,1)S(1)} %get-tuple-element.119.hot_ref, ...), custom_call_target="tpu_custom_call" | custom-call | flops 6 | bytes 256 | tf_op jit(solution)/shard_map/pallas_call | solution.py:396
  30.4 0.8 collective-permute-done.7.refs_3_
  31.2 1.5 %collective-permute-start.10 = (bf16[256,512]{1,0:T(8,128)(2,1)S(1)}, bf16[256,512]{1,0:T(8,128)(2,1)S(1)}, u32[]{:S(2)}, u32[]{:S(2)}) collective-permute-start(bf16[256,512]{1,0:T(8,128)(2,1)S(1)} %collective-permute-done.6.refs_1_), channel_id=1, source_target_pairs={{0,4},{4,8},{8,12},{12,14},{14,10},{10,6},{6,2},{2,0},{1,5},{5,9},... | collective-permute-start | bytes 786440 | tf_op jit(solution)/shard_map/ppermute | solution.py:390
  33.2 2.1 %shard_map.87 = (f32[2,1,1024]{2,1,0:T(1,128)S(1)}, f32[2,1,1024]{2,1,0:T(1,128)S(1)}, f32[2,128,1024]{2,1,0:T(8,128)S(1)}) custom-call(bf16[256,2048]{1,0:T(8,128)(2,1)S(1)} %copy-done, bf16[256,128]{1,0:T(8,128)(2,1)S(1)} %get-tuple-element.118.mask_ref, ...), custom_call_target="tpu_custom_call", output_to_operand_aliasing={{0}: (7, {}), {1}: (8, {}), {2}: (9, {})} | custom-call | flops 4 | bytes 256 | tf_op jit(solution)/shard_map/pallas_call | solution.py:396
  35.3 2.9 %shard_map.88 = (f32[2,1,1024]{2,1,0:T(1,128)S(1)}, f32[2,1,1024]{2,1,0:T(1,128)S(1)}, f32[2,128,1024]{2,1,0:T(8,128)S(1)}) custom-call(bf16[256,2048]{1,0:T(8,128)(2,1)S(1)} %copy-done, bf16[256,128]{1,0:T(8,128)(2,1)S(1)} %get-tuple-element.118.mask_ref, bf16[8,256,128]{2,1,0:T(8,128)(2,1)S(1)} %get-tuple-element.119.hot_ref, ...), custom_call_target="tpu_custom_call" | custom-call | flops 6 | bytes 256 | tf_op jit(solution)/shard_map/pallas_call | solution.py:396
  38.3 1.5 %collective-permute-start.12 = (bf16[256,512]{1,0:T(8,128)(2,1)S(1)}, bf16[256,512]{1,0:T(8,128)(2,1)S(1)}, u32[]{:S(2)}, u32[]{:S(2)}) collective-permute-start(bf16[256,512]{1,0:T(8,128)(2,1)S(1)} %collective-permute-done.8.refs_0_), channel_id=1, source_target_pairs={{0,4},{4,8},{8,12},{12,14},{14,10},{10,6},{6,2},{2,0},{1,5},{5,9},... | collective-permute-start | bytes 786440 | tf_op jit(solution)/shard_map/ppermute | solution.py:390
  39.8 2.1 %shard_map.89 = (f32[2,1,1024]{2,1,0:T(1,128)S(1)}, f32[2,1,1024]{2,1,0:T(1,128)S(1)}, f32[2,128,1024]{2,1,0:T(8,128)S(1)}) custom-call(bf16[256,2048]{1,0:T(8,128)(2,1)S(1)} %copy-done, bf16[256,128]{1,0:T(8,128)(2,1)S(1)} %get-tuple-element.118.mask_ref, ...), custom_call_target="tpu_custom_call", output_to_operand_aliasing={{0}: (7, {}), {1}: (8, {}), {2}: (9, {})} | custom-call | flops 4 | bytes 256 | tf_op jit(solution)/shard_map/pallas_call | solution.py:396
  41.9 0.9 collective-permute-start.13
  42.8 2.1 %shard_map.90 = (f32[2,1,1024]{2,1,0:T(1,128)S(1)}, f32[2,1,1024]{2,1,0:T(1,128)S(1)}, f32[2,128,1024]{2,1,0:T(8,128)S(1)}) custom-call(bf16[256,2048]{1,0:T(8,128)(2,1)S(1)} %copy-done, bf16[256,128]{1,0:T(8,128)(2,1)S(1)} %get-tuple-element.118.mask_ref, ...), custom_call_target="tpu_custom_call", output_to_operand_aliasing={{0}: (7, {}), {1}: (8, {}), {2}: (9, {})} | custom-call | flops 4 | bytes 256 | tf_op jit(solution)/shard_map/pallas_call | solution.py:396
  45.0 2.1 %shard_map.91 = (f32[2,1,1024]{2,1,0:T(1,128)S(1)}, f32[2,1,1024]{2,1,0:T(1,128)S(1)}, f32[2,128,1024]{2,1,0:T(8,128)S(1)}) custom-call(bf16[256,2048]{1,0:T(8,128)(2,1)S(1)} %copy-done, bf16[256,128]{1,0:T(8,128)(2,1)S(1)} %get-tuple-element.118.mask_ref, ...), custom_call_target="tpu_custom_call", output_to_operand_aliasing={{0}: (7, {}), {1}: (8, {}), {2}: (9, {})} | custom-call | flops 4 | bytes 256 | tf_op jit(solution)/shard_map/pallas_call | solution.py:396
  47.1 1.2 %collective-permute-done.13.v_ref = bf16[256,512]{1,0:T(8,128)(2,1)S(1)} collective-permute-done((bf16[256,512]{1,0:T(8,128)(2,1)S(1)}, bf16[256,512]{1,0:T(8,128)(2,1)S(1)}, u32[]{:S(2)}, u32[]{:S(2)}) %collective-permute-start.13) | collective-permute-done | bytes 262176 | tf_op jit(solution)/shard_map/ppermute | solution.py:393
  48.3 2.7 %shard_map.92 = (f32[2,1,1024]{2,1,0:T(1,128)S(1)}, f32[2,1,1024]{2,1,0:T(1,128)S(1)}, f32[2,128,1024]{2,1,0:T(8,128)S(1)}, bf16[2,256,256]{2,1,0:T(8,128)(2,1)S(1)}) custom-call(bf16[256,2048]{1,0:T(8,128)(2,1)S(1)} %copy-done, bf16[256,2048]{1,0:T(8,128)(2,1)S(1)} %copy-done.1, ...), custom_call_target="tpu_custom_call", output_to_operand_aliasing={{0}: (6, {}), {1}: (7, {}), {2}: (8, {})} | custom-call | flops 7 | bytes 256 | tf_op jit(solution)/shard_map/pallas_call | solution.py:396
  51.0 1.1 %collective-permute-start.14 = (bf16[2,256,256]{2,1,0:T(8,128)(2,1)S(1)}, bf16[2,256,256]{2,1,0:T(8,128)(2,1)S(1)}, u32[]{:S(2)}, u32[]{:S(2)}) collective-permute-start(bf16[2,256,256]{2,1,0:T(8,128)(2,1)S(1)} %get-tuple-element.184), channel_id=1, source_target_pairs={{4,0},{8,4},{12,8},{14,12},{10,14},{6,10},{2,6},{0,2},{5,1},{9,5},... | collective-permute-start | bytes 786440 | tf_op jit(solution)/shard_map/ppermute | solution.py:393
  52.2 2.7 %shard_map.93 = (f32[2,1,1024]{2,1,0:T(1,128)S(1)}, f32[2,1,1024]{2,1,0:T(1,128)S(1)}, f32[2,128,1024]{2,1,0:T(8,128)S(1)}, bf16[2,256,256]{2,1,0:T(8,128)(2,1)S(1)}) custom-call(bf16[256,2048]{1,0:T(8,128)(2,1)S(1)} %copy-done, bf16[256,2048]{1,0:T(8,128)(2,1)S(1)} %copy-done.1, ...), custom_call_target="tpu_custom_call", output_to_operand_aliasing={{0}: (6, {}), {1}: (7, {}), {2}: (8, {})} | custom-call | flops 7 | bytes 256 | tf_op jit(solution)/shard_map/pallas_call | solution.py:396
  54.9 1.2 %collective-permute-start.15 = (bf16[2,256,256]{2,1,0:T(8,128)(2,1)S(1)}, bf16[2,256,256]{2,1,0:T(8,128)(2,1)S(1)}, u32[]{:S(2)}, u32[]{:S(2)}) collective-permute-start(bf16[2,256,256]{2,1,0:T(8,128)(2,1)S(1)} %get-tuple-element.192), channel_id=1, source_target_pairs={{0,4},{4,8},{8,12},{12,14},{14,10},{10,6},{6,2},{2,0},{1,5},{5,9},... | collective-permute-start | bytes 786440 | tf_op jit(solution)/shard_map/ppermute | solution.py:390
  56.0 2.9 %shard_map.94 = (f32[2,128,1024]{2,1,0:T(8,128)S(1)}, f32[2,256,256]{2,1,0:T(8,128)S(1)}, f32[2,256,256]{2,1,0:T(8,128)S(1)}) custom-call(bf16[256,2048]{1,0:T(8,128)(2,1)S(1)} %copy-done, bf16[256,2048]{1,0:T(8,128)(2,1)S(1)} %copy-done.1, bf16[256,128]{1,0:T(8,128)(2,1)S(1)} %get-tuple-element.118.mask_ref, ...), custom_call_target="tpu_custom_call", output_to_operand_aliasing={{0}: (10, {})} | custom-call | flops 10 | bytes 256 | tf_op jit(solution)/shard_map/pallas_call | solution.py:396
  59.1 1.0 %collective-permute-start.16 = (bf16[2,256,256]{2,1,0:T(8,128)(2,1)S(1)}, bf16[2,256,256]{2,1,0:T(8,128)(2,1)S(1)}, u32[]{:S(2)}, u32[]{:S(2)}) collective-permute-start(bf16[2,256,256]{2,1,0:T(8,128)(2,1)S(1)} %add_convert_fusion.11), channel_id=1, source_target_pairs={{4,0},{8,4},{12,8},{14,12},{10,14},{6,10},{2,6},{0,2},{5,1},{9,5},... | collective-permute-start | bytes 786440 | tf_op jit(solution)/shard_map/ppermute | solution.py:393
  60.0 1.1 %collective-permute-start.17 = (bf16[2,256,256]{2,1,0:T(8,128)(2,1)S(1)}, bf16[2,256,256]{2,1,0:T(8,128)(2,1)S(1)}, u32[]{:S(2)}, u32[]{:S(2)}) collective-permute-start(bf16[2,256,256]{2,1,0:T(8,128)(2,1)S(1)} %convert_element_type.86), channel_id=1, source_target_pairs={{0,4},{4,8},{8,12},{12,14},{14,10},{10,6},{6,2},{2,0},{1,5},{5,9},... | collective-permute-start | bytes 786440 | tf_op jit(solution)/shard_map/ppermute | solution.py:390
  61.2 2.9 %shard_map.95 = (f32[2,128,1024]{2,1,0:T(8,128)S(1)}, f32[2,256,256]{2,1,0:T(8,128)S(1)}, f32[2,256,256]{2,1,0:T(8,128)S(1)}) custom-call(bf16[256,2048]{1,0:T(8,128)(2,1)S(1)} %copy-done, bf16[256,2048]{1,0:T(8,128)(2,1)S(1)} %copy-done.1, bf16[256,128]{1,0:T(8,128)(2,1)S(1)} %get-tuple-element.118.mask_ref, ...), custom_call_target="tpu_custom_call", output_to_operand_aliasing={{0}: (10, {})} | custom-call | flops 10 | bytes 256 | tf_op jit(solution)/shard_map/pallas_call | solution.py:396
  64.2 1.0 %collective-permute-start.18 = (bf16[2,256,256]{2,1,0:T(8,128)(2,1)S(1)}, bf16[2,256,256]{2,1,0:T(8,128)(2,1)S(1)}, u32[]{:S(2)}, u32[]{:S(2)}) collective-permute-start(bf16[2,256,256]{2,1,0:T(8,128)(2,1)S(1)} %convert_element_type.87), channel_id=1, source_target_pairs={{4,0},{8,4},{12,8},{14,12},{10,14},{6,10},{2,6},{0,2},{5,1},{9,5},... | collective-permute-start | bytes 786440 | tf_op jit(solution)/shard_map/ppermute | solution.py:393
  65.2 1.0 %collective-permute-start.19 = (bf16[2,256,256]{2,1,0:T(8,128)(2,1)S(1)}, bf16[2,256,256]{2,1,0:T(8,128)(2,1)S(1)}, u32[]{:S(2)}, u32[]{:S(2)}) collective-permute-start(bf16[2,256,256]{2,1,0:T(8,128)(2,1)S(1)} %add_convert_fusion.10), channel_id=1, source_target_pairs={{0,4},{4,8},{8,12},{12,14},{14,10},{10,6},{6,2},{2,0},{1,5},{5,9},... | collective-permute-start | bytes 786440 | tf_op jit(solution)/shard_map/ppermute | solution.py:390
  66.3 2.9 %shard_map.96 = (f32[2,128,1024]{2,1,0:T(8,128)S(1)}, f32[2,256,256]{2,1,0:T(8,128)S(1)}, f32[2,256,256]{2,1,0:T(8,128)S(1)}) custom-call(bf16[256,2048]{1,0:T(8,128)(2,1)S(1)} %copy-done, bf16[256,2048]{1,0:T(8,128)(2,1)S(1)} %copy-done.1, bf16[256,128]{1,0:T(8,128)(2,1)S(1)} %get-tuple-element.118.mask_ref, ...), custom_call_target="tpu_custom_call", output_to_operand_aliasing={{0}: (10, {})} | custom-call | flops 10 | bytes 256 | tf_op jit(solution)/shard_map/pallas_call | solution.py:396
  69.6 1.3 %collective-permute-start.20 = (bf16[2,256,256]{2,1,0:T(8,128)(2,1)S(1)}, bf16[2,256,256]{2,1,0:T(8,128)(2,1)S(1)}, u32[]{:S(2)}, u32[]{:S(2)}) collective-permute-start(bf16[2,256,256]{2,1,0:T(8,128)(2,1)S(1)} %add_convert_fusion.9), channel_id=1, source_target_pairs={{4,0},{8,4},{12,8},{14,12},{10,14},{6,10},{2,6},{0,2},{5,1},{9,5},... | collective-permute-start | bytes 786440 | tf_op jit(solution)/shard_map/ppermute | solution.py:393
  70.8 0.8 collective-permute-start.21
  71.6 2.9 %shard_map.97 = (f32[2,128,1024]{2,1,0:T(8,128)S(1)}, f32[2,256,256]{2,1,0:T(8,128)S(1)}, f32[2,256,256]{2,1,0:T(8,128)S(1)}) custom-call(bf16[256,2048]{1,0:T(8,128)(2,1)S(1)} %copy-done, bf16[256,2048]{1,0:T(8,128)(2,1)S(1)} %copy-done.1, bf16[256,128]{1,0:T(8,128)(2,1)S(1)} %get-tuple-element.118.mask_ref, ...), custom_call_target="tpu_custom_call", output_to_operand_aliasing={{0}: (10, {})} | custom-call | flops 10 | bytes 256 | tf_op jit(solution)/shard_map/pallas_call | solution.py:396
  75.2 1.3 %collective-permute-start.22 = (bf16[2,256,256]{2,1,0:T(8,128)(2,1)S(1)}, bf16[2,256,256]{2,1,0:T(8,128)(2,1)S(1)}, u32[]{:S(2)}, u32[]{:S(2)}) collective-permute-start(bf16[2,256,256]{2,1,0:T(8,128)(2,1)S(1)} %add_convert_fusion.7), channel_id=1, source_target_pairs={{4,0},{8,4},{12,8},{14,12},{10,14},{6,10},{2,6},{0,2},{5,1},{9,5},... | collective-permute-start | bytes 786440 | tf_op jit(solution)/shard_map/ppermute | solution.py:393
  76.5 0.8 collective-permute-start.23
  77.3 2.9 %shard_map.98 = (f32[2,128,1024]{2,1,0:T(8,128)S(1)}, f32[2,256,256]{2,1,0:T(8,128)S(1)}, f32[2,256,256]{2,1,0:T(8,128)S(1)}) custom-call(bf16[256,2048]{1,0:T(8,128)(2,1)S(1)} %copy-done, bf16[256,2048]{1,0:T(8,128)(2,1)S(1)} %copy-done.1, bf16[256,128]{1,0:T(8,128)(2,1)S(1)} %get-tuple-element.118.mask_ref, ...), custom_call_target="tpu_custom_call", output_to_operand_aliasing={{0}: (10, {})} | custom-call | flops 10 | bytes 256 | tf_op jit(solution)/shard_map/pallas_call | solution.py:396
  80.8 1.3 %collective-permute-start.24 = (bf16[2,256,256]{2,1,0:T(8,128)(2,1)S(1)}, bf16[2,256,256]{2,1,0:T(8,128)(2,1)S(1)}, u32[]{:S(2)}, u32[]{:S(2)}) collective-permute-start(bf16[2,256,256]{2,1,0:T(8,128)(2,1)S(1)} %add_convert_fusion.5), channel_id=1, source_target_pairs={{4,0},{8,4},{12,8},{14,12},{10,14},{6,10},{2,6},{0,2},{5,1},{9,5},... | collective-permute-start | bytes 786440 | tf_op jit(solution)/shard_map/ppermute | solution.py:393
  82.1 0.8 collective-permute-start.25
  82.9 2.9 %shard_map.99 = (f32[2,128,1024]{2,1,0:T(8,128)S(1)}, f32[2,256,256]{2,1,0:T(8,128)S(1)}, f32[2,256,256]{2,1,0:T(8,128)S(1)}) custom-call(bf16[256,2048]{1,0:T(8,128)(2,1)S(1)} %copy-done, bf16[256,2048]{1,0:T(8,128)(2,1)S(1)} %copy-done.1, bf16[256,128]{1,0:T(8,128)(2,1)S(1)} %get-tuple-element.118.mask_ref, ...), custom_call_target="tpu_custom_call", output_to_operand_aliasing={{0}: (10, {})} | custom-call | flops 10 | bytes 256 | tf_op jit(solution)/shard_map/pallas_call | solution.py:396
  86.4 1.3 %collective-permute-start.26 = (bf16[2,256,256]{2,1,0:T(8,128)(2,1)S(1)}, bf16[2,256,256]{2,1,0:T(8,128)(2,1)S(1)}, u32[]{:S(2)}, u32[]{:S(2)}) collective-permute-start(bf16[2,256,256]{2,1,0:T(8,128)(2,1)S(1)} %add_convert_fusion.3), channel_id=1, source_target_pairs={{4,0},{8,4},{12,8},{14,12},{10,14},{6,10},{2,6},{0,2},{5,1},{9,5},... | collective-permute-start | bytes 786440 | tf_op jit(solution)/shard_map/ppermute | solution.py:393
  87.7 0.8 collective-permute-start.27
  88.5 1.7 %shard_map.101 = (f32[2,128,1024]{2,1,0:T(8,128)S(1)}, f32[2,256,256]{2,1,0:T(8,128)S(1)}) custom-call(bf16[256,2048]{1,0:T(8,128)(2,1)S(1)} %copy-done, bf16[256,2048]{1,0:T(8,128)(2,1)S(1)} %copy-done.1, bf16[256,128]{1,0:T(8,128)(2,1)S(1)} %get-tuple-element.118.mask_ref, ...), custom_call_target="tpu_custom_call", output_to_operand_aliasing={{0}: (8, {})} | custom-call | flops 5 | bytes 256 | tf_op jit(solution)/shard_map/pallas_call | solution.py:396
  90.2 1.7 %shard_map.100 = (f32[2,128,1024]{2,1,0:T(8,128)S(1)}, f32[2,256,256]{2,1,0:T(8,128)S(1)}) custom-call(bf16[256,2048]{1,0:T(8,128)(2,1)S(1)} %copy-done, bf16[256,2048]{1,0:T(8,128)(2,1)S(1)} %copy-done.1, bf16[256,128]{1,0:T(8,128)(2,1)S(1)} %get-tuple-element.118.mask_ref, ...), custom_call_target="tpu_custom_call", output_to_operand_aliasing={{0}: (8, {})} | custom-call | flops 5 | bytes 256 | tf_op jit(solution)/shard_map/pallas_call | solution.py:396
  92.0 1.5 %shard_map.102 = bf16[256,2048]{1,0:T(8,128)(2,1)} custom-call(f32[2,128,1024]{2,1,0:T(8,128)S(1)} %get-tuple-element.225.refs_0_, f32[2,128,1024]{2,1,0:T(8,128)S(1)} %get-tuple-element.226.refs_1_), custom_call_target="tpu_custom_call" | custom-call | bytes 256 | tf_op jit(solution)/shard_map/pallas_call | solution.py:396
  94.1 0.8 fusion.2
  (52 shorter events, 6.1 us)
Async XLA Ops:
  0.6 27.0 %copy-start = (bf16[256,2048]{1,0:T(8,128)(2,1)S(1)}, bf16[256,2048]{1,0:T(8,128)(2,1)}, u32[]{:S(2)}) copy-start(bf16[256,2048]{1,0:T(8,128)(2,1)} %q_ref.31) | copy-start | bytes 3145732
  0.6 13.4 %collective-permute-start.2 = (bf16[256,512]{1,0:T(8,128)(2,1)}, bf16[256,512]{1,0:T(8,128)(2,1)S(1)}, u32[]{:S(2)}, u32[]{:S(2)}) collective-permute-start(bf16[256,512]{1,0:T(8,128)(2,1)} %param.7), channel_id=1, source_target_pairs={{0,4},{4,8},{8,12},{12,14},{14,10},{10,6},{6,2},{2,0},{1,5},{5,9},... | collective-permute-start | bytes 786440 | tf_op jit(solution)/shard_map/ppermute | solution.py:390
  3.7 10.4 %collective-permute-start.3 = (bf16[256,512]{1,0:T(8,128)(2,1)}, bf16[256,512]{1,0:T(8,128)(2,1)S(1)}, u32[]{:S(2)}, u32[]{:S(2)}) collective-permute-start(bf16[256,512]{1,0:T(8,128)(2,1)} %param.7), channel_id=1, source_target_pairs={{4,0},{8,4},{12,8},{14,12},{10,14},{6,10},{2,6},{0,2},{5,1},{9,5},... | collective-permute-start | bytes 786440 | tf_op jit(solution)/shard_map/ppermute | solution.py:393
  3.7 17.3 %collective-permute-start = (bf16[256,512]{1,0:T(8,128)(2,1)}, bf16[256,512]{1,0:T(8,128)(2,1)S(1)}, u32[]{:S(2)}, u32[]{:S(2)}) collective-permute-start(bf16[256,512]{1,0:T(8,128)(2,1)} %param.8), channel_id=1, source_target_pairs={{0,4},{4,8},{8,12},{12,14},{14,10},{10,6},{6,2},{2,0},{1,5},{5,9},... | collective-permute-start | bytes 786440 | tf_op jit(solution)/shard_map/ppermute | solution.py:390
  5.7 15.3 %collective-permute-start.1 = (bf16[256,512]{1,0:T(8,128)(2,1)}, bf16[256,512]{1,0:T(8,128)(2,1)S(1)}, u32[]{:S(2)}, u32[]{:S(2)}) collective-permute-start(bf16[256,512]{1,0:T(8,128)(2,1)} %param.8), channel_id=1, source_target_pairs={{4,0},{8,4},{12,8},{14,12},{10,14},{6,10},{2,6},{0,2},{5,1},{9,5},... | collective-permute-start | bytes 786440 | tf_op jit(solution)/shard_map/ppermute | solution.py:393
  7.8 13.2 %all-to-all-start = ((s32[8,8,128]{2,1,0:T(8,128)}), s32[8,8,128]{2,1,0:T(8,128)S(1)}, u32[]{:S(2)}, u32[]{:S(2)}) async-start(s32[8,8,128]{2,1,0:T(8,128)} %broadcast_in_dim.2), calls=%async_computation | async-start | bytes 65536 | tf_op jit(solution)/shard_map/all_to_all | solution.py:413
  14.1 10.6 %collective-permute-start.4 = (bf16[256,512]{1,0:T(8,128)(2,1)S(1)}, bf16[256,512]{1,0:T(8,128)(2,1)S(1)}, u32[]{:S(2)}, u32[]{:S(2)}) collective-permute-start(bf16[256,512]{1,0:T(8,128)(2,1)S(1)} %collective-permute-done.2.refs_2_.refs_0_), channel_id=1, source_target_pairs={{0,4},{4,8},{8,12},{12,14},{14,10},{10,6},{6,2},{2,0},{1,5},{5,9},... | collective-permute-start | bytes 786440 | tf_op jit(solution)/shard_map/ppermute | solution.py:390
  16.2 9.4 %collective-permute-start.5 = (bf16[256,512]{1,0:T(8,128)(2,1)S(1)}, bf16[256,512]{1,0:T(8,128)(2,1)S(1)}, u32[]{:S(2)}, u32[]{:S(2)}) collective-permute-start(bf16[256,512]{1,0:T(8,128)(2,1)S(1)} %collective-permute-done.3.refs_4_.refs_2_), channel_id=1, source_target_pairs={{4,0},{8,4},{12,8},{14,12},{10,14},{6,10},{2,6},{0,2},{5,1},{9,5},... | collective-permute-start | bytes 786440 | tf_op jit(solution)/shard_map/ppermute | solution.py:393
  21.1 9.4 %collective-permute-start.6 = (bf16[256,512]{1,0:T(8,128)(2,1)S(1)}, bf16[256,512]{1,0:T(8,128)(2,1)S(1)}, u32[]{:S(2)}, u32[]{:S(2)}) collective-permute-start(bf16[256,512]{1,0:T(8,128)(2,1)S(1)} %collective-permute-done.refs_3_.refs_1_), channel_id=1, source_target_pairs={{0,4},{4,8},{8,12},{12,14},{14,10},{10,6},{6,2},{2,0},{1,5},{5,9},... | collective-permute-start | bytes 786440 | tf_op jit(solution)/shard_map/ppermute | solution.py:390
  21.8 9.4 %collective-permute-start.7 = (bf16[256,512]{1,0:T(8,128)(2,1)S(1)}, bf16[256,512]{1,0:T(8,128)(2,1)S(1)}, u32[]{:S(2)}, u32[]{:S(2)}) collective-permute-start(bf16[256,512]{1,0:T(8,128)(2,1)S(1)} %collective-permute-done.1.refs_5_.refs_3_), channel_id=1, source_target_pairs={{4,0},{8,4},{12,8},{14,12},{10,14},{6,10},{2,6},{0,2},{5,1},{9,5},... | collective-permute-start | bytes 786440 | tf_op jit(solution)/shard_map/ppermute | solution.py:393
  25.6 12.7 %collective-permute-start.8 = (bf16[256,512]{1,0:T(8,128)(2,1)S(1)}, bf16[256,512]{1,0:T(8,128)(2,1)S(1)}, u32[]{:S(2)}, u32[]{:S(2)}) collective-permute-start(bf16[256,512]{1,0:T(8,128)(2,1)S(1)} %collective-permute-done.4.refs_0_), channel_id=1, source_target_pairs={{0,4},{4,8},{8,12},{12,14},{14,10},{10,6},{6,2},{2,0},{1,5},{5,9},... | collective-permute-start | bytes 786440 | tf_op jit(solution)/shard_map/ppermute | solution.py:390
  27.0 11.2 %collective-permute-start.9 = (bf16[256,512]{1,0:T(8,128)(2,1)S(1)}, bf16[256,512]{1,0:T(8,128)(2,1)S(1)}, u32[]{:S(2)}, u32[]{:S(2)}) collective-permute-start(bf16[256,512]{1,0:T(8,128)(2,1)S(1)} %collective-permute-done.5.refs_2_), channel_id=1, source_target_pairs={{4,0},{8,4},{12,8},{14,12},{10,14},{6,10},{2,6},{0,2},{5,1},{9,5},... | collective-permute-start | bytes 786440 | tf_op jit(solution)/shard_map/ppermute | solution.py:393
  31.2 10.7 %collective-permute-start.10 = (bf16[256,512]{1,0:T(8,128)(2,1)S(1)}, bf16[256,512]{1,0:T(8,128)(2,1)S(1)}, u32[]{:S(2)}, u32[]{:S(2)}) collective-permute-start(bf16[256,512]{1,0:T(8,128)(2,1)S(1)} %collective-permute-done.6.refs_1_), channel_id=1, source_target_pairs={{0,4},{4,8},{8,12},{12,14},{14,10},{10,6},{6,2},{2,0},{1,5},{5,9},... | collective-permute-start | bytes 786440 | tf_op jit(solution)/shard_map/ppermute | solution.py:390
  32.7 9.2 %collective-permute-start.11 = (bf16[256,512]{1,0:T(8,128)(2,1)S(1)}, bf16[256,512]{1,0:T(8,128)(2,1)S(1)}, u32[]{:S(2)}, u32[]{:S(2)}) collective-permute-start(bf16[256,512]{1,0:T(8,128)(2,1)S(1)} %collective-permute-done.7.refs_3_), channel_id=1, source_target_pairs={{4,0},{8,4},{12,8},{14,12},{10,14},{6,10},{2,6},{0,2},{5,1},{9,5},... | collective-permute-start | bytes 786440 | tf_op jit(solution)/shard_map/ppermute | solution.py:393
  38.3 8.8 %collective-permute-start.12 = (bf16[256,512]{1,0:T(8,128)(2,1)S(1)}, bf16[256,512]{1,0:T(8,128)(2,1)S(1)}, u32[]{:S(2)}, u32[]{:S(2)}) collective-permute-start(bf16[256,512]{1,0:T(8,128)(2,1)S(1)} %collective-permute-done.8.refs_0_), channel_id=1, source_target_pairs={{0,4},{4,8},{8,12},{12,14},{14,10},{10,6},{6,2},{2,0},{1,5},{5,9},... | collective-permute-start | bytes 786440 | tf_op jit(solution)/shard_map/ppermute | solution.py:390
  41.9 6.4 %collective-permute-start.13 = (bf16[256,512]{1,0:T(8,128)(2,1)S(1)}, bf16[256,512]{1,0:T(8,128)(2,1)S(1)}, u32[]{:S(2)}, u32[]{:S(2)}) collective-permute-start(bf16[256,512]{1,0:T(8,128)(2,1)S(1)} %collective-permute-done.11.refs_3_), channel_id=1, source_target_pairs={{4,0},{8,4},{12,8},{14,12},{10,14},{6,10},{2,6},{0,2},{5,1},{9,5},... | collective-permute-start | bytes 786440 | tf_op jit(solution)/shard_map/ppermute | solution.py:393
  45.0 3.4 %copy-start.1 = (bf16[256,2048]{1,0:T(8,128)(2,1)S(1)}, bf16[256,2048]{1,0:T(8,128)(2,1)}, u32[]{:S(2)}) copy-start(bf16[256,2048]{1,0:T(8,128)(2,1)} %g_ref.19) | copy-start | bytes 3145732
  51.0 8.0 %collective-permute-start.14 = (bf16[2,256,256]{2,1,0:T(8,128)(2,1)S(1)}, bf16[2,256,256]{2,1,0:T(8,128)(2,1)S(1)}, u32[]{:S(2)}, u32[]{:S(2)}) collective-permute-start(bf16[2,256,256]{2,1,0:T(8,128)(2,1)S(1)} %get-tuple-element.184), channel_id=1, source_target_pairs={{4,0},{8,4},{12,8},{14,12},{10,14},{6,10},{2,6},{0,2},{5,1},{9,5},... | collective-permute-start | bytes 786440 | tf_op jit(solution)/shard_map/ppermute | solution.py:393
  54.9 9.2 %collective-permute-start.15 = (bf16[2,256,256]{2,1,0:T(8,128)(2,1)S(1)}, bf16[2,256,256]{2,1,0:T(8,128)(2,1)S(1)}, u32[]{:S(2)}, u32[]{:S(2)}) collective-permute-start(bf16[2,256,256]{2,1,0:T(8,128)(2,1)S(1)} %get-tuple-element.192), channel_id=1, source_target_pairs={{0,4},{4,8},{8,12},{12,14},{14,10},{10,6},{6,2},{2,0},{1,5},{5,9},... | collective-permute-start | bytes 786440 | tf_op jit(solution)/shard_map/ppermute | solution.py:390
  59.1 10.1 %collective-permute-start.16 = (bf16[2,256,256]{2,1,0:T(8,128)(2,1)S(1)}, bf16[2,256,256]{2,1,0:T(8,128)(2,1)S(1)}, u32[]{:S(2)}, u32[]{:S(2)}) collective-permute-start(bf16[2,256,256]{2,1,0:T(8,128)(2,1)S(1)} %add_convert_fusion.11), channel_id=1, source_target_pairs={{4,0},{8,4},{12,8},{14,12},{10,14},{6,10},{2,6},{0,2},{5,1},{9,5},... | collective-permute-start | bytes 786440 | tf_op jit(solution)/shard_map/ppermute | solution.py:393
  60.0 9.5 %collective-permute-start.17 = (bf16[2,256,256]{2,1,0:T(8,128)(2,1)S(1)}, bf16[2,256,256]{2,1,0:T(8,128)(2,1)S(1)}, u32[]{:S(2)}, u32[]{:S(2)}) collective-permute-start(bf16[2,256,256]{2,1,0:T(8,128)(2,1)S(1)} %convert_element_type.86), channel_id=1, source_target_pairs={{0,4},{4,8},{8,12},{12,14},{14,10},{10,6},{6,2},{2,0},{1,5},{5,9},... | collective-permute-start | bytes 786440 | tf_op jit(solution)/shard_map/ppermute | solution.py:390
  64.2 10.4 %collective-permute-start.18 = (bf16[2,256,256]{2,1,0:T(8,128)(2,1)S(1)}, bf16[2,256,256]{2,1,0:T(8,128)(2,1)S(1)}, u32[]{:S(2)}, u32[]{:S(2)}) collective-permute-start(bf16[2,256,256]{2,1,0:T(8,128)(2,1)S(1)} %convert_element_type.87), channel_id=1, source_target_pairs={{4,0},{8,4},{12,8},{14,12},{10,14},{6,10},{2,6},{0,2},{5,1},{9,5},... | collective-permute-start | bytes 786440 | tf_op jit(solution)/shard_map/ppermute | solution.py:393
  65.2 9.9 %collective-permute-start.19 = (bf16[2,256,256]{2,1,0:T(8,128)(2,1)S(1)}, bf16[2,256,256]{2,1,0:T(8,128)(2,1)S(1)}, u32[]{:S(2)}, u32[]{:S(2)}) collective-permute-start(bf16[2,256,256]{2,1,0:T(8,128)(2,1)S(1)} %add_convert_fusion.10), channel_id=1, source_target_pairs={{0,4},{4,8},{8,12},{12,14},{14,10},{10,6},{6,2},{2,0},{1,5},{5,9},... | collective-permute-start | bytes 786440 | tf_op jit(solution)/shard_map/ppermute | solution.py:390
  69.6 10.6 %collective-permute-start.20 = (bf16[2,256,256]{2,1,0:T(8,128)(2,1)S(1)}, bf16[2,256,256]{2,1,0:T(8,128)(2,1)S(1)}, u32[]{:S(2)}, u32[]{:S(2)}) collective-permute-start(bf16[2,256,256]{2,1,0:T(8,128)(2,1)S(1)} %add_convert_fusion.9), channel_id=1, source_target_pairs={{4,0},{8,4},{12,8},{14,12},{10,14},{6,10},{2,6},{0,2},{5,1},{9,5},... | collective-permute-start | bytes 786440 | tf_op jit(solution)/shard_map/ppermute | solution.py:393
  70.8 9.9 %collective-permute-start.21 = (bf16[2,256,256]{2,1,0:T(8,128)(2,1)S(1)}, bf16[2,256,256]{2,1,0:T(8,128)(2,1)S(1)}, u32[]{:S(2)}, u32[]{:S(2)}) collective-permute-start(bf16[2,256,256]{2,1,0:T(8,128)(2,1)S(1)} %add_convert_fusion.8), channel_id=1, source_target_pairs={{0,4},{4,8},{8,12},{12,14},{14,10},{10,6},{6,2},{2,0},{1,5},{5,9},... | collective-permute-start | bytes 786440 | tf_op jit(solution)/shard_map/ppermute | solution.py:390
  75.2 10.6 %collective-permute-start.22 = (bf16[2,256,256]{2,1,0:T(8,128)(2,1)S(1)}, bf16[2,256,256]{2,1,0:T(8,128)(2,1)S(1)}, u32[]{:S(2)}, u32[]{:S(2)}) collective-permute-start(bf16[2,256,256]{2,1,0:T(8,128)(2,1)S(1)} %add_convert_fusion.7), channel_id=1, source_target_pairs={{4,0},{8,4},{12,8},{14,12},{10,14},{6,10},{2,6},{0,2},{5,1},{9,5},... | collective-permute-start | bytes 786440 | tf_op jit(solution)/shard_map/ppermute | solution.py:393
  76.5 9.9 %collective-permute-start.23 = (bf16[2,256,256]{2,1,0:T(8,128)(2,1)S(1)}, bf16[2,256,256]{2,1,0:T(8,128)(2,1)S(1)}, u32[]{:S(2)}, u32[]{:S(2)}) collective-permute-start(bf16[2,256,256]{2,1,0:T(8,128)(2,1)S(1)} %add_convert_fusion.6), channel_id=1, source_target_pairs={{0,4},{4,8},{8,12},{12,14},{14,10},{10,6},{6,2},{2,0},{1,5},{5,9},... | collective-permute-start | bytes 786440 | tf_op jit(solution)/shard_map/ppermute | solution.py:390
  80.8 11.1 %collective-permute-start.24 = (bf16[2,256,256]{2,1,0:T(8,128)(2,1)S(1)}, bf16[2,256,256]{2,1,0:T(8,128)(2,1)S(1)}, u32[]{:S(2)}, u32[]{:S(2)}) collective-permute-start(bf16[2,256,256]{2,1,0:T(8,128)(2,1)S(1)} %add_convert_fusion.5), channel_id=1, source_target_pairs={{4,0},{8,4},{12,8},{14,12},{10,14},{6,10},{2,6},{0,2},{5,1},{9,5},... | collective-permute-start | bytes 786440 | tf_op jit(solution)/shard_map/ppermute | solution.py:393
  82.1 9.9 %collective-permute-start.25 = (bf16[2,256,256]{2,1,0:T(8,128)(2,1)S(1)}, bf16[2,256,256]{2,1,0:T(8,128)(2,1)S(1)}, u32[]{:S(2)}, u32[]{:S(2)}) collective-permute-start(bf16[2,256,256]{2,1,0:T(8,128)(2,1)S(1)} %add_convert_fusion.4), channel_id=1, source_target_pairs={{0,4},{4,8},{8,12},{12,14},{14,10},{10,6},{6,2},{2,0},{1,5},{5,9},... | collective-permute-start | bytes 786440 | tf_op jit(solution)/shard_map/ppermute | solution.py:390
  86.4 7.1 %collective-permute-start.26 = (bf16[2,256,256]{2,1,0:T(8,128)(2,1)S(1)}, bf16[2,256,256]{2,1,0:T(8,128)(2,1)S(1)}, u32[]{:S(2)}, u32[]{:S(2)}) collective-permute-start(bf16[2,256,256]{2,1,0:T(8,128)(2,1)S(1)} %add_convert_fusion.3), channel_id=1, source_target_pairs={{4,0},{8,4},{12,8},{14,12},{10,14},{6,10},{2,6},{0,2},{5,1},{9,5},... | collective-permute-start | bytes 786440 | tf_op jit(solution)/shard_map/ppermute | solution.py:393
  87.7 6.4 %collective-permute-start.27 = (bf16[2,256,256]{2,1,0:T(8,128)(2,1)S(1)}, bf16[2,256,256]{2,1,0:T(8,128)(2,1)S(1)}, u32[]{:S(2)}, u32[]{:S(2)}) collective-permute-start(bf16[2,256,256]{2,1,0:T(8,128)(2,1)S(1)} %add_convert_fusion.2), channel_id=1, source_target_pairs={{0,4},{4,8},{8,12},{12,14},{14,10},{10,6},{6,2},{2,0},{1,5},{5,9},... | collective-permute-start | bytes 786440 | tf_op jit(solution)/shard_map/ppermute | solution.py:390
